TPU v7x, 512 devices: a whole 4x4x16 slice. The times are simulated.
512 devices in a mesh: row: 32 (over y, x, core), col: 16 (over z).
Axes of the slice: x: 4, y: 4, z: 16, core: 2. Of those that a mesh axis runs over, the one named last changes fastest.
Arguments:
- col_samples: float32 [64, 2, 2048, 128], P('row', None, 'col'), may hold values from -6 to 6
- row_samples: float32 [64, 2, 128, 2048], P('row', None, None, 'col'), may hold values from -6 to 6
- pivot_rows: int32 [64, 128], P('row'), may hold values from 0 to 2047
- rank_blocks: int32 [64], P('row'), may hold values from 1 to 8
- upper_inverse: float32 [2, 2048, 2048], P(None, 'col', 'row'), as said below
- upanel_left: float32 [16, 2, 2048, 128], P('col'), may hold values from -0.125 to 0.125
Outputs:
- panel_right: float32 [64, 2, 128, 2048], P('row', None, None, 'col')
- cores: float32 [64, 16, 2, 128, 128], P('row', 'col')
Inputs may be any that keep to these rules, and one draw needn't show every extreme that they name: `rank_blocks`: the tile's rank is 16 times this. `upper_inverse`: zero below the diagonal in both parts.
All inputs are finite; a program needn't handle non-finite values.
Results may differ from a plain program's by a relative error of at most 0.00007.
Values sent between devices are 32-bit elements; how exact they have to be, the bound alone decides.
No kernel may reach another device: no remote copies, remote signals or barrier semaphores. Data moves between devices by JAX's collectives and lax.ppermute only.
A program may use at most 64 MiB of HBM per device.

v0:
```python
import jax
import jax.numpy as jnp
from jax import lax
from jax.sharding import PartitionSpec as P

RANK_STEP = 16


def complex_product(pattern, left_real, left_imag, right_real, right_imag):

    def single(left, right):
        return jnp.einsum(
            pattern,
            left,
            right,
            precision=lax.Precision.HIGHEST,
            preferred_element_type=jnp.float32,
        )

    real_part = single(left_real, right_real) - single(left_imag, right_imag)
    imag_part = single(left_real, right_imag) + single(left_imag, right_real)
    return (real_part, imag_part)


def scale_rows(values, weight_real, weight_imag):
    wr = weight_real[:, :, None]
    wi = weight_imag[:, :, None]
    real_part = values[:, 0] * wr - values[:, 1] * wi
    imag_part = values[:, 0] * wi + values[:, 1] * wr
    return jnp.stack((real_part, imag_part), axis=1)


def on_device(col_samples, row_samples, pivot_rows, rank_blocks, upper_inverse, upanel_left):
    width_local = col_samples.shape[2]
    ranks_max = row_samples.shape[2]
    offset = lax.axis_index("col") * width_local
    positions = offset + lax.broadcasted_iota(jnp.int32, (1, 1, width_local), 2)
    hits = (pivot_rows[:, :, None] == positions).astype(jnp.float32)
    flipped = jnp.swapaxes(col_samples, 2, 3)
    partial_entries = jnp.sum(flipped * hits[:, None], axis=3)
    entries = lax.psum(partial_entries, "col")
    levels = lax.broadcasted_iota(jnp.int32, (1, ranks_max), 1)
    keeping = (levels < RANK_STEP * rank_blocks[:, None]).astype(jnp.float32)
    magnitude = jnp.maximum(entries[:, 0] * entries[:, 0] + entries[:, 1] * entries[:, 1], 1.0)
    factor_real = keeping * entries[:, 0] / magnitude
    factor_imag = -keeping * entries[:, 1] / magnitude
    scaled = scale_rows(row_samples, factor_real, factor_imag)
    portion = lax.all_gather(upper_inverse, "row", axis=2, tiled=True)
    real_part, imag_part = complex_product(
        "trk,kn->trn", scaled[:, 0], scaled[:, 1], portion[0], portion[1]
    )
    partial_panel = jnp.stack((real_part, imag_part), axis=1)
    panel_local = lax.psum_scatter(partial_panel, "col", scatter_dimension=3, tiled=True)
    portion = lax.all_gather(panel_local, "col", axis=3, tiled=True)
    core_real, core_imag = complex_product(
        "trn,jns->tjrs", portion[:, 0], portion[:, 1], upanel_left[:, 0], upanel_left[:, 1]
    )
    cores = jnp.stack((core_real, core_imag), axis=2)
    return (panel_local, cores)


def solution(mesh):
    in_specs = (
        P("row", None, "col", None),
        P("row", None, None, "col"),
        P("row", None),
        P("row"),
        P(None, "col", "row"),
        P("col", None, None, None),
    )
    out_specs = (P("row", None, None, "col"), P("row", "col", None, None, None))
    return jax.shard_map(
        on_device, mesh=mesh, in_specs=in_specs, out_specs=out_specs, check_vma=False
    )
```

profile of v0, /device:TPU:2, one launch (start us, length us, event | category | flops | bytes accessed | tf_op | source)
XLA Modules:
  0.0 281.9 jit_solution(7301261295972462733)
XLA Ops:
  7.2 0.0 all-gather.3.cloned.1.call-start
  7.2 1.5 copy.12
  8.7 0.0 all-gather.3.cloned.1.call-update
  8.8 0.0 reduce-scatter.2.cloned.1.call-start
  8.8 0.8 compare_convert_fusion
  9.6 1.0 fusion.18
  10.6 36.5 %psum.7 = f32[2,2,128]{2,1,0:T(2,128)S(1)} all-reduce(f32[2,2,128]{2,1,0:T(2,128)S(1)} %fusion.18), channel_id=1, replica_groups=mesh['row'=32,'col'=16] {'col'}, use_global_device_ids=true, to_apply=%region_1.0 | all-reduce | flops 512 | bytes 4096 | tf_op jit(solution)/shard_map/psum | solution.py:41
  47.1 0.7 broadcast_multiply_fusion
  47.8 0.1 select_divide_fusion
  47.8 0.0 copy-start.2
  47.8 27.1 %all-gather.3.cloned.1.call-done = f32[2,128,2048]{1,0,2:T(2,128)} async-done(((f32[2,128,64]{1,0,2:T(2,128)}), f32[2,128,2048]{1,0,2:T(2,128)}) %all-gather.3.cloned.1.call-update) | async-done | bytes 2097168 | tf_op jit(solution)/shard_map/all_gather | solution.py:48
  74.9 4.0 %fusion.25 = (f32[1,128,2048]{1,0,2:T(1,128)S(1)}, f32[1,128,2048]{1,0,2:T(1,128)S(1)}) fusion(f32[2,128,2048]{1,0,2:T(2,128)} %all-gather.3.cloned.1.call-done), kind=kLoop, calls=%fused_computation.41 | loop fusion | bytes 4194304 | tf_op jit(solution)/shard_map/slice | solution.py:50
  78.9 0.0 copy-done.2
  78.9 1.8 fusion.21
  80.8 1.8 fusion.23
  82.6 1.9 fusion
  84.5 1.9 fusion.1
  86.4 2.2 pad_maximum_fusion
  88.6 0.0 reduce-scatter.2.cloned.1.call-update
  88.7 0.2 all-gather.5.cloned.1.call-start
  88.9 79.6 %reduce-scatter.2.cloned.1.call-done = f32[2,2,128,128]{3,2,0,1:T(8,128)} async-done(((f32[2,2,128,2048]{3,2,0,1:T(8,128)}), f32[2,2,128,128]{3,2,0,1:T(8,128)}) %reduce-scatter.2.cloned.1.call-update) | async-done | bytes 262160 | tf_op jit(solution)/shard_map/reduce_scatter | solution.py:53
  168.5 0.0 all-gather.5.cloned.1.call-update
  168.5 1.7 copy.15
  170.2 93.8 %all-gather.5.cloned.1.call-done = f32[2,2,128,2048]{3,2,0,1:T(8,128)} async-done(((f32[2,2,128,128]{3,2,0,1:T(8,128)}), f32[2,2,128,2048]{3,2,0,1:T(8,128)}) %all-gather.5.cloned.1.call-update) | async-done | bytes 4194320 | tf_op jit(solution)/shard_map/all_gather | solution.py:54
  263.9 0.0 copy-done.1
  263.9 0.0 copy-start
  263.9 3.6 %fusion.2 = f32[2,128,128]{2,1,0:T(8,128)S(1)} fusion(f32[2,2,128,2048]{3,2,0,1:T(8,128)} %all-gather.5.cloned.1.call-done, f32[1,2,2048,128]{3,2,1,0:T(8,128)S(1)} %copy-done.1), kind=kOutput, calls=%fused_computation.7 | convolution fusion | flops 805306368 | bytes 3276800 | tf_op jit(solution)/shard_map/trn,jns->tjrs/dot_general | solution.py:12
  267.5 3.4 %fusion.3 = f32[2,128,128]{2,1,0:T(8,128)S(1)} fusion(f32[2,2,128,2048]{3,2,0,1:T(8,128)} %all-gather.5.cloned.1.call-done, f32[1,2,2048,128]{3,2,1,0:T(8,128)S(1)} %copy-done.1), kind=kOutput, calls=%fused_computation.8 | convolution fusion | flops 805306368 | bytes 3276800 | tf_op jit(solution)/shard_map/trn,jns->tjrs/dot_general | solution.py:12
  270.9 0.0 copy-done
  270.9 1.8 fusion.9
  272.8 1.8 fusion.7
  274.6 0.7 copy.16
  (4 shorter events, 0.0 us)
Async XLA Ops:
  7.2 67.7 %all-gather.3.cloned.1.call-start = ((), (), s32[]{:S(2)}) async-start(), calls=%async_computation.1 | async-start | bytes 2162688 | tf_op jit(solution)/shard_map/all_gather | solution.py:48
  8.8 159.7 %reduce-scatter.2.cloned.1.call-start = ((), (), s32[]{:S(2)}) async-start(), calls=%async_computation.2 | async-start | bytes 4456448 | tf_op jit(solution)/shard_map/reduce_scatter | solution.py:53
  47.8 31.1 %copy-start.2 = (f32[2,2,128,128]{3,2,1,0:T(8,128)S(1)}, f32[2,2,128,128]{3,2,1,0:T(8,128)}, u32[]{:S(2)}) copy-start(f32[2,2,128,128]{3,2,1,0:T(8,128)} %param.7) | copy-start | bytes 786436
  88.6 175.3 %copy-start.1 = (f32[1,2,2048,128]{3,2,1,0:T(8,128)S(1)}, f32[1,2,2048,128]{3,2,1,0:T(8,128)}, u32[]{:S(2)}) copy-start(f32[1,2,2048,128]{3,2,1,0:T(8,128)} %param.11) | copy-start | bytes 6291460
  88.7 175.3 %all-gather.5.cloned.1.call-start = ((), (), s32[]{:S(2)}) async-start(), calls=%async_computation.3 | async-start | bytes 4456448 | tf_op jit(solution)/shard_map/all_gather | solution.py:54
  263.9 7.0 %copy-start = (f32[2,2,128,2048]{3,2,0,1:T(8,128)S(1)}, f32[2,2,128,2048]{3,2,0,1:T(8,128)}, u32[]{:S(2)}) copy-start(f32[2,2,128,2048]{3,2,0,1:T(8,128)} %all-gather.5.cloned.1.call-done) | copy-start | bytes 12582916
Sparse Core Ops, SparseCore 0:
  11.7 63.1 all-gather.2
  88.8 79.6 reduce-scatter.1
  170.5 93.4 all-gather.4
where the time goes:
time: 282 us
  waiting for transfers between devices  200 us (71%)
  blocking collectives  36.5 us (13%)
  matrix products  18.1 us (6%)
  between operations  13.9 us (5%)
  local copies, waits for them, and re-layouts  7.92 us (3%)
  other arithmetic  4.73 us (2%)
    all_gather x1, waiting for transfers between devices, on_device(): portion = lax.all_gather(panel_local, 'col', axis=3, tiled=True)  93.8 us
    reduce_scatter x1, waiting for transfers between devices, on_device(): lax.psum_scatter(partial_panel, 'col', scatter_dimension=3, tiled=True)  79.6 us
    psum x1, blocking collectives, on_device(): entries = lax.psum(partial_entries, 'col')  36.5 us
    all_gather x1, waiting for transfers between devices, on_device(): portion = lax.all_gather(upper_inverse, 'row', axis=2, tiled=True)  27.1 us
    dot_general x8, matrix products, single(): jnp.einsum(pattern, left, right, precision=lax.Precision.HIGHEST, preferr...  18.1 us
  transfers between devices with their start and end apart: 3, of which 3 were waited for; matrix products, arithmetic and copies ran while one was open for 1% of the time, Pallas kernels for 0%

commit v1 on v0

v1 whole, which is shorter than its diff:
```python
import jax
import jax.numpy as jnp
from jax import lax
from jax.experimental import pallas as pl
from jax.experimental.pallas import tpu as pltpu
from jax.sharding import Mesh
from jax.sharding import PartitionSpec as P

RANK_STEP = 16
CHIPS = ("y", "x")
SCALE = 2.0 ** -12
UNSCALE = 2.0 ** 12


def params():
    return pltpu.CompilerParams(vmem_limit_bytes=48 * 1024 * 1024)


def cost(flops, moved):
    return pl.CostEstimate(flops=flops, bytes_accessed=moved, transcendentals=0)


def split(x):
    high = x.astype(jnp.bfloat16)
    low = (x - high.astype(jnp.float32)).astype(jnp.bfloat16)
    return high, low


def dot(a, b):
    return jnp.dot(a, b, preferred_element_type=jnp.float32)


def entries_kernel(pivots_ref, cols_ref, out_ref):
    width = cols_ref.shape[2]
    rows = lax.broadcasted_iota(jnp.int32, cols_ref.shape[2:], 0) + lax.axis_index("col") * width
    for i in range(2):
        hit = pivots_ref[i : i + 1, :] == rows
        for p in range(2):
            out_ref[2 * i + p : 2 * i + p + 1, :] = jnp.sum(
                jnp.where(hit, cols_ref[i, p], 0.0), axis=0, keepdims=True
            )


def pack_kernel(own_ref, moved_ref, out_ref):
    chip = lax.axis_index("y") * lax.axis_size("x") + lax.axis_index("x")
    place = lax.axis_index("col")
    swap = jnp.logical_and(chip == 1, place == lax.axis_size("col") - 1)
    core = lax.axis_index("c")
    parts = []
    for p in range(2):
        block = jnp.where(swap, moved_ref[p], own_ref[p])
        parts.append(block.T.reshape(16, 8, 128))
    first = lax.broadcasted_iota(jnp.int32, (16, 8, 128), 1) < 4
    low = jnp.where(first, parts[0], jnp.roll(parts[1], 4, axis=1))
    high = jnp.where(first, jnp.roll(parts[0], 4, axis=1), parts[1])
    out_ref[...] = jnp.where(core == 0, low, high)


def right_kernel(ranks_ref, rows_ref, left_ref, out_ref, factor_ref):
    place = lax.axis_index("col")
    corner = rows_ref[15, 0:8, :]
    total = None
    for q in range(16):
        if q == 0:
            x = jnp.concatenate([corner, jnp.zeros((120, 128), jnp.float32)], axis=0)
        elif q == 1:
            x = jnp.concatenate(
                [rows_ref[0:15, 0:8, :].reshape(120, 128), jnp.zeros((8, 128), jnp.float32)], axis=0
            )
        else:
            x = rows_ref[:, 8 * q - 8 : 8 * q, :].reshape(128, 128)
        y = jnp.concatenate(
            [left_ref[0, 128 * q : 128 * q + 128, :], left_ref[1, 128 * q : 128 * q + 128, :]], axis=1
        )
        xh, xl = split(x)
        yh, yl = split(y * SCALE)
        term = dot(xh, yh) + (dot(xh, yl) + dot(xl, yh))
        total = term if total is None else total + term
    by_real = total[:, :128].reshape(16, 8, 128)
    by_imag = jnp.roll(total[:, 128:].reshape(16, 8, 128), 4, axis=1)
    first = lax.broadcasted_iota(jnp.int32, (16, 8, 128), 1) < 4
    product = by_real + jnp.where(first, -by_imag, by_imag)
    start = pl.multiple_of(jnp.maximum(place - 1, 0) * 8, 8)
    block = rows_ref[:, pl.ds(start, 8), :]
    which = lax.broadcasted_iota(jnp.int32, (16, 8, 128), 0)
    block = jnp.where(jnp.logical_and(place == 1, which == 15), 0.0, block)
    at_zero = jnp.where(which == 0, corner[None], 0.0)
    block = jnp.where(place == 0, at_zero, block)
    for d in range(16):
        out_ref[d, :, 0] = block
        out_ref[d, :, 1] = product
    entries = jnp.sum(rows_ref[:, 120:124, :], axis=0)
    levels = lax.broadcasted_iota(jnp.int32, (1, 128), 1)
    for i in range(2):
        real, imag = entries[2 * i : 2 * i + 1], entries[2 * i + 1 : 2 * i + 2]
        keeping = (levels < RANK_STEP * ranks_ref[i]).astype(jnp.float32)
        magnitude = jnp.maximum(real * real + imag * imag, 1.0)
        factor_ref[2 * i : 2 * i + 1, :] = keeping * real / magnitude
        factor_ref[2 * i + 1 : 2 * i + 2, :] = -keeping * imag / magnitude
    factor_ref[4:8, :] = jnp.zeros((4, 128), jnp.float32)


def left_kernel(factor_ref, rows_ref, out_ref):
    core = lax.axis_index("c")
    columns = factor_ref[...].T
    first = (lax.broadcasted_iota(jnp.int32, (128, 128), 1) & 7) < 4
    for i in range(2):
        wr, wi = columns[:, 2 * i : 2 * i + 1], columns[:, 2 * i + 1 : 2 * i + 2]
        vr, vi = rows_ref[0, i, 0], rows_ref[0, i, 1]
        real, imag = vr * wr - vi * wi, vr * wi + vi * wr
        for p, (a, b) in enumerate(((real, -imag), (imag, real))):
            span = pl.ds(256 * p + 128 * i, 128)
            for slot, v in (
                (core, jnp.where(first, a, pltpu.roll(b, 4, 1))),
                (1 - core, jnp.where(first, pltpu.roll(a, 124, 1), b)),
            ):
                high, low = split(v)
                out_ref[slot, 0, span, :] = high
                out_ref[slot, 1, span, :] = low


def partial_sum(left_ref, right_ref):
    pieces = []
    for z in range(right_ref.shape[1]):
        pieces.append(
            jnp.concatenate(
                [right_ref[:, z, 0].reshape(128, 128), right_ref[:, z, 1].reshape(128, 128)], axis=1
            )
        )
    high, low = split(jnp.concatenate(pieces, axis=0))
    lh, ll = left_ref[0, 0], left_ref[0, 1]
    return dot(lh, high) + (dot(lh, low) + dot(ll, high))


def first_kernel(left_ref, right_ref, out_ref):
    @pl.when(pl.program_id(0) == 0)
    def _():
        out_ref[...] = jnp.zeros_like(out_ref)

    out_ref[...] += partial_sum(left_ref, right_ref)


def second_kernel(left_ref, right_ref, start_ref, panel_ref, cores_ref, total_ref):
    step = pl.program_id(0)

    @pl.when(step == 0)
    def _():
        total_ref[...] = start_ref[...]

    total_ref[...] += partial_sum(left_ref, right_ref)

    @pl.when(step == pl.num_programs(0) - 1)
    def _():
        for i in range(2):
            for p in range(2):
                span = slice(256 * p + 128 * i, 256 * p + 128 * i + 128)
                panel_ref[i, p] = total_ref[span, 0:128]
                cores_ref[i, 0, p] = total_ref[span, 128:256] * UNSCALE


STEPS = 4


def product_call(slot, left, right, start=None):
    depth = 16 // STEPS
    in_specs = [
        pl.BlockSpec((1, 2, 512, 128 * depth), lambda s: (slot, 0, 0, s)),
        pl.BlockSpec((16, depth, 2, 8, 128), lambda s: (0, s, 0, 0, 0)),
    ]
    estimate = cost(2 * 3 * 512 * 2048 * 256, 7 * 1024 * 1024)
    if start is None:
        return pl.pallas_call(
            first_kernel,
            grid=(STEPS,),
            in_specs=in_specs,
            out_specs=pl.BlockSpec((512, 256), lambda s: (0, 0)),
            out_shape=jax.ShapeDtypeStruct((512, 256), jnp.float32),
            compiler_params=params(),
            cost_estimate=estimate,
        )(left, right)
    return pl.pallas_call(
        second_kernel,
        grid=(STEPS,),
        in_specs=in_specs + [pl.BlockSpec((512, 256), lambda s: (0, 0))],
        out_specs=(
            pl.BlockSpec((2, 2, 128, 128), lambda s: (0, 0, 0, 0)),
            pl.BlockSpec((2, 1, 2, 128, 128), lambda s: (0, 0, 0, 0, 0)),
        ),
        out_shape=(
            jax.ShapeDtypeStruct((2, 2, 128, 128), jnp.float32),
            jax.ShapeDtypeStruct((2, 1, 2, 128, 128), jnp.float32),
        ),
        scratch_shapes=[pltpu.VMEM((512, 256), jnp.float32)],
        compiler_params=params(),
        cost_estimate=estimate,
    )(left, right, start)


def on_device(col_samples, row_samples, pivot_rows, rank_blocks, upper_inverse, upanel_left):
    f32 = jnp.float32
    vmem = pl.BlockSpec(memory_space=pltpu.VMEM)
    rows = lax.all_gather(row_samples, "col", axis=0)

    flipped = jnp.swapaxes(upper_inverse, 1, 2)
    flipped = lax.all_gather(flipped, "c", axis=1, tiled=True)
    last = lax.axis_size("col") - 1
    moved = lax.ppermute(
        flipped, CHIPS + ("col",), [(0, 1 * (last + 1) + last)]
    )
    entries = pl.pallas_call(
        entries_kernel,
        in_specs=[vmem, vmem],
        out_specs=vmem,
        out_shape=jax.ShapeDtypeStruct((4, 128), f32),
        compiler_params=params(),
        cost_estimate=cost(2**17, 2**18),
    )(pivot_rows, col_samples)
    packed = pl.pallas_call(
        pack_kernel,
        in_specs=[vmem, vmem],
        out_specs=vmem,
        out_shape=jax.ShapeDtypeStruct((16, 8, 128), f32),
        compiler_params=params(),
        cost_estimate=cost(2**17, 2**18),
    )(flipped, moved)
    packed = lax.all_to_all(packed, CHIPS, 0, 0)
    packed = jnp.concatenate([packed.reshape(128, 128)[8:], entries], axis=0)
    packed = lax.all_gather(packed, "col", axis=0)
    right, factor = pl.pallas_call(
        right_kernel,
        in_specs=[pl.BlockSpec(memory_space=pltpu.SMEM), vmem, vmem],
        out_specs=(vmem, vmem),
        out_shape=(jax.ShapeDtypeStruct((16, 16, 2, 8, 128), f32), jax.ShapeDtypeStruct((8, 128), f32)),
        compiler_params=params(),
        cost_estimate=cost(2 * 3 * 128 * 2048 * 256, 5 * 2**20),
    )(rank_blocks, packed, upanel_left[0])
    own = lax.all_to_all(right, CHIPS, 0, 0)
    left = pl.pallas_call(
        left_kernel,
        grid=(16,),
        in_specs=[
            pl.BlockSpec((8, 128), lambda z: (0, 0)),
            pl.BlockSpec((1, 2, 2, 128, 128), lambda z: (z, 0, 0, 0, 0)),
        ],
        out_specs=pl.BlockSpec((2, 2, 512, 128), lambda z: (0, 0, 0, z)),
        out_shape=jax.ShapeDtypeStruct((2, 2, 512, 2048), jnp.bfloat16),
        compiler_params=params(),
        cost_estimate=cost(2**24, 12 * 2**20),
    )(factor, rows)
    other = lax.ppermute(own, "c", [(0, 1), (1, 0)])
    total = product_call(0, left, own)
    return product_call(1, left, other, total)


def solution(mesh):
    chips = mesh.devices.reshape(4, 4, 2, 16)
    fine = Mesh(chips, ("y", "x", "c", "col"))
    row = ("y", "x", "c")
    in_specs = (
        P(row, None, "col", None),
        P(row, None, None, "col"),
        P(row, None),
        P(row),
        P(None, "col", row),
        P("col", None, None, None),
    )
    out_specs = (P(row, None, None, "col"), P(row, "col", None, None, None))
    return jax.shard_map(
        on_device, mesh=fine, in_specs=in_specs, out_specs=out_specs, check_vma=False
    )
```

time: 282 us -> 145 us (0.51)
  the two profiles are of different devices: /device:TPU:2 before, /device:TPU:1 now
where the time goes in v1:
time: 145 us; the launch traced here: 144 us
  blocking collectives  74.6 us (51%)
  Pallas kernels  23.4 us (16%)
  starting transfers between devices  19.8 us (14%)
  between operations  14.1 us (10%)
  waiting for transfers between devices  8.03 us (6%)
  local copies, waits for them, and re-layouts  4.47 us (3%)
    all_gather x1, blocking collectives, on_device(): packed = lax.all_gather(packed, 'col', axis=0)  41 us
    all_to_all x1, blocking collectives, on_device(): own = lax.all_to_all(right, CHIPS, 0, 0)  24.9 us
    pallas_call x1, Pallas kernels, on_device(): pl.pallas_call(left_kernel, grid=(16,), in_specs=[pl.BlockSpec((8, 128),...  11 us
    ppermute x1, starting transfers between devices, on_device(): other = lax.ppermute(own, 'c', [(0, 1), (1, 0)])  9.6 us
    all_gather x1, blocking collectives, on_device(): flipped = lax.all_gather(flipped, 'c', axis=1, tiled=True)  8.79 us
    ppermute x1, starting transfers between devices, on_device(): lax.ppermute(flipped, CHIPS + ('col',), [(0, 1 * (last + 1) + last)])  6.67 us
    pallas_call x1, Pallas kernels, product_call(): pl.pallas_call(second_kernel, grid=(STEPS,), in_specs=in_specs + [pl.Bloc...  5.51 us
    all_to_all x1, waiting for transfers between devices, on_device(): packed = lax.all_to_all(packed, CHIPS, 0, 0)  4.81 us
  transfers between devices with their start and end apart: 4, of which 2 were waited for; matrix products, arithmetic and copies ran while one was open for 0% of the time, Pallas kernels for 12%

profile of v1, /device:TPU:1, one launch (start us, length us, event | category | flops | bytes accessed | tf_op | source)
XLA Modules:
  0.0 144.4 jit_solution(222421594887283250)
XLA Ops:
  7.2 0.0 copy-start.1
  7.2 0.0 all-gather.5.cloned.1.call-start
  7.2 0.7 all-gather.5.cloned.1.call-update
  7.9 8.8 %all_gather.15.own_ref = f32[2,128,128]{2,1,0:T(8,128)S(1)} all-gather(f32[2,64,128]{2,1,0:T(8,128)} %bitcast.9), channel_id=1, replica_groups=mesh['y'=4,'x'=4,'c'=2,'col'=16] {'c'}, dimensions={1}, use_global_device_ids=true | all-gather | bytes 196608 | tf_op jit(solution)/shard_map/all_gather | solution.py:205
  16.7 6.7 %collective-permute-start = (f32[2,128,128]{2,1,0:T(8,128)S(1)}, f32[2,128,128]{2,1,0:T(8,128)S(1)}, u32[]{:S(2)}, u32[]{:S(2)}) collective-permute-start(f32[2,128,128]{2,1,0:T(8,128)S(1)} %all_gather.15.own_ref), channel_id=1, source_target_pairs={{0,47},{16,63}} | collective-permute-start | bytes 393224 | tf_op jit(solution)/shard_map/ppermute | solution.py:207
  23.4 2.5 %collective-permute-done.moved_ref = f32[2,128,128]{2,1,0:T(8,128)S(1)} collective-permute-done((f32[2,128,128]{2,1,0:T(8,128)S(1)}, f32[2,128,128]{2,1,0:T(8,128)S(1)}, u32[]{:S(2)}, u32[]{:S(2)}) %collective-permute-start) | collective-permute-done | bytes 131104 | tf_op jit(solution)/shard_map/ppermute | solution.py:207
  25.9 0.7 shard_map.77
  26.6 3.5 %all-to-all-start = ((f32[16,8,128]{2,1,0:T(8,128)}), f32[16,8,128]{2,1,0:T(8,128)S(1)}, u32[]{:S(2)}, u32[]{:S(2)}) async-start(f32[16,8,128]{2,1,0:T(8,128)} %shard_map.77), calls=%async_computation | async-start | bytes 131072 | tf_op jit(solution)/shard_map/all_to_all | solution.py:226
  30.1 0.0 copy-start.2
  30.1 0.9 copy-done.2
  31.1 0.0 copy-start.3
  31.1 0.7 copy-done.3
  31.8 4.8 %all-to-all-done = f32[16,8,128]{2,1,0:T(8,128)S(1)} async-done(((f32[16,8,128]{2,1,0:T(8,128)}), f32[16,8,128]{2,1,0:T(8,128)S(1)}, u32[]{:S(2)}, u32[]{:S(2)}) %all-to-all-start) | async-done | bytes 65568 | tf_op jit(solution)/shard_map/all_to_all | solution.py:226
  36.6 41.0 %all-gather.2.rows_ref = f32[16,124,128]{2,1,0:T(8,128)S(1)} all-gather(f32[1,124,128]{2,1,0:T(8,128)S(1)} %maximum_bitcast_fusion), channel_id=2, replica_groups=mesh['y'=4,'x'=4,'c'=2,'col'=16] {'col'}, dimensions={0}, use_global_device_ids=true | all-gather | bytes 1079296 | tf_op jit(solution)/shard_map/all_gather | solution.py:228
  77.6 0.0 copy-done.1
  77.6 0.0 copy-start.4
  77.6 0.7 copy-done.4
  78.3 1.7 %shard_map.79 = (f32[16,16,2,8,128]{4,3,2,1,0:T(8,128)S(1)}, f32[8,128]{1,0:T(8,128)S(1)}) custom-call(s32[2]{0:T(128)S(1)} %copy-done.4, f32[16,124,128]{2,1,0:T(8,128)S(1)} %all-gather.2.rows_ref, f32[2,2048,128]{2,1,0:T(8,128)S(1)} %bitcast.8), custom_call_target="tpu_custom_call" | custom-call | flops 402653184 | bytes 5242880 | tf_op jit(solution)/shard_map/pallas_call | solution.py:229
  80.0 24.9 %all_to_all.10.right_ref = f32[16,16,2,8,128]{4,3,2,1,0:T(8,128)S(1)} all-to-all(f32[16,16,2,8,128]{4,3,2,1,0:T(8,128)S(1)} %get-tuple-element.5), channel_id=1, replica_groups=mesh['y'=4,'x'=4,'c'=2,'col'=16] {'y','x'}, dimensions={0} | all-to-all | bytes 4194304 | tf_op jit(solution)/shard_map/all_to_all | solution.py:237
  104.9 9.6 %collective-permute-start.1 = (f32[16,16,2,8,128]{4,3,2,1,0:T(8,128)S(1)}, f32[16,16,2,8,128]{4,3,2,1,0:T(8,128)}, u32[]{:S(2)}, u32[]{:S(2)}) collective-permute-start(f32[16,16,2,8,128]{4,3,2,1,0:T(8,128)S(1)} %all_to_all.10.right_ref), channel_id=1, source_target_pairs={{0,16},{16,0},{1,17},{17,1},{2,18},{18,2},{3,19},{19,3},{4,20},{20... | collective-permute-start | bytes 6291464 | tf_op jit(solution)/shard_map/ppermute | solution.py:250
  114.5 0.0 all-gather.5.cloned.1.call-done
  114.5 0.0 copy-start
  114.5 2.2 %copy-done = f32[32,2,128,128]{3,2,1,0:T(8,128)S(1)} copy-done((f32[32,2,128,128]{3,2,1,0:T(8,128)S(1)}, f32[32,2,128,128]{3,2,1,0:T(8,128)}, u32[]{:S(2)}) %copy-start) | copy-done | bytes 4194328
  116.7 11.0 %shard_map.80.left_ref = bf16[2,2,512,2048]{3,2,1,0:T(8,128)(2,1)} custom-call(f32[8,128]{1,0:T(8,128)S(1)} %get-tuple-element.4.factor_ref, f32[16,2,2,128,128]{4,3,2,1,0:T(8,128)S(1)} %bitcast.7), custom_call_target="tpu_custom_call" | custom-call | flops 16777216 | bytes 12582912 | tf_op jit(solution)/shard_map/pallas_call | solution.py:238
  127.6 4.4 %shard_map.81.start_ref = f32[512,256]{1,0:T(8,128)S(1)} custom-call(bf16[2,2,512,2048]{3,2,1,0:T(8,128)(2,1)} %shard_map.80.left_ref, f32[16,16,2,8,128]{4,3,2,1,0:T(8,128)S(1)} %all_to_all.10.right_ref), custom_call_target="tpu_custom_call" | custom-call | flops 1610612736 | bytes 7340032 | tf_op jit(solution)/shard_map/pallas_call | solution.py:172
  132.0 0.0 collective-permute-done.1.right_ref
  132.0 5.5 %shard_map.82 = (f32[2,2,128,128]{3,2,1,0:T(8,128)}, f32[2,1,2,128,128]{4,3,2,1,0:T(8,128)}) custom-call(bf16[2,2,512,2048]{3,2,1,0:T(8,128)(2,1)} %shard_map.80.left_ref, f32[16,16,2,8,128]{4,3,2,1,0:T(8,128)} %collective-permute-done.1.right_ref, f32[512,256]{1,0:T(8,128)S(1)} %shard_map.81.start_ref), custom_call_target="tpu_custom_call" | custom-call | flops 1610612736 | bytes 7340032 | tf_op jit(solution)/shard_map/pallas_call | solution.py:181
  (3 shorter events, 0.1 us)
Async XLA Ops:
  7.2 70.4 %copy-start.1 = (f32[1,2,2048,128]{3,2,1,0:T(8,128)S(1)}, f32[1,2,2048,128]{3,2,1,0:T(8,128)}, u32[]{:S(2)}) copy-start(f32[1,2,2048,128]{3,2,1,0:T(8,128)} %param.11) | copy-start | bytes 6291460
  7.2 107.3 %all-gather.5.cloned.1.call-start = ((), (), s32[]{:S(2)}) async-start(), calls=%async_computation.2 | async-start | bytes 4456448 | tf_op jit(solution)/shard_map/all_gather | solution.py:202
  16.7 9.2 %collective-permute-start = (f32[2,128,128]{2,1,0:T(8,128)S(1)}, f32[2,128,128]{2,1,0:T(8,128)S(1)}, u32[]{:S(2)}, u32[]{:S(2)}) collective-permute-start(f32[2,128,128]{2,1,0:T(8,128)S(1)} %all_gather.15.own_ref), channel_id=1, source_target_pairs={{0,47},{16,63}} | collective-permute-start | bytes 393224 | tf_op jit(solution)/shard_map/ppermute | solution.py:207
  26.6 10.0 %all-to-all-start = ((f32[16,8,128]{2,1,0:T(8,128)}), f32[16,8,128]{2,1,0:T(8,128)S(1)}, u32[]{:S(2)}, u32[]{:S(2)}) async-start(f32[16,8,128]{2,1,0:T(8,128)} %shard_map.77), calls=%async_computation | async-start | bytes 131072 | tf_op jit(solution)/shard_map/all_to_all | solution.py:226
  30.1 1.0 copy-start.2
  31.1 0.7 copy-start.3
  77.6 0.7 copy-start.4
  104.9 27.2 %collective-permute-start.1 = (f32[16,16,2,8,128]{4,3,2,1,0:T(8,128)S(1)}, f32[16,16,2,8,128]{4,3,2,1,0:T(8,128)}, u32[]{:S(2)}, u32[]{:S(2)}) collective-permute-start(f32[16,16,2,8,128]{4,3,2,1,0:T(8,128)S(1)} %all_to_all.10.right_ref), channel_id=1, source_target_pairs={{0,16},{16,0},{1,17},{17,1},{2,18},{18,2},{3,19},{19,3},{4,20},{20... | collective-permute-start | bytes 6291464 | tf_op jit(solution)/shard_map/ppermute | solution.py:250
  114.5 2.2 %copy-start = (f32[32,2,128,128]{3,2,1,0:T(8,128)S(1)}, f32[32,2,128,128]{3,2,1,0:T(8,128)}, u32[]{:S(2)}) copy-start(f32[32,2,128,128]{3,2,1,0:T(8,128)} %all-gather.5.cloned.1.call-done) | copy-start | bytes 12582916
Sparse Core Ops, SparseCore 0:
  10.1 84.2 all-gather.4

commit v2 on v1

v2 whole, which is shorter than its diff:
```python
import jax
import jax.numpy as jnp
from jax import lax
from jax.experimental import pallas as pl
from jax.experimental.pallas import tpu as pltpu
from jax.sharding import Mesh
from jax.sharding import PartitionSpec as P

RANK_STEP = 16
CHIPS = ("y", "x")
DOWN_INVERSE, UP_INVERSE = 2.0 ** -16, 2.0 ** 16
DOWN_PRODUCT, UP_PRODUCT = 2.0 ** -24, 2.0 ** 24
PAIRS = 8
DEPTH = 2


def params(mebibytes=24):
    return pltpu.CompilerParams(vmem_limit_bytes=mebibytes * 1024 * 1024)


def cost(flops, moved):
    return pl.CostEstimate(flops=flops, bytes_accessed=moved, transcendentals=0)


def split(x):
    high = x.astype(jnp.bfloat16)
    low = (x - high.astype(jnp.float32)).astype(jnp.bfloat16)
    return high, low


def dot(a, b):
    return jnp.dot(a, b, preferred_element_type=jnp.float32)


def entries_kernel(ranks_ref, pivots_ref, cols_ref, out_ref):
    levels = lax.broadcasted_iota(jnp.int32, (1, cols_ref.shape[3]), 1)
    width = cols_ref.shape[2]
    rows = lax.broadcasted_iota(jnp.int32, cols_ref.shape[2:], 0) + lax.axis_index("col") * width
    for i in range(2):
        hit = jnp.logical_and(pivots_ref[i : i + 1, :] == rows, levels < RANK_STEP * ranks_ref[i])
        for p in range(2):
            out_ref[2 * i + p : 2 * i + p + 1, :] = jnp.sum(
                jnp.where(hit, cols_ref[i, p], 0.0), axis=0, keepdims=True
            )


def pack_kernel(own_ref, moved_ref, out_ref):
    chip = lax.axis_index("y") * lax.axis_size("x") + lax.axis_index("x")
    place = lax.axis_index("col")
    swap = jnp.logical_and(chip == 1, place == lax.axis_size("col") - 1)
    core = lax.axis_index("c")
    parts = []
    for p in range(2):
        block = jnp.where(swap, moved_ref[p], own_ref[p])
        parts.append(block.T.reshape(16, 8, 128))
    first = lax.broadcasted_iota(jnp.int32, (16, 8, 128), 1) < 4
    low = jnp.where(first, parts[0], jnp.roll(parts[1], 4, axis=1))
    high = jnp.where(first, jnp.roll(parts[0], 4, axis=1), parts[1])
    out_ref[...] = jnp.where(core == 0, low, high)


def right_kernel(rows_ref, left_ref, out_ref, factor_ref):
    place = lax.axis_index("col")
    corner = rows_ref[15, 0:8, :]
    total = None
    for q in range(16):
        if q == 0:
            x = jnp.concatenate([corner, jnp.zeros((120, 128), jnp.float32)], axis=0)
        elif q == 1:
            x = jnp.concatenate(
                [rows_ref[0:15, 0:8, :].reshape(120, 128), jnp.zeros((8, 128), jnp.float32)], axis=0
            )
        else:
            x = rows_ref[:, 8 * q - 8 : 8 * q, :].reshape(128, 128)
        y = jnp.concatenate(
            [left_ref[0, 128 * q : 128 * q + 128, :], left_ref[1, 128 * q : 128 * q + 128, :]], axis=1
        )
        xh, xl = split(x)
        yh, yl = split(y * DOWN_PRODUCT)
        term = dot(xh, yh) + (dot(xh, yl) + dot(xl, yh))
        total = term if total is None else total + term
    by_real = total[:, :128].reshape(16, 8, 128)
    by_imag = jnp.roll(total[:, 128:].reshape(16, 8, 128), 4, axis=1)
    first = lax.broadcasted_iota(jnp.int32, (16, 8, 128), 1) < 4
    product = by_real + jnp.where(first, -by_imag, by_imag)
    start = pl.multiple_of(jnp.maximum(place - 1, 0) * 8, 8)
    block = rows_ref[:, pl.ds(start, 8), :]
    which = lax.broadcasted_iota(jnp.int32, (16, 8, 128), 0)
    block = jnp.where(jnp.logical_and(place == 1, which == 15), 0.0, block)
    at_zero = jnp.where(which == 0, corner[None], 0.0)
    block = jnp.where(place == 0, at_zero, block)
    lower = lax.broadcasted_iota(jnp.int32, (PAIRS, 8, 128), 1) < 4
    for n, x in enumerate((block * DOWN_INVERSE, product)):
        x = x.reshape(PAIRS, 2, 8, 128)
        even, odd = x[:, 0], x[:, 1]
        real = jnp.where(lower, even, jnp.roll(odd, 4, axis=1))
        imag = jnp.where(lower, jnp.roll(even, 4, axis=1), odd)
        for d in range(16):
            out_ref[d, :, 2 * n] = real
            out_ref[d, :, 2 * n + 1] = imag
    entries = jnp.sum(rows_ref[:, 120:124, :], axis=0)
    for i in range(2):
        real, imag = entries[2 * i : 2 * i + 1], entries[2 * i + 1 : 2 * i + 2]
        magnitude = jnp.maximum(real * real + imag * imag, 1.0)
        factor_ref[2 * i : 2 * i + 1, :] = real / magnitude
        factor_ref[2 * i + 1 : 2 * i + 2, :] = -imag / magnitude
    factor_ref[4:8, :] = jnp.zeros((4, 128), jnp.float32)


def product(own, rows_ref, right_ref, held_ref, sems):
    copies = [pltpu.make_async_copy(rows_ref.at[z], held_ref.at[z], sems.at[z]) for z in range(16)]
    for copy in copies:
        copy.start()
    core = lax.axis_index("c")
    turn = core if own else 1 - core
    shift = jnp.where(turn == 0, 4, 124)
    keep = ((lax.broadcasted_iota(jnp.int32, (128, 128), 1) & 7) < 4) == (turn == 0)
    total = None
    for step in range(PAIRS // DEPTH):
        lefts, rights = [], []
        for n in range(step * DEPTH, step * DEPTH + DEPTH):
            copies[2 * n].wait()
            copies[2 * n + 1].wait()
            blocks = []
            for p in range(2):
                for i in range(2):
                    still = held_ref[2 * n + turn, i, p]
                    moved = pltpu.roll(held_ref[2 * n + 1 - turn, i, p], shift, 1)
                    blocks.append(jnp.where(keep, still, moved))
            lefts.append(jnp.concatenate(blocks, axis=0))
        for block in right_ref(step):
            rights.append(jnp.concatenate([block[:, m].reshape(128, 128) for m in range(4)], axis=1))
        rh, rl = split(jnp.concatenate(rights, axis=0))
        lh, ll = split(jnp.concatenate(lefts, axis=1))
        term = dot(lh, rh) + (dot(lh, rl) + dot(ll, rh))
        total = term if total is None else total + term
    return total


def first_kernel(rows_ref, right_ref, out_ref, held_ref, sems):
    def right(step):
        return [right_ref[:, n] for n in range(step * DEPTH, step * DEPTH + DEPTH)]

    out_ref[...] = product(True, rows_ref, right, held_ref, sems)


def second_kernel(factor_ref, start_ref, rows_ref, right_ref, panel_ref, cores_ref, held_ref, sems, near_ref, near_sems):
    copies = [
        pltpu.make_async_copy(right_ref.at[:, n], near_ref.at[n], near_sems.at[n]) for n in range(PAIRS)
    ]
    for copy in copies:
        copy.start()

    def right(step):
        span = range(step * DEPTH, step * DEPTH + DEPTH)
        for n in span:
            copies[n].wait()
        return [near_ref[n] for n in span]

    total = start_ref[...] + product(False, rows_ref, right, held_ref, sems)
    columns = factor_ref[...].T
    for i in range(2):
        fr, fi = columns[:, 2 * i : 2 * i + 1], columns[:, 2 * i + 1 : 2 * i + 2]
        by_real, by_imag = total[128 * i : 128 * i + 128], total[256 + 128 * i : 384 + 128 * i]
        for n, up in enumerate((UP_INVERSE, UP_PRODUCT)):
            re, im = slice(256 * n, 256 * n + 128), slice(256 * n + 128, 256 * n + 256)
            real = by_real[:, re] - by_imag[:, im]
            imag = by_real[:, im] + by_imag[:, re]
            pair = (fr * real - fi * imag) * up, (fr * imag + fi * real) * up
            for p in range(2):
                if n == 0:
                    panel_ref[i, p] = pair[p]
                else:
                    cores_ref[i, 0, p] = pair[p]


def first_call(rows, right):
    vmem = pl.BlockSpec(memory_space=pltpu.VMEM)
    return pl.pallas_call(
        first_kernel,
        in_specs=[pl.BlockSpec(memory_space=pltpu.HBM), vmem],
        out_specs=vmem,
        out_shape=jax.ShapeDtypeStruct((512, 512), jnp.float32),
        scratch_shapes=[pltpu.VMEM((16, 2, 2, 128, 128), jnp.float32), pltpu.SemaphoreType.DMA((16,))],
        compiler_params=params(48),
        cost_estimate=cost(2 * 3 * 512 * 1024 * 512, 7 * 2**20),
    )(rows, right)


def second_call(factor, start, rows, right):
    vmem = pl.BlockSpec(memory_space=pltpu.VMEM)
    hbm = pl.BlockSpec(memory_space=pltpu.HBM)
    return pl.pallas_call(
        second_kernel,
        in_specs=[vmem, vmem, hbm, hbm],
        out_specs=(vmem, vmem),
        out_shape=(
            jax.ShapeDtypeStruct((2, 2, 128, 128), jnp.float32),
            jax.ShapeDtypeStruct((2, 1, 2, 128, 128), jnp.float32),
        ),
        scratch_shapes=[
            pltpu.VMEM((16, 2, 2, 128, 128), jnp.float32),
            pltpu.SemaphoreType.DMA((16,)),
            pltpu.VMEM((PAIRS, 16, 4, 8, 128), jnp.float32),
            pltpu.SemaphoreType.DMA((PAIRS,)),
        ],
        compiler_params=params(48),
        cost_estimate=cost(2 * 3 * 512 * 1024 * 512, 8 * 2**20),
    )(factor, start, rows, right)


def on_device(col_samples, row_samples, pivot_rows, rank_blocks, upper_inverse, upanel_left):
    f32 = jnp.float32
    vmem = pl.BlockSpec(memory_space=pltpu.VMEM)
    rows = lax.all_gather(row_samples, "col", axis=0)

    flipped = jnp.swapaxes(upper_inverse, 1, 2)
    flipped = lax.all_gather(flipped, "c", axis=1, tiled=True)
    last = lax.axis_size("col") - 1
    moved = lax.ppermute(
        flipped, CHIPS + ("col",), [(0, 1 * (last + 1) + last)]
    )
    entries = pl.pallas_call(
        entries_kernel,
        in_specs=[pl.BlockSpec(memory_space=pltpu.SMEM), vmem, vmem],
        out_specs=vmem,
        out_shape=jax.ShapeDtypeStruct((4, 128), f32),
        compiler_params=params(),
        cost_estimate=cost(2**17, 2**18),
    )(rank_blocks, pivot_rows, col_samples)
    packed = pl.pallas_call(
        pack_kernel,
        in_specs=[vmem, vmem],
        out_specs=vmem,
        out_shape=jax.ShapeDtypeStruct((16, 8, 128), f32),
        compiler_params=params(),
        cost_estimate=cost(2**17, 2**18),
    )(flipped, moved)
    packed = lax.all_to_all(packed, CHIPS, 0, 0)
    packed = jnp.concatenate([packed.reshape(128, 128)[8:], entries], axis=0)
    packed = lax.all_gather(packed, "col", axis=0)
    right, factor = pl.pallas_call(
        right_kernel,
        in_specs=[vmem, vmem],
        out_specs=(vmem, vmem),
        out_shape=(jax.ShapeDtypeStruct((16, PAIRS, 4, 8, 128), f32), jax.ShapeDtypeStruct((8, 128), f32)),
        compiler_params=params(),
        cost_estimate=cost(2 * 3 * 128 * 2048 * 256, 5 * 2**20),
    )(packed, upanel_left[0])
    own = lax.all_to_all(right, CHIPS, 0, 0)
    other = lax.ppermute(own, "c", [(0, 1), (1, 0)])
    return second_call(factor, first_call(rows, own), rows, other)


def solution(mesh):
    chips = mesh.devices.reshape(4, 4, 2, 16)
    fine = Mesh(chips, ("y", "x", "c", "col"))
    row = ("y", "x", "c")
    in_specs = (
        P(row, None, "col", None),
        P(row, None, None, "col"),
        P(row, None),
        P(row),
        P(None, "col", row),
        P("col", None, None, None),
    )
    out_specs = (P(row, None, None, "col"), P(row, "col", None, None, None))
    return jax.shard_map(
        on_device, mesh=fine, in_specs=in_specs, out_specs=out_specs, check_vma=False
    )
```

time: 145 us -> 131 us (0.903)
  Pallas kernels: 23.4 us -> 12.5 us
  local copies, waits for them, and re-layouts: 4.47 us -> 2.29 us
    pallas_call x5 -> x4, Pallas kernels: 22.6 us -> 11.8 us  [the longest x1 6.17 us: second_call(): pl.pallas_call(second_kernel, in_specs=[vmem, vmem, hbm, hbm], out_specs=...]
    unnamed x10 -> x8, local copies, waits for them, and re-layouts: 4.47 us -> 2.28 us
  transfers between devices with their start and end apart: 4 -> 4, of which waited for: 2 -> 2; matrix products, arithmetic and copies ran while one was open for 0% -> 0% of each run, Pallas kernels for 12% -> 5%
where the time goes in v2:
time: 131 us; the launch traced here: 130 us
  blocking collectives  74.6 us (57%)
  starting transfers between devices  19.8 us (15%)
  between operations  14.1 us (11%)
  Pallas kernels  12.5 us (10%)
  waiting for transfers between devices  6.83 us (5%)
  local copies, waits for them, and re-layouts  2.29 us (2%)
    all_gather x1, blocking collectives, on_device(): packed = lax.all_gather(packed, 'col', axis=0)  41 us
    all_to_all x1, blocking collectives, on_device(): own = lax.all_to_all(right, CHIPS, 0, 0)  24.9 us
    ppermute x1, starting transfers between devices, on_device(): other = lax.ppermute(own, 'c', [(0, 1), (1, 0)])  9.6 us
    all_gather x1, blocking collectives, on_device(): flipped = lax.all_gather(flipped, 'c', axis=1, tiled=True)  8.79 us
    ppermute x1, starting transfers between devices, on_device(): lax.ppermute(flipped, CHIPS + ('col',), [(0, 1 * (last + 1) + last)])  6.67 us
    pallas_call x1, Pallas kernels, second_call(): pl.pallas_call(second_kernel, in_specs=[vmem, vmem, hbm, hbm], out_specs=...  6.17 us
    pallas_call x1, Pallas kernels, first_call(): pl.pallas_call(first_kernel, in_specs=[pl.BlockSpec(memory_space=pltpu.HB...  3.91 us
    all_to_all x1, waiting for transfers between devices, on_device(): packed = lax.all_to_all(packed, CHIPS, 0, 0)  3.61 us
  transfers between devices with their start and end apart: 4, of which 2 were waited for; matrix products, arithmetic and copies ran while one was open for 0% of the time, Pallas kernels for 5%

profile of v2, /device:TPU:1, one launch (start us, length us, event | category | flops | bytes accessed | tf_op | source)
XLA Modules:
  0.0 130.2 jit_solution(14541247514150161547)
XLA Ops:
  7.2 0.0 copy-start
  7.2 0.0 all-gather.5.cloned.1.call-start
  7.2 0.7 all-gather.5.cloned.1.call-update
  7.9 8.8 %all_gather.15.own_ref = f32[2,128,128]{2,1,0:T(8,128)S(1)} all-gather(f32[2,64,128]{2,1,0:T(8,128)} %bitcast.10), channel_id=1, replica_groups=mesh['y'=4,'x'=4,'c'=2,'col'=16] {'c'}, dimensions={1}, use_global_device_ids=true | all-gather | bytes 196608 | tf_op jit(solution)/shard_map/all_gather | solution.py:218
  16.7 6.7 %collective-permute-start = (f32[2,128,128]{2,1,0:T(8,128)S(1)}, f32[2,128,128]{2,1,0:T(8,128)S(1)}, u32[]{:S(2)}, u32[]{:S(2)}) collective-permute-start(f32[2,128,128]{2,1,0:T(8,128)S(1)} %all_gather.15.own_ref), channel_id=1, source_target_pairs={{0,47},{16,63}} | collective-permute-start | bytes 393224 | tf_op jit(solution)/shard_map/ppermute | solution.py:220
  23.4 2.5 %collective-permute-done.moved_ref = f32[2,128,128]{2,1,0:T(8,128)S(1)} collective-permute-done((f32[2,128,128]{2,1,0:T(8,128)S(1)}, f32[2,128,128]{2,1,0:T(8,128)S(1)}, u32[]{:S(2)}, u32[]{:S(2)}) %collective-permute-start) | collective-permute-done | bytes 131104 | tf_op jit(solution)/shard_map/ppermute | solution.py:220
  25.9 0.7 shard_map.77
  26.6 3.5 %all-to-all-start = ((f32[16,8,128]{2,1,0:T(8,128)}), f32[16,8,128]{2,1,0:T(8,128)S(1)}, u32[]{:S(2)}, u32[]{:S(2)}) async-start(f32[16,8,128]{2,1,0:T(8,128)} %shard_map.77), calls=%async_computation | async-start | bytes 131072 | tf_op jit(solution)/shard_map/all_to_all | solution.py:239
  30.1 0.0 copy-start.1
  30.1 0.9 copy-done.1
  31.1 0.0 copy-start.2
  31.1 0.7 copy-done.2
  31.8 0.0 copy-start.3
  31.8 0.7 copy-done.3
  32.4 0.6 shard_map.78
  33.0 3.6 %all-to-all-done = f32[16,8,128]{2,1,0:T(8,128)S(1)} async-done(((f32[16,8,128]{2,1,0:T(8,128)}), f32[16,8,128]{2,1,0:T(8,128)S(1)}, u32[]{:S(2)}, u32[]{:S(2)}) %all-to-all-start) | async-done | bytes 65568 | tf_op jit(solution)/shard_map/all_to_all | solution.py:239
  36.6 41.0 %all-gather.2.rows_ref = f32[16,124,128]{2,1,0:T(8,128)S(1)} all-gather(f32[1,124,128]{2,1,0:T(8,128)S(1)} %maximum_bitcast_fusion), channel_id=2, replica_groups=mesh['y'=4,'x'=4,'c'=2,'col'=16] {'col'}, dimensions={0}, use_global_device_ids=true | all-gather | bytes 1079296 | tf_op jit(solution)/shard_map/all_gather | solution.py:241
  77.6 0.0 copy-done
  77.6 1.1 shard_map.79
  78.8 24.9 %all_to_all.10.right_ref = f32[16,8,4,8,128]{4,3,2,1,0:T(8,128)S(1)} all-to-all(f32[16,8,4,8,128]{4,3,2,1,0:T(8,128)S(1)} %get-tuple-element.5), channel_id=1, replica_groups=mesh['y'=4,'x'=4,'c'=2,'col'=16] {'y','x'}, dimensions={0} | all-to-all | bytes 4194304 | tf_op jit(solution)/shard_map/all_to_all | solution.py:250
  103.6 9.6 %collective-permute-start.1 = (f32[16,8,4,8,128]{4,3,2,1,0:T(8,128)S(1)}, f32[16,8,4,8,128]{4,3,2,1,0:T(8,128)}, u32[]{:S(2)}, u32[]{:S(2)}) collective-permute-start(f32[16,8,4,8,128]{4,3,2,1,0:T(8,128)S(1)} %all_to_all.10.right_ref), channel_id=1, source_target_pairs={{0,16},{16,0},{1,17},{17,1},{2,18},{18,2},{3,19},{19,3},{4,20},{20... | collective-permute-start | bytes 6291464 | tf_op jit(solution)/shard_map/ppermute | solution.py:251
  113.2 0.0 all-gather.5.cloned.1.call-done
  113.3 3.9 %shard_map.80.start_ref = f32[512,512]{1,0:T(8,128)S(1)} custom-call(f32[16,2,2,128,128]{4,3,2,1,0:T(8,128)} %bitcast.8, f32[16,8,4,8,128]{4,3,2,1,0:T(8,128)S(1)} %all_to_all.10.right_ref), custom_call_target="tpu_custom_call" | custom-call | flops 1610612736 | bytes 7340032 | tf_op jit(solution)/shard_map/pallas_call | solution.py:179
  117.2 0.0 collective-permute-done.1.right_ref
  117.2 6.2 %shard_map.81 = (f32[2,2,128,128]{3,2,1,0:T(8,128)}, f32[2,1,2,128,128]{4,3,2,1,0:T(8,128)}) custom-call(f32[8,128]{1,0:T(8,128)S(1)} %get-tuple-element.4.factor_ref, f32[512,512]{1,0:T(8,128)S(1)} %shard_map.80.start_ref, f32[16,2,2,128,128]{4,3,2,1,0:T(8,128)} %bitcast.9, f32[16,8,4,8,128]{4,3,2,1,0:T(8,128)} %collective-permute-done.1.right_ref), custom_call_target="tpu_custom_call" | custom-call | flops 1610612736 | bytes 8388608 | tf_op jit(solution)/shard_map/pallas_call | solution.py:193
  (2 shorter events, 0.0 us)
Async XLA Ops:
  7.2 70.4 %copy-start = (f32[1,2,2048,128]{3,2,1,0:T(8,128)S(1)}, f32[1,2,2048,128]{3,2,1,0:T(8,128)}, u32[]{:S(2)}) copy-start(f32[1,2,2048,128]{3,2,1,0:T(8,128)} %param.11) | copy-start | bytes 6291460
  7.2 106.1 %all-gather.5.cloned.1.call-start = ((), (), s32[]{:S(2)}) async-start(), calls=%async_computation.2 | async-start | bytes 4456448 | tf_op jit(solution)/shard_map/all_gather | solution.py:215
  16.7 9.2 %collective-permute-start = (f32[2,128,128]{2,1,0:T(8,128)S(1)}, f32[2,128,128]{2,1,0:T(8,128)S(1)}, u32[]{:S(2)}, u32[]{:S(2)}) collective-permute-start(f32[2,128,128]{2,1,0:T(8,128)S(1)} %all_gather.15.own_ref), channel_id=1, source_target_pairs={{0,47},{16,63}} | collective-permute-start | bytes 393224 | tf_op jit(solution)/shard_map/ppermute | solution.py:220
  26.6 10.0 %all-to-all-start = ((f32[16,8,128]{2,1,0:T(8,128)}), f32[16,8,128]{2,1,0:T(8,128)S(1)}, u32[]{:S(2)}, u32[]{:S(2)}) async-start(f32[16,8,128]{2,1,0:T(8,128)} %shard_map.77), calls=%async_computation | async-start | bytes 131072 | tf_op jit(solution)/shard_map/all_to_all | solution.py:239
  30.1 1.0 copy-start.1
  31.1 0.7 copy-start.2
  31.8 0.7 copy-start.3
  103.6 13.6 %collective-permute-start.1 = (f32[16,8,4,8,128]{4,3,2,1,0:T(8,128)S(1)}, f32[16,8,4,8,128]{4,3,2,1,0:T(8,128)}, u32[]{:S(2)}, u32[]{:S(2)}) collective-permute-start(f32[16,8,4,8,128]{4,3,2,1,0:T(8,128)S(1)} %all_to_all.10.right_ref), channel_id=1, source_target_pairs={{0,16},{16,0},{1,17},{17,1},{2,18},{18,2},{3,19},{19,3},{4,20},{20... | collective-permute-start | bytes 6291464 | tf_op jit(solution)/shard_map/ppermute | solution.py:251
Sparse Core Ops, SparseCore 0:
  10.1 84.4 all-gather.4

commit v3 on v2

--- a/solution.py
+++ b/solution.py
@@ -42,36 +42,48 @@
             out_ref[2 * i + p : 2 * i + p + 1, :] = jnp.sum(
                 jnp.where(hit, cols_ref[i, p], 0.0), axis=0, keepdims=True
             )
-
-
-def pack_kernel(own_ref, moved_ref, out_ref):
-    chip = lax.axis_index("y") * lax.axis_size("x") + lax.axis_index("x")
-    place = lax.axis_index("col")
-    swap = jnp.logical_and(chip == 1, place == lax.axis_size("col") - 1)
-    core = lax.axis_index("c")
-    parts = []
-    for p in range(2):
-        block = jnp.where(swap, moved_ref[p], own_ref[p])
-        parts.append(block.T.reshape(16, 8, 128))
-    first = lax.broadcasted_iota(jnp.int32, (16, 8, 128), 1) < 4
-    low = jnp.where(first, parts[0], jnp.roll(parts[1], 4, axis=1))
-    high = jnp.where(first, jnp.roll(parts[0], 4, axis=1), parts[1])
-    out_ref[...] = jnp.where(core == 0, low, high)
+    out_ref[4:8, :] = jnp.zeros((4, 128), jnp.float32)
+
+
+def sublanes(shape):
+    return lax.broadcasted_iota(jnp.int32, shape, len(shape) - 2)
+
+
+def interleave(even, odd):
+    row = sublanes(even.shape)
+
+    def turn(x, n):
+        return jnp.roll(x, n, axis=x.ndim - 2)
+
+    even2, odd2, even4, odd4, even6, odd6 = (turn(x, n) for n in (2, 4, 6) for x in (even, odd))
+    low = jnp.where(row < 2, even, jnp.where(row < 4, odd2, jnp.where(row < 6, even2, odd4)))
+    high = jnp.where(row < 2, even4, jnp.where(row < 4, odd6, jnp.where(row < 6, even6, odd)))
+    return low, high
+
+
+def pack_kernel(block_ref, out_ref):
+    rows = jnp.concatenate([block_ref[0].T, block_ref[1].T], axis=1).reshape(16, 8, 128)
+    low, high = interleave(rows[:8], rows[8:])
+    out_ref[0:8] = low
+    out_ref[8:16] = high
+
+
+def straight(x):
+    lane = lax.broadcasted_iota(jnp.int32, x.shape, x.ndim - 1)
+    same = (sublanes(x.shape) < 4) == (lane < 64)
+    return jnp.where(same, x, jnp.roll(jnp.roll(x, 4, axis=x.ndim - 2), 64, axis=x.ndim - 1))
 
 
 def right_kernel(rows_ref, left_ref, out_ref, factor_ref):
     place = lax.axis_index("col")
-    corner = rows_ref[15, 0:8, :]
+    last = rows_ref[0, 120:126, :]
+    corner = straight(jnp.concatenate([last[0:2], jnp.zeros((2, 128), jnp.float32), last[2:6]], axis=0))
     total = None
     for q in range(16):
         if q == 0:
             x = jnp.concatenate([corner, jnp.zeros((120, 128), jnp.float32)], axis=0)
-        elif q == 1:
-            x = jnp.concatenate(
-                [rows_ref[0:15, 0:8, :].reshape(120, 128), jnp.zeros((8, 128), jnp.float32)], axis=0
-            )
         else:
-            x = rows_ref[:, 8 * q - 8 : 8 * q, :].reshape(128, 128)
+            x = straight(rows_ref[:, 8 * q - 8 : 8 * q, :]).reshape(128, 128)
         y = jnp.concatenate(
             [left_ref[0, 128 * q : 128 * q + 128, :], left_ref[1, 128 * q : 128 * q + 128, :]], axis=1
         )
@@ -81,24 +93,18 @@
         total = term if total is None else total + term
     by_real = total[:, :128].reshape(16, 8, 128)
     by_imag = jnp.roll(total[:, 128:].reshape(16, 8, 128), 4, axis=1)
-    first = lax.broadcasted_iota(jnp.int32, (16, 8, 128), 1) < 4
-    product = by_real + jnp.where(first, -by_imag, by_imag)
+    product = by_real + jnp.where(sublanes((16, 8, 128)) < 4, -by_imag, by_imag)
     start = pl.multiple_of(jnp.maximum(place - 1, 0) * 8, 8)
-    block = rows_ref[:, pl.ds(start, 8), :]
+    block = straight(rows_ref[:, pl.ds(start, 8), :])
     which = lax.broadcasted_iota(jnp.int32, (16, 8, 128), 0)
-    block = jnp.where(jnp.logical_and(place == 1, which == 15), 0.0, block)
-    at_zero = jnp.where(which == 0, corner[None], 0.0)
-    block = jnp.where(place == 0, at_zero, block)
-    lower = lax.broadcasted_iota(jnp.int32, (PAIRS, 8, 128), 1) < 4
+    block = jnp.where(place == 0, jnp.where(which == 0, corner[None], 0.0), block)
     for n, x in enumerate((block * DOWN_INVERSE, product)):
         x = x.reshape(PAIRS, 2, 8, 128)
-        even, odd = x[:, 0], x[:, 1]
-        real = jnp.where(lower, even, jnp.roll(odd, 4, axis=1))
-        imag = jnp.where(lower, jnp.roll(even, 4, axis=1), odd)
+        real, imag = interleave(x[:, 0], x[:, 1])
         for d in range(16):
             out_ref[d, :, 2 * n] = real
             out_ref[d, :, 2 * n + 1] = imag
-    entries = jnp.sum(rows_ref[:, 120:124, :], axis=0)
+    entries = jnp.sum(rows_ref[1:16, 120:124, :], axis=0)
     for i in range(2):
         real, imag = entries[2 * i : 2 * i + 1], entries[2 * i + 1 : 2 * i + 2]
         magnitude = jnp.maximum(real * real + imag * imag, 1.0)
@@ -113,8 +119,9 @@
         copy.start()
     core = lax.axis_index("c")
     turn = core if own else 1 - core
-    shift = jnp.where(turn == 0, 4, 124)
-    keep = ((lax.broadcasted_iota(jnp.int32, (128, 128), 1) & 7) < 4) == (turn == 0)
+    shift = jnp.where(turn == 0, 2, 126)
+    keep = ((lax.broadcasted_iota(jnp.int32, (128, 128), 1) & 3) < 2) == (turn == 0)
+    first = sublanes((8, 8, 128)) < 4
     total = None
     for step in range(PAIRS // DEPTH):
         lefts, rights = [], []
@@ -129,7 +136,15 @@
                     blocks.append(jnp.where(keep, still, moved))
             lefts.append(jnp.concatenate(blocks, axis=0))
         for block in right_ref(step):
-            rights.append(jnp.concatenate([block[:, m].reshape(128, 128) for m in range(4)], axis=1))
+            columns = []
+            for m in range(4):
+                low, high = block[0:8, m], block[8:16, m]
+                tiles = (
+                    jnp.where(first, low, jnp.roll(high, 4, axis=1)),
+                    jnp.where(first, jnp.roll(low, 4, axis=1), high),
+                )
+                columns.append(jnp.concatenate(tiles, axis=0).reshape(128, 128))
+            rights.append(jnp.concatenate(columns, axis=1))
         rh, rl = split(jnp.concatenate(rights, axis=0))
         lh, ll = split(jnp.concatenate(lefts, axis=1))
         term = dot(lh, rh) + (dot(lh, rl) + dot(ll, rh))
@@ -214,30 +229,27 @@
     vmem = pl.BlockSpec(memory_space=pltpu.VMEM)
     rows = lax.all_gather(row_samples, "col", axis=0)
 
-    flipped = jnp.swapaxes(upper_inverse, 1, 2)
-    flipped = lax.all_gather(flipped, "c", axis=1, tiled=True)
-    last = lax.axis_size("col") - 1
-    moved = lax.ppermute(
-        flipped, CHIPS + ("col",), [(0, 1 * (last + 1) + last)]
-    )
+    packed = pl.pallas_call(
+        pack_kernel,
+        in_specs=[vmem],
+        out_specs=vmem,
+        out_shape=jax.ShapeDtypeStruct((16, 8, 128), f32),
+        compiler_params=params(),
+        cost_estimate=cost(2**17, 2**18),
+    )(jnp.swapaxes(upper_inverse, 1, 2))
+    packed = lax.all_to_all(packed.reshape(32, 4, 128), CHIPS + ("c",), 0, 0).reshape(128, 128)
     entries = pl.pallas_call(
         entries_kernel,
         in_specs=[pl.BlockSpec(memory_space=pltpu.SMEM), vmem, vmem],
         out_specs=vmem,
-        out_shape=jax.ShapeDtypeStruct((4, 128), f32),
+        out_shape=jax.ShapeDtypeStruct((8, 128), f32),
         compiler_params=params(),
         cost_estimate=cost(2**17, 2**18),
     )(rank_blocks, pivot_rows, col_samples)
-    packed = pl.pallas_call(
-        pack_kernel,
-        in_specs=[vmem, vmem],
-        out_specs=vmem,
-        out_shape=jax.ShapeDtypeStruct((16, 8, 128), f32),
-        compiler_params=params(),
-        cost_estimate=cost(2**17, 2**18),
-    )(flipped, moved)
-    packed = lax.all_to_all(packed, CHIPS, 0, 0)
-    packed = jnp.concatenate([packed.reshape(128, 128)[8:], entries], axis=0)
+    place, last = lax.axis_index("col"), lax.axis_size("col") - 1
+    entries = entries + lax.ppermute(entries, "col", [(0, last)])
+    ends = jnp.concatenate([packed[0:2], packed[4:8]], axis=0)
+    packed = jnp.concatenate([packed[8:], jnp.where(place == 0, ends, entries[:6])], axis=0)
     packed = lax.all_gather(packed, "col", axis=0)
     right, factor = pl.pallas_call(
         right_kernel,

time: 131 us -> 130 us (level)
  starting transfers between devices: 19.8 us -> 29.6 us
  blocking collectives: 74.6 us -> 68.3 us
  waiting for transfers between devices: 6.83 us -> 1.44 us
    all_gather x1 -> x0, blocking collectives: 8.79 us -> none  [on_device(): flipped = lax.all_gather(flipped, 'c', axis=1, tiled=True)]
    all_to_all x1, starting transfers between devices: 3.5 us -> 10.4 us  [on_device(): lax.all_to_all(packed.reshape(32, 4, 128), CHIPS + ('c',), 0, 0)]
    all_to_all x1, waiting for transfers between devices: 3.61 us -> 0.01 us  [on_device(): lax.all_to_all(packed.reshape(32, 4, 128), CHIPS + ('c',), 0, 0)]
    ppermute x1, starting transfers between devices: 6.67 us -> 9.32 us  [on_device(): entries = entries + lax.ppermute(entries, 'col', [(0, last)])]
    all_to_all x1, blocking collectives: 24.9 us -> 27.2 us  [on_device(): own = lax.all_to_all(right, CHIPS, 0, 0)]
    ppermute x1, waiting for transfers between devices: 2.51 us -> 0.73 us  [on_device(): entries = entries + lax.ppermute(entries, 'col', [(0, last)])]
    unnamed x8 -> x10, local copies, waits for them, and re-layouts: 2.28 us -> 3.12 us
  transfers between devices with their start and end apart: 4 -> 4, of which waited for: 2 -> 1; matrix products, arithmetic and copies ran while one was open for 0% -> 0% of each run, Pallas kernels for 5% -> 5%
where the time goes in v3:
time: 130 us; the launch traced here: 129 us
  blocking collectives  68.3 us (53%)
  starting transfers between devices  29.6 us (23%)
  between operations  14.2 us (11%)
  Pallas kernels  12.8 us (10%)
  local copies, waits for them, and re-layouts  3.12 us (2%)
  waiting for transfers between devices  1.44 us (1%)
    all_gather x1, blocking collectives, on_device(): packed = lax.all_gather(packed, 'col', axis=0)  41.1 us
    all_to_all x1, blocking collectives, on_device(): own = lax.all_to_all(right, CHIPS, 0, 0)  27.2 us
    all_to_all x1, starting transfers between devices, on_device(): lax.all_to_all(packed.reshape(32, 4, 128), CHIPS + ('c',), 0, 0)  10.4 us
    ppermute x1, starting transfers between devices, on_device(): other = lax.ppermute(own, 'c', [(0, 1), (1, 0)])  9.81 us
    ppermute x1, starting transfers between devices, on_device(): entries = entries + lax.ppermute(entries, 'col', [(0, last)])  9.32 us
    pallas_call x1, Pallas kernels, second_call(): pl.pallas_call(second_kernel, in_specs=[vmem, vmem, hbm, hbm], out_specs=...  6.28 us
    pallas_call x1, Pallas kernels, first_call(): pl.pallas_call(first_kernel, in_specs=[pl.BlockSpec(memory_space=pltpu.HB...  3.96 us
    unnamed x10, local copies, waits for them, and re-layouts  3.12 us
  transfers between devices with their start and end apart: 4, of which 1 were waited for; matrix products, arithmetic and copies ran while one was open for 0% of the time, Pallas kernels for 5%

profile of v3, /device:TPU:1, one launch (start us, length us, event | category | flops | bytes accessed | tf_op | source)
XLA Modules:
  0.0 129.5 jit_solution(3140381532981424163)
XLA Ops:
  7.2 0.0 copy-start
  7.2 0.0 all-gather.5.cloned.1.call-start
  7.2 0.7 all-gather.5.cloned.1.call-update
  7.9 0.0 copy-start.2
  7.9 0.8 copy-done.2
  8.7 0.8 shard_map.77
  9.5 10.4 %all-to-all-start = ((f32[32,4,128]{2,1,0:T(4,128)}), f32[32,4,128]{2,1,0:T(4,128)S(1)}, u32[]{:S(2)}, u32[]{:S(2)}) async-start(f32[32,4,128]{2,1,0:T(4,128)} %bitcast.1), calls=%async_computation | async-start | bytes 131072 | tf_op jit(solution)/shard_map/all_to_all | solution.py:240
  19.9 0.0 copy-start.1
  20.0 0.9 copy-done.1
  20.9 0.0 copy-start.3
  20.9 0.7 copy-done.3
  21.6 0.0 copy-start.4
  21.6 0.7 copy-done.4
  22.2 0.6 shard_map.78
  22.8 9.3 %collective-permute-start = (f32[8,128]{1,0:T(8,128)S(1)}, f32[8,128]{1,0:T(8,128)S(1)}, u32[]{:S(2)}, u32[]{:S(2)}) collective-permute-start(f32[8,128]{1,0:T(8,128)S(1)} %shard_map.78), channel_id=1, source_target_pairs={{0,15},{16,31},{32,47},{48,63},{64,79},{80,95},{96,111},{112,127},... | collective-permute-start | bytes 12296 | tf_op jit(solution)/shard_map/ppermute | solution.py:250
  32.2 0.7 collective-permute-done
  32.9 0.0 all-to-all-done
  32.9 41.1 %all-gather.2.rows_ref = f32[16,126,128]{2,1,0:T(8,128)S(1)} all-gather(f32[1,126,128]{2,1,0:T(8,128)S(1)} %maximum_bitcast_fusion), channel_id=2, replica_groups=mesh['y'=4,'x'=4,'c'=2,'col'=16] {'col'}, dimensions={0}, use_global_device_ids=true | all-gather | bytes 1096704 | tf_op jit(solution)/shard_map/all_gather | solution.py:253
  74.1 0.0 copy-done
  74.1 1.2 shard_map.79
  75.3 27.2 %all_to_all.10.right_ref = f32[16,8,4,8,128]{4,3,2,1,0:T(8,128)S(1)} all-to-all(f32[16,8,4,8,128]{4,3,2,1,0:T(8,128)S(1)} %get-tuple-element.5), channel_id=1, replica_groups=mesh['y'=4,'x'=4,'c'=2,'col'=16] {'y','x'}, dimensions={0} | all-to-all | bytes 4194304 | tf_op jit(solution)/shard_map/all_to_all | solution.py:262
  102.5 9.8 %collective-permute-start.1 = (f32[16,8,4,8,128]{4,3,2,1,0:T(8,128)S(1)}, f32[16,8,4,8,128]{4,3,2,1,0:T(8,128)}, u32[]{:S(2)}, u32[]{:S(2)}) collective-permute-start(f32[16,8,4,8,128]{4,3,2,1,0:T(8,128)S(1)} %all_to_all.10.right_ref), channel_id=1, source_target_pairs={{0,16},{16,0},{1,17},{17,1},{2,18},{18,2},{3,19},{19,3},{4,20},{20... | collective-permute-start | bytes 6291464 | tf_op jit(solution)/shard_map/ppermute | solution.py:263
  112.3 0.0 all-gather.5.cloned.1.call-done
  112.3 4.0 %shard_map.80.start_ref = f32[512,512]{1,0:T(8,128)S(1)} custom-call(f32[16,2,2,128,128]{4,3,2,1,0:T(8,128)} %bitcast.12, f32[16,8,4,8,128]{4,3,2,1,0:T(8,128)S(1)} %all_to_all.10.right_ref), custom_call_target="tpu_custom_call" | custom-call | flops 1610612736 | bytes 7340032 | tf_op jit(solution)/shard_map/pallas_call | solution.py:194
  116.3 0.0 collective-permute-done.1.right_ref
  116.3 6.3 %shard_map.81 = (f32[2,2,128,128]{3,2,1,0:T(8,128)}, f32[2,1,2,128,128]{4,3,2,1,0:T(8,128)}) custom-call(f32[8,128]{1,0:T(8,128)S(1)} %get-tuple-element.4.factor_ref, f32[512,512]{1,0:T(8,128)S(1)} %shard_map.80.start_ref, f32[16,2,2,128,128]{4,3,2,1,0:T(8,128)} %bitcast.13, f32[16,8,4,8,128]{4,3,2,1,0:T(8,128)} %collective-permute-done.1.right_ref), custom_call_target="tpu_custom_call" | custom-call | flops 1610612736 | bytes 8388608 | tf_op jit(solution)/shard_map/pallas_call | solution.py:208
  (6 shorter events, 0.0 us)
Async XLA Ops:
  7.2 66.9 %copy-start = (f32[1,2,2048,128]{3,2,1,0:T(8,128)S(1)}, f32[1,2,2048,128]{3,2,1,0:T(8,128)}, u32[]{:S(2)}) copy-start(f32[1,2,2048,128]{3,2,1,0:T(8,128)} %param.11) | copy-start | bytes 6291460
  7.2 105.2 %all-gather.5.cloned.1.call-start = ((), (), s32[]{:S(2)}) async-start(), calls=%async_computation.2 | async-start | bytes 4456448 | tf_op jit(solution)/shard_map/all_gather | solution.py:230
  7.9 0.8 copy-start.2
  9.5 23.3 %all-to-all-start = ((f32[32,4,128]{2,1,0:T(4,128)}), f32[32,4,128]{2,1,0:T(4,128)S(1)}, u32[]{:S(2)}, u32[]{:S(2)}) async-start(f32[32,4,128]{2,1,0:T(4,128)} %bitcast.1), calls=%async_computation | async-start | bytes 131072 | tf_op jit(solution)/shard_map/all_to_all | solution.py:240
  19.9 1.0 copy-start.1
  20.9 0.7 copy-start.3
  21.6 0.7 copy-start.4
  22.8 10.1 %collective-permute-start = (f32[8,128]{1,0:T(8,128)S(1)}, f32[8,128]{1,0:T(8,128)S(1)}, u32[]{:S(2)}, u32[]{:S(2)}) collective-permute-start(f32[8,128]{1,0:T(8,128)S(1)} %shard_map.78), channel_id=1, source_target_pairs={{0,15},{16,31},{32,47},{48,63},{64,79},{80,95},{96,111},{112,127},... | collective-permute-start | bytes 12296 | tf_op jit(solution)/shard_map/ppermute | solution.py:250
  102.5 13.8 %collective-permute-start.1 = (f32[16,8,4,8,128]{4,3,2,1,0:T(8,128)S(1)}, f32[16,8,4,8,128]{4,3,2,1,0:T(8,128)}, u32[]{:S(2)}, u32[]{:S(2)}) collective-permute-start(f32[16,8,4,8,128]{4,3,2,1,0:T(8,128)S(1)} %all_to_all.10.right_ref), channel_id=1, source_target_pairs={{0,16},{16,0},{1,17},{17,1},{2,18},{18,2},{3,19},{19,3},{4,20},{20... | collective-permute-start | bytes 6291464 | tf_op jit(solution)/shard_map/ppermute | solution.py:263
Sparse Core Ops, SparseCore 0:
  10.1 84.4 all-gather.4

commit v4 on v3

v4 whole, which is shorter than its diff:
```python
import jax
import jax.numpy as jnp
from jax import lax
from jax.experimental import pallas as pl
from jax.experimental.pallas import tpu as pltpu
from jax.sharding import Mesh
from jax.sharding import PartitionSpec as P

RANK_STEP = 16
CHIPS = ("y", "x")
DOWN_INVERSE, UP_INVERSE = 2.0 ** -16, 2.0 ** 16
DOWN_PRODUCT, UP_PRODUCT = 2.0 ** -24, 2.0 ** 24
PAIRS = 8
DEPTH = 2


def params(mebibytes=24):
    return pltpu.CompilerParams(vmem_limit_bytes=mebibytes * 1024 * 1024)


def cost(flops, moved):
    return pl.CostEstimate(flops=flops, bytes_accessed=moved, transcendentals=0)


def split(x):
    high = x.astype(jnp.bfloat16)
    low = (x - high.astype(jnp.float32)).astype(jnp.bfloat16)
    return high, low


def dot(a, b):
    return jnp.dot(a, b, preferred_element_type=jnp.float32)


def sublanes(shape):
    return lax.broadcasted_iota(jnp.int32, shape, len(shape) - 2)


def interleave(even, odd):
    row = sublanes(even.shape)

    def turn(x, n):
        return jnp.roll(x, n, axis=x.ndim - 2)

    even2, odd2, even4, odd4, even6, odd6 = (turn(x, n) for n in (2, 4, 6) for x in (even, odd))
    low = jnp.where(row < 2, even, jnp.where(row < 4, odd2, jnp.where(row < 6, even2, odd4)))
    high = jnp.where(row < 2, even4, jnp.where(row < 4, odd6, jnp.where(row < 6, even6, odd)))
    return low, high


def start_kernel(block_hbm, cols_hbm, pivots_hbm, ranks_hbm, out_ref, entries_ref, block_ref, cols_ref, pivots_ref, ranks_ref, sems):
    pairs = ((block_hbm, block_ref), (cols_hbm, cols_ref), (pivots_hbm, pivots_ref), (ranks_hbm, ranks_ref))
    copies = [pltpu.make_async_copy(a, b, sems.at[n]) for n, (a, b) in enumerate(pairs)]
    for copy in copies:
        copy.start()
    copies[0].wait()
    rows = jnp.concatenate([block_ref[0].T, block_ref[1].T], axis=1).reshape(16, 8, 128)
    low, high = interleave(rows[:8], rows[8:])
    out_ref[0:8] = low
    out_ref[8:16] = high
    for copy in copies[1:]:
        copy.wait()
    width = cols_ref.shape[2]
    levels = lax.broadcasted_iota(jnp.int32, (1, cols_ref.shape[3]), 1)
    rows = lax.broadcasted_iota(jnp.int32, cols_ref.shape[2:], 0) + lax.axis_index("col") * width
    for i in range(2):
        hit = jnp.logical_and(pivots_ref[i : i + 1, :] == rows, levels < RANK_STEP * ranks_ref[i])
        for p in range(2):
            entries_ref[2 * i + p : 2 * i + p + 1, :] = jnp.sum(
                jnp.where(hit, cols_ref[i, p], 0.0), axis=0, keepdims=True
            )
    entries_ref[4:8, :] = jnp.zeros((4, 128), jnp.float32)


def straight(x):
    lane = lax.broadcasted_iota(jnp.int32, x.shape, x.ndim - 1)
    same = (sublanes(x.shape) < 4) == (lane < 64)
    return jnp.where(same, x, jnp.roll(jnp.roll(x, 4, axis=x.ndim - 2), 64, axis=x.ndim - 1))


def right_kernel(rows_ref, left_ref, out_ref, factor_ref):
    place = lax.axis_index("col")
    last = rows_ref[0, 120:126, :]
    corner = straight(jnp.concatenate([last[0:2], jnp.zeros((2, 128), jnp.float32), last[2:6]], axis=0))
    total = None
    for q in range(16):
        if q == 0:
            x = jnp.concatenate([corner, jnp.zeros((120, 128), jnp.float32)], axis=0)
        else:
            x = straight(rows_ref[:, 8 * q - 8 : 8 * q, :]).reshape(128, 128)
        y = jnp.concatenate(
            [left_ref[0, 128 * q : 128 * q + 128, :], left_ref[1, 128 * q : 128 * q + 128, :]], axis=1
        )
        xh, xl = split(x)
        yh, yl = split(y * DOWN_PRODUCT)
        term = dot(xh, yh) + (dot(xh, yl) + dot(xl, yh))
        total = term if total is None else total + term
    by_real = total[:, :128].reshape(16, 8, 128)
    by_imag = jnp.roll(total[:, 128:].reshape(16, 8, 128), 4, axis=1)
    product = by_real + jnp.where(sublanes((16, 8, 128)) < 4, -by_imag, by_imag)
    start = pl.multiple_of(jnp.maximum(place - 1, 0) * 8, 8)
    block = straight(rows_ref[:, pl.ds(start, 8), :])
    which = lax.broadcasted_iota(jnp.int32, (16, 8, 128), 0)
    block = jnp.where(place == 0, jnp.where(which == 0, corner[None], 0.0), block)
    for n, x in enumerate((block * DOWN_INVERSE, product)):
        x = x.reshape(PAIRS, 2, 8, 128)
        real, imag = interleave(x[:, 0], x[:, 1])
        for d in range(16):
            out_ref[d, :, 2 * n] = real
            out_ref[d, :, 2 * n + 1] = imag
    entries = jnp.sum(rows_ref[1:16, 120:124, :], axis=0)
    for i in range(2):
        real, imag = entries[2 * i : 2 * i + 1], entries[2 * i + 1 : 2 * i + 2]
        magnitude = jnp.maximum(real * real + imag * imag, 1.0)
        factor_ref[2 * i : 2 * i + 1, :] = real / magnitude
        factor_ref[2 * i + 1 : 2 * i + 2, :] = -imag / magnitude
    factor_ref[4:8, :] = jnp.zeros((4, 128), jnp.float32)


def tiles(block):
    first = sublanes((8, 8, 128)) < 4
    low, high = block[0:8], block[8:16]
    pair = (jnp.where(first, low, jnp.roll(high, 4, axis=1)), jnp.where(first, jnp.roll(low, 4, axis=1), high))
    return jnp.concatenate(pair, axis=0).reshape(128, 128)


def dot3(left_high, left_low, right):
    high, low = split(right)
    return dot(left_high, high) + (dot(left_high, low) + dot(left_low, high))


def first_kernel(rows_ref, right_ref, out_ref, later_ref, held_ref, sems):
    copies = [pltpu.make_async_copy(rows_ref.at[z], held_ref.at[z], sems.at[z]) for z in range(16)]
    for copy in copies:
        copy.start()
    core = lax.axis_index("c")
    shift = jnp.where(core == 0, 2, 126)
    keep = ((lax.broadcasted_iota(jnp.int32, (128, 128), 1) & 3) < 2) == (core == 0)
    total = None
    for step in range(PAIRS // DEPTH):
        lefts, rights = [], []
        for n in range(step * DEPTH, step * DEPTH + DEPTH):
            copies[2 * n].wait()
            copies[2 * n + 1].wait()
            blocks = []
            for p in range(2):
                for i in range(2):
                    near, far = held_ref[2 * n + core, i, p], held_ref[2 * n + 1 - core, i, p]
                    blocks.append(jnp.where(keep, near, pltpu.roll(far, shift, 1)))
                    high, low = split(jnp.where(keep, pltpu.roll(near, 128 - shift, 1), far))
                    span = slice(256 * p + 128 * i, 256 * p + 128 * i + 128)
                    later_ref[0, span, 128 * n : 128 * n + 128] = high
                    later_ref[1, span, 128 * n : 128 * n + 128] = low
            lefts.append(jnp.concatenate(blocks, axis=0))
            rights.append(jnp.concatenate([tiles(right_ref[:, n, m]) for m in range(4)], axis=1))
        high, low = split(jnp.concatenate(lefts, axis=1))
        term = dot3(high, low, jnp.concatenate(rights, axis=0))
        total = term if total is None else total + term
    out_ref[...] = total


def second_kernel(
    factor_ref, start_ref, left_ref, right_ref, panel_ref, cores_ref, near_ref, panel_vmem, cores_vmem, sems, out_sems
):
    copies = [
        pltpu.make_async_copy(right_ref.at[:, :, 2 * n : 2 * n + 2], near_ref.at[n], sems.at[n]) for n in range(2)
    ]
    for copy in copies:
        copy.start()
    columns = factor_ref[...].T
    results = (
        (pltpu.make_async_copy(panel_vmem, panel_ref, out_sems.at[0]), panel_vmem, UP_INVERSE),
        (pltpu.make_async_copy(cores_vmem, cores_ref, out_sems.at[1]), cores_vmem, UP_PRODUCT),
    )
    for n, (result, out, up) in enumerate(results):
        copies[n].wait()
        right = jnp.concatenate(
            [
                jnp.concatenate([tiles(near_ref[n, :, z, p]) for p in range(2)], axis=1)
                for z in range(PAIRS)
            ],
            axis=0,
        )
        total = start_ref[:, 256 * n : 256 * n + 256] + dot3(left_ref[0], left_ref[1], right)
        for i in range(2):
            fr, fi = columns[:, 2 * i : 2 * i + 1], columns[:, 2 * i + 1 : 2 * i + 2]
            by_real, by_imag = total[128 * i : 128 * i + 128], total[256 + 128 * i : 384 + 128 * i]
            real = by_real[:, :128] - by_imag[:, 128:]
            imag = by_real[:, 128:] + by_imag[:, :128]
            where = (i,) if n == 0 else (i, 0)
            out[where + (0,)] = (fr * real - fi * imag) * up
            out[where + (1,)] = (fr * imag + fi * real) * up
        result.start()
    for result, _, _ in results:
        result.wait()


def first_call(rows, right):
    vmem = pl.BlockSpec(memory_space=pltpu.VMEM)
    return pl.pallas_call(
        first_kernel,
        in_specs=[pl.BlockSpec(memory_space=pltpu.HBM), vmem],
        out_specs=(vmem, vmem),
        out_shape=(
            jax.ShapeDtypeStruct((512, 512), jnp.float32),
            jax.ShapeDtypeStruct((2, 512, 1024), jnp.bfloat16),
        ),
        scratch_shapes=[pltpu.VMEM((16, 2, 2, 128, 128), jnp.float32), pltpu.SemaphoreType.DMA((16,))],
        compiler_params=params(48),
        cost_estimate=cost(2 * 3 * 512 * 1024 * 512, 7 * 2**20),
    )(rows, right)


def second_call(factor, start, left, right):
    vmem = pl.BlockSpec(memory_space=pltpu.VMEM)
    hbm = pl.BlockSpec(memory_space=pltpu.HBM)
    shapes = (2, 2, 128, 128), (2, 1, 2, 128, 128)
    return pl.pallas_call(
        second_kernel,
        in_specs=[vmem, vmem, vmem, hbm],
        out_specs=(hbm, hbm),
        out_shape=tuple(jax.ShapeDtypeStruct(shape, jnp.float32) for shape in shapes),
        scratch_shapes=[
            pltpu.VMEM((2, 16, PAIRS, 2, 8, 128), jnp.float32),
            pltpu.VMEM(shapes[0], jnp.float32),
            pltpu.VMEM(shapes[1], jnp.float32),
            pltpu.SemaphoreType.DMA((2,)),
            pltpu.SemaphoreType.DMA((2,)),
        ],
        compiler_params=params(48),
        cost_estimate=cost(2 * 3 * 512 * 1024 * 512, 8 * 2**20),
    )(factor, start, left, right)


def on_device(col_samples, row_samples, pivot_rows, rank_blocks, upper_inverse, upanel_left):
    f32 = jnp.float32
    vmem = pl.BlockSpec(memory_space=pltpu.VMEM)
    rows = lax.all_gather(row_samples, "col", axis=0)

    hbm = pl.BlockSpec(memory_space=pltpu.HBM)
    packed, entries = pl.pallas_call(
        start_kernel,
        in_specs=[hbm] * 4,
        out_specs=(vmem, vmem),
        out_shape=(jax.ShapeDtypeStruct((16, 8, 128), f32), jax.ShapeDtypeStruct((8, 128), f32)),
        scratch_shapes=[
            pltpu.VMEM((2, 64, 128), f32),
            pltpu.VMEM(col_samples.shape, f32),
            pltpu.VMEM(pivot_rows.shape, jnp.int32),
            pltpu.SMEM(rank_blocks.shape, jnp.int32),
            pltpu.SemaphoreType.DMA((4,)),
        ],
        compiler_params=params(48),
        cost_estimate=cost(2**17, 2**18),
    )(jnp.swapaxes(upper_inverse, 1, 2), col_samples, pivot_rows, rank_blocks)
    packed = lax.all_to_all(packed.reshape(32, 4, 128), CHIPS + ("c",), 0, 0).reshape(128, 128)
    place, last = lax.axis_index("col"), lax.axis_size("col") - 1
    entries = entries + lax.ppermute(entries, "col", [(0, last)])
    ends = jnp.concatenate([packed[0:2], packed[4:8]], axis=0)
    packed = jnp.concatenate([packed[8:], jnp.where(place == 0, ends, entries[:6])], axis=0)
    packed = lax.all_gather(packed, "col", axis=0)
    right, factor = pl.pallas_call(
        right_kernel,
        in_specs=[vmem, vmem],
        out_specs=(vmem, vmem),
        out_shape=(jax.ShapeDtypeStruct((16, PAIRS, 4, 8, 128), f32), jax.ShapeDtypeStruct((8, 128), f32)),
        compiler_params=params(),
        cost_estimate=cost(2 * 3 * 128 * 2048 * 256, 5 * 2**20),
    )(packed, upanel_left[0])
    own = lax.all_to_all(right, CHIPS, 0, 0)
    other = lax.ppermute(own, "c", [(0, 1), (1, 0)])
    start, left = first_call(rows, own)
    return second_call(factor, start, left, other)


def solution(mesh):
    chips = mesh.devices.reshape(4, 4, 2, 16)
    fine = Mesh(chips, ("y", "x", "c", "col"))
    row = ("y", "x", "c")
    in_specs = (
        P(row, None, "col", None),
        P(row, None, None, "col"),
        P(row, None),
        P(row),
        P(None, "col", row),
        P("col", None, None, None),
    )
    out_specs = (P(row, None, None, "col"), P(row, "col", None, None, None))
    return jax.shard_map(
        on_device, mesh=fine, in_specs=in_specs, out_specs=out_specs, check_vma=False
    )
```

time: 130 us -> 130 us (level)
    pallas_call x3 -> x2, Pallas kernels: 7.66 us -> 6.84 us  [the longest x1 5.56 us: second_call(): pl.pallas_call(second_kernel, in_specs=[vmem, vmem, vmem, hbm], out_specs...]
where the time goes in v4:
time: 130 us
  blocking collectives  69.5 us (53%)
  starting transfers between devices  29.3 us (23%)
  between operations  14.2 us (11%)
  Pallas kernels  12.4 us (10%)
  local copies, waits for them, and re-layouts  3.13 us (2%)
  waiting for transfers between devices  1.44 us (1%)
    all_gather x1, blocking collectives, on_device(): packed = lax.all_gather(packed, 'col', axis=0)  42.1 us
    all_to_all x1, blocking collectives, on_device(): own = lax.all_to_all(right, CHIPS, 0, 0)  27.4 us
    all_to_all x1, starting transfers between devices, on_device(): lax.all_to_all(packed.reshape(32, 4, 128), CHIPS + ('c',), 0, 0)  10.4 us
    ppermute x1, starting transfers between devices, on_device(): other = lax.ppermute(own, 'c', [(0, 1), (1, 0)])  9.59 us
    ppermute x1, starting transfers between devices, on_device(): entries = entries + lax.ppermute(entries, 'col', [(0, last)])  9.32 us
    pallas_call x1, Pallas kernels, second_call(): pl.pallas_call(second_kernel, in_specs=[vmem, vmem, vmem, hbm], out_specs...  5.56 us
    pallas_call x1, Pallas kernels, first_call(): pl.pallas_call(first_kernel, in_specs=[pl.BlockSpec(memory_space=pltpu.HB...  4.38 us
    unnamed x10, local copies, waits for them, and re-layouts  3.12 us
  transfers between devices with their start and end apart: 4, of which 1 were waited for; matrix products, arithmetic and copies ran while one was open for 0% of the time, Pallas kernels for 5%

profile of v4, /device:TPU:1, one launch (start us, length us, event | category | flops | bytes accessed | tf_op | source)
XLA Modules:
  0.0 130.0 jit_solution(9814565670600079808)
XLA Ops:
  7.2 0.0 copy-start
  7.2 0.0 all-gather.5.cloned.1.call-start
  7.2 0.7 all-gather.5.cloned.1.call-update
  7.9 0.0 copy-start.1
  7.9 0.9 copy-done.1
  8.9 0.0 copy-start.2
  8.9 0.8 copy-done.2
  9.7 0.0 copy-start.3
  9.7 0.7 copy-done.3
  10.4 0.0 copy-start.4
  10.4 0.7 copy-done.4
  11.0 1.3 shard_map.77
  12.3 10.4 %all-to-all-start = ((f32[32,4,128]{2,1,0:T(4,128)}), f32[32,4,128]{2,1,0:T(4,128)S(1)}, u32[]{:S(2)}, u32[]{:S(2)}) async-start(f32[32,4,128]{2,1,0:T(4,128)} %bitcast.1), calls=%async_computation | async-start | bytes 131072 | tf_op jit(solution)/shard_map/all_to_all | solution.py:256
  22.7 9.3 %collective-permute-start = (f32[8,128]{1,0:T(8,128)S(1)}, f32[8,128]{1,0:T(8,128)S(1)}, u32[]{:S(2)}, u32[]{:S(2)}) collective-permute-start(f32[8,128]{1,0:T(8,128)S(1)} %get-tuple-element.9), channel_id=1, source_target_pairs={{0,15},{16,31},{32,47},{48,63},{64,79},{80,95},{96,111},{112,127},... | collective-permute-start | bytes 12296 | tf_op jit(solution)/shard_map/ppermute | solution.py:258
  32.1 0.7 collective-permute-done
  32.8 0.0 all-to-all-done
  32.9 42.1 %all-gather.2.rows_ref = f32[16,126,128]{2,1,0:T(8,128)S(1)} all-gather(f32[1,126,128]{2,1,0:T(8,128)S(1)} %maximum_bitcast_fusion), channel_id=2, replica_groups=mesh['y'=4,'x'=4,'c'=2,'col'=16] {'col'}, dimensions={0}, use_global_device_ids=true | all-gather | bytes 1096704 | tf_op jit(solution)/shard_map/all_gather | solution.py:261
  75.0 0.0 copy-done
  75.0 1.2 shard_map.78
  76.2 27.4 %all_to_all.10.right_ref = f32[16,8,4,8,128]{4,3,2,1,0:T(8,128)S(1)} all-to-all(f32[16,8,4,8,128]{4,3,2,1,0:T(8,128)S(1)} %get-tuple-element.11), channel_id=1, replica_groups=mesh['y'=4,'x'=4,'c'=2,'col'=16] {'y','x'}, dimensions={0} | all-to-all | bytes 4194304 | tf_op jit(solution)/shard_map/all_to_all | solution.py:270
  103.6 9.6 %collective-permute-start.1 = (f32[16,8,4,8,128]{4,3,2,1,0:T(8,128)S(1)}, f32[16,8,4,8,128]{4,3,2,1,0:T(8,128)}, u32[]{:S(2)}, u32[]{:S(2)}) collective-permute-start(f32[16,8,4,8,128]{4,3,2,1,0:T(8,128)S(1)} %all_to_all.10.right_ref), channel_id=1, source_target_pairs={{0,16},{16,0},{1,17},{17,1},{2,18},{18,2},{3,19},{19,3},{4,20},{20... | collective-permute-start | bytes 6291464 | tf_op jit(solution)/shard_map/ppermute | solution.py:271
  113.2 0.0 all-gather.5.cloned.1.call-done
  113.2 4.4 %shard_map.79 = (f32[512,512]{1,0:T(8,128)S(1)}, bf16[2,512,1024]{2,1,0:T(8,128)(2,1)S(1)}) custom-call(f32[16,2,2,128,128]{4,3,2,1,0:T(8,128)} %bitcast.12, f32[16,8,4,8,128]{4,3,2,1,0:T(8,128)S(1)} %all_to_all.10.right_ref), custom_call_target="tpu_custom_call" | custom-call | flops 1610612736 | bytes 7340032 | tf_op jit(solution)/shard_map/pallas_call | solution.py:200
  117.6 0.0 collective-permute-done.1.right_ref
  117.6 5.6 %shard_map.80 = (f32[2,2,128,128]{3,2,1,0:T(8,128)}, f32[2,1,2,128,128]{4,3,2,1,0:T(8,128)}) custom-call(f32[8,128]{1,0:T(8,128)S(1)} %get-tuple-element.10.factor_ref, f32[512,512]{1,0:T(8,128)S(1)} %get-tuple-element.12.start_ref, bf16[2,512,1024]{2,1,0:T(8,128)(2,1)S(1)} %get-tuple-element.13.left_ref, f32[16,8,4,8,128]{4,3,2,1,0:T(8,128)} %collective-permute-done.1.right_ref), custom_call_target="tpu_custom_call" | custom-call | flops 1610612736 | bytes 8388608 | tf_op jit(solution)/shard_map/pallas_call | solution.py:218
  (6 shorter events, 0.0 us)
Async XLA Ops:
  7.2 67.8 %copy-start = (f32[1,2,2048,128]{3,2,1,0:T(8,128)S(1)}, f32[1,2,2048,128]{3,2,1,0:T(8,128)}, u32[]{:S(2)}) copy-start(f32[1,2,2048,128]{3,2,1,0:T(8,128)} %param.11) | copy-start | bytes 6291460
  7.2 106.0 %all-gather.5.cloned.1.call-start = ((), (), s32[]{:S(2)}) async-start(), calls=%async_computation.2 | async-start | bytes 4456448 | tf_op jit(solution)/shard_map/all_gather | solution.py:238
  7.9 1.0 copy-start.1
  8.9 0.8 copy-start.2
  9.7 0.7 copy-start.3
  10.4 0.7 copy-start.4
  12.3 20.5 %all-to-all-start = ((f32[32,4,128]{2,1,0:T(4,128)}), f32[32,4,128]{2,1,0:T(4,128)S(1)}, u32[]{:S(2)}, u32[]{:S(2)}) async-start(f32[32,4,128]{2,1,0:T(4,128)} %bitcast.1), calls=%async_computation | async-start | bytes 131072 | tf_op jit(solution)/shard_map/all_to_all | solution.py:256
  22.7 10.1 %collective-permute-start = (f32[8,128]{1,0:T(8,128)S(1)}, f32[8,128]{1,0:T(8,128)S(1)}, u32[]{:S(2)}, u32[]{:S(2)}) collective-permute-start(f32[8,128]{1,0:T(8,128)S(1)} %get-tuple-element.9), channel_id=1, source_target_pairs={{0,15},{16,31},{32,47},{48,63},{64,79},{80,95},{96,111},{112,127},... | collective-permute-start | bytes 12296 | tf_op jit(solution)/shard_map/ppermute | solution.py:258
  103.6 14.0 %collective-permute-start.1 = (f32[16,8,4,8,128]{4,3,2,1,0:T(8,128)S(1)}, f32[16,8,4,8,128]{4,3,2,1,0:T(8,128)}, u32[]{:S(2)}, u32[]{:S(2)}) collective-permute-start(f32[16,8,4,8,128]{4,3,2,1,0:T(8,128)S(1)} %all_to_all.10.right_ref), channel_id=1, source_target_pairs={{0,16},{16,0},{1,17},{17,1},{2,18},{18,2},{3,19},{19,3},{4,20},{20... | collective-permute-start | bytes 6291464 | tf_op jit(solution)/shard_map/ppermute | solution.py:271
Sparse Core Ops, SparseCore 0:
  10.1 84.3 all-gather.4

commit v5 on v4

--- a/solution.py
+++ b/solution.py
@@ -11,11 +11,12 @@
 DOWN_INVERSE, UP_INVERSE = 2.0 ** -16, 2.0 ** 16
 DOWN_PRODUCT, UP_PRODUCT = 2.0 ** -24, 2.0 ** 24
 PAIRS = 8
-DEPTH = 2
+DEPTH = 4
+ROWS = 512
 
 
 def params(mebibytes=24):
-    return pltpu.CompilerParams(vmem_limit_bytes=mebibytes * 1024 * 1024)
+    return pltpu.CompilerParams(vmem_limit_bytes=int(mebibytes * 2**20))
 
 
 def cost(flops, moved):
@@ -48,8 +49,17 @@
     return low, high
 
 
-def start_kernel(block_hbm, cols_hbm, pivots_hbm, ranks_hbm, out_ref, entries_ref, block_ref, cols_ref, pivots_ref, ranks_ref, sems):
-    pairs = ((block_hbm, block_ref), (cols_hbm, cols_ref), (pivots_hbm, pivots_ref), (ranks_hbm, ranks_ref))
+def start_kernel(
+    block_hbm, rows_hbm, cols_hbm, pivots_hbm, ranks_hbm, out_ref, sent_ref, block_ref, cols_ref, pivots_ref, ranks_ref, entries_ref, sems
+):
+    entries_to = sent_ref.at[ROWS : ROWS + 8]
+    pairs = (
+        (block_hbm, block_ref),
+        (cols_hbm, cols_ref),
+        (pivots_hbm, pivots_ref),
+        (ranks_hbm, ranks_ref),
+        (rows_hbm, sent_ref.at[0:ROWS]),
+    )
     copies = [pltpu.make_async_copy(a, b, sems.at[n]) for n, (a, b) in enumerate(pairs)]
     for copy in copies:
         copy.start()
@@ -58,7 +68,7 @@
     low, high = interleave(rows[:8], rows[8:])
     out_ref[0:8] = low
     out_ref[8:16] = high
-    for copy in copies[1:]:
+    for copy in copies[1:4]:
         copy.wait()
     width = cols_ref.shape[2]
     levels = lax.broadcasted_iota(jnp.int32, (1, cols_ref.shape[3]), 1)
@@ -70,6 +80,10 @@
                 jnp.where(hit, cols_ref[i, p], 0.0), axis=0, keepdims=True
             )
     entries_ref[4:8, :] = jnp.zeros((4, 128), jnp.float32)
+    last = pltpu.make_async_copy(entries_ref, entries_to, sems.at[5])
+    last.start()
+    copies[4].wait()
+    last.wait()
 
 
 def straight(x):
@@ -78,7 +92,7 @@
     return jnp.where(same, x, jnp.roll(jnp.roll(x, 4, axis=x.ndim - 2), 64, axis=x.ndim - 1))
 
 
-def right_kernel(rows_ref, left_ref, out_ref, factor_ref):
+def right_kernel(rows_ref, left_ref, out_ref):
     place = lax.axis_index("col")
     last = rows_ref[0, 120:126, :]
     corner = straight(jnp.concatenate([last[0:2], jnp.zeros((2, 128), jnp.float32), last[2:6]], axis=0))
@@ -108,13 +122,6 @@
         for d in range(16):
             out_ref[d, :, 2 * n] = real
             out_ref[d, :, 2 * n + 1] = imag
-    entries = jnp.sum(rows_ref[1:16, 120:124, :], axis=0)
-    for i in range(2):
-        real, imag = entries[2 * i : 2 * i + 1], entries[2 * i + 1 : 2 * i + 2]
-        magnitude = jnp.maximum(real * real + imag * imag, 1.0)
-        factor_ref[2 * i : 2 * i + 1, :] = real / magnitude
-        factor_ref[2 * i + 1 : 2 * i + 2, :] = -imag / magnitude
-    factor_ref[4:8, :] = jnp.zeros((4, 128), jnp.float32)
 
 
 def tiles(block):
@@ -129,7 +136,7 @@
     return dot(left_high, high) + (dot(left_high, low) + dot(left_low, high))
 
 
-def first_kernel(rows_ref, right_ref, out_ref, later_ref, held_ref, sems):
+def first_kernel(rows_ref, right_ref, out_ref, later_ref, factor_ref, held_ref, sems):
     copies = [pltpu.make_async_copy(rows_ref.at[z], held_ref.at[z], sems.at[z]) for z in range(16)]
     for copy in copies:
         copy.start()
@@ -145,7 +152,8 @@
             blocks = []
             for p in range(2):
                 for i in range(2):
-                    near, far = held_ref[2 * n + core, i, p], held_ref[2 * n + 1 - core, i, p]
+                    at = slice(256 * i + 128 * p, 256 * i + 128 * p + 128)
+                    near, far = held_ref[2 * n + core, at], held_ref[2 * n + 1 - core, at]
                     blocks.append(jnp.where(keep, near, pltpu.roll(far, shift, 1)))
                     high, low = split(jnp.where(keep, pltpu.roll(near, 128 - shift, 1), far))
                     span = slice(256 * p + 128 * i, 256 * p + 128 * i + 128)
@@ -157,15 +165,26 @@
         term = dot3(high, low, jnp.concatenate(rights, axis=0))
         total = term if total is None else total + term
     out_ref[...] = total
+    entries = jnp.sum(held_ref[:, ROWS : ROWS + 8], axis=0)
+    for i in range(2):
+        real, imag = entries[2 * i : 2 * i + 1], entries[2 * i + 1 : 2 * i + 2]
+        magnitude = jnp.maximum(real * real + imag * imag, 1.0)
+        factor_ref[2 * i : 2 * i + 1, :] = real / magnitude
+        factor_ref[2 * i + 1 : 2 * i + 2, :] = -imag / magnitude
+    factor_ref[4:8, :] = jnp.zeros((4, 128), jnp.float32)
 
 
 def second_kernel(
     factor_ref, start_ref, left_ref, right_ref, panel_ref, cores_ref, near_ref, panel_vmem, cores_vmem, sems, out_sems
 ):
     copies = [
-        pltpu.make_async_copy(right_ref.at[:, :, 2 * n : 2 * n + 2], near_ref.at[n], sems.at[n]) for n in range(2)
+        [
+            pltpu.make_async_copy(right_ref.at[:, z, 2 * n : 2 * n + 2], near_ref.at[n, z], sems.at[n, z])
+            for z in range(PAIRS)
+        ]
+        for n in range(2)
     ]
-    for copy in copies:
+    for copy in copies[0] + copies[1]:
         copy.start()
     columns = factor_ref[...].T
     results = (
@@ -173,10 +192,11 @@
         (pltpu.make_async_copy(cores_vmem, cores_ref, out_sems.at[1]), cores_vmem, UP_PRODUCT),
     )
     for n, (result, out, up) in enumerate(results):
-        copies[n].wait()
+        for copy in copies[n]:
+            copy.wait()
         right = jnp.concatenate(
             [
-                jnp.concatenate([tiles(near_ref[n, :, z, p]) for p in range(2)], axis=1)
+                jnp.concatenate([tiles(near_ref[n, z, :, p]) for p in range(2)], axis=1)
                 for z in range(PAIRS)
             ],
             axis=0,
@@ -200,12 +220,13 @@
     return pl.pallas_call(
         first_kernel,
         in_specs=[pl.BlockSpec(memory_space=pltpu.HBM), vmem],
-        out_specs=(vmem, vmem),
+        out_specs=(vmem, vmem, vmem),
         out_shape=(
             jax.ShapeDtypeStruct((512, 512), jnp.float32),
             jax.ShapeDtypeStruct((2, 512, 1024), jnp.bfloat16),
+            jax.ShapeDtypeStruct((8, 128), jnp.float32),
         ),
-        scratch_shapes=[pltpu.VMEM((16, 2, 2, 128, 128), jnp.float32), pltpu.SemaphoreType.DMA((16,))],
+        scratch_shapes=[pltpu.VMEM((16, ROWS + 8, 128), jnp.float32), pltpu.SemaphoreType.DMA((16,))],
         compiler_params=params(48),
         cost_estimate=cost(2 * 3 * 512 * 1024 * 512, 7 * 2**20),
     )(rows, right)
@@ -221,10 +242,10 @@
         out_specs=(hbm, hbm),
         out_shape=tuple(jax.ShapeDtypeStruct(shape, jnp.float32) for shape in shapes),
         scratch_shapes=[
-            pltpu.VMEM((2, 16, PAIRS, 2, 8, 128), jnp.float32),
+            pltpu.VMEM((2, PAIRS, 16, 2, 8, 128), jnp.float32),
             pltpu.VMEM(shapes[0], jnp.float32),
             pltpu.VMEM(shapes[1], jnp.float32),
-            pltpu.SemaphoreType.DMA((2,)),
+            pltpu.SemaphoreType.DMA((2, PAIRS)),
             pltpu.SemaphoreType.DMA((2,)),
         ],
         compiler_params=params(48),
@@ -235,41 +256,38 @@
 def on_device(col_samples, row_samples, pivot_rows, rank_blocks, upper_inverse, upanel_left):
     f32 = jnp.float32
     vmem = pl.BlockSpec(memory_space=pltpu.VMEM)
-    rows = lax.all_gather(row_samples, "col", axis=0)
-
     hbm = pl.BlockSpec(memory_space=pltpu.HBM)
-    packed, entries = pl.pallas_call(
+    packed, sent = pl.pallas_call(
         start_kernel,
-        in_specs=[hbm] * 4,
-        out_specs=(vmem, vmem),
-        out_shape=(jax.ShapeDtypeStruct((16, 8, 128), f32), jax.ShapeDtypeStruct((8, 128), f32)),
+        in_specs=[hbm] * 5,
+        out_specs=(vmem, hbm),
+        out_shape=(jax.ShapeDtypeStruct((16, 8, 128), f32), jax.ShapeDtypeStruct((ROWS + 8, 128), f32)),
         scratch_shapes=[
             pltpu.VMEM((2, 64, 128), f32),
             pltpu.VMEM(col_samples.shape, f32),
             pltpu.VMEM(pivot_rows.shape, jnp.int32),
             pltpu.SMEM(rank_blocks.shape, jnp.int32),
-            pltpu.SemaphoreType.DMA((4,)),
+            pltpu.VMEM((8, 128), f32),
+            pltpu.SemaphoreType.DMA((6,)),
         ],
-        compiler_params=params(48),
+        compiler_params=params(61.75),
         cost_estimate=cost(2**17, 2**18),
-    )(jnp.swapaxes(upper_inverse, 1, 2), col_samples, pivot_rows, rank_blocks)
+    )(jnp.swapaxes(upper_inverse, 1, 2), row_samples.reshape(ROWS, 128), col_samples, pivot_rows, rank_blocks)
+    rows = lax.all_gather(sent, "col", axis=0)
     packed = lax.all_to_all(packed.reshape(32, 4, 128), CHIPS + ("c",), 0, 0).reshape(128, 128)
-    place, last = lax.axis_index("col"), lax.axis_size("col") - 1
-    entries = entries + lax.ppermute(entries, "col", [(0, last)])
-    ends = jnp.concatenate([packed[0:2], packed[4:8]], axis=0)
-    packed = jnp.concatenate([packed[8:], jnp.where(place == 0, ends, entries[:6])], axis=0)
+    packed = jnp.concatenate([packed[8:], packed[0:2], packed[4:8]], axis=0)
     packed = lax.all_gather(packed, "col", axis=0)
-    right, factor = pl.pallas_call(
+    right = pl.pallas_call(
         right_kernel,
         in_specs=[vmem, vmem],
-        out_specs=(vmem, vmem),
-        out_shape=(jax.ShapeDtypeStruct((16, PAIRS, 4, 8, 128), f32), jax.ShapeDtypeStruct((8, 128), f32)),
+        out_specs=vmem,
+        out_shape=jax.ShapeDtypeStruct((16, PAIRS, 4, 8, 128), f32),
         compiler_params=params(),
         cost_estimate=cost(2 * 3 * 128 * 2048 * 256, 5 * 2**20),
     )(packed, upanel_left[0])
     own = lax.all_to_all(right, CHIPS, 0, 0)
     other = lax.ppermute(own, "c", [(0, 1), (1, 0)])
-    start, left = first_call(rows, own)
+    start, left, factor = first_call(rows, own)
     return second_call(factor, start, left, other)
 
 

time: 130 us -> 132 us (1.015)
  starting transfers between devices: 29.3 us -> 9.51 us
  blocking collectives: 69.5 us -> 87.2 us
  Pallas kernels: 12.4 us -> 21.1 us
  local copies, waits for them, and re-layouts: 3.13 us -> 0.01 us
  waiting for transfers between devices: 1.44 us -> 0.04 us
    all_to_all x0 -> x1, blocking collectives: none -> 17.8 us  [on_device(): lax.all_to_all(packed.reshape(32, 4, 128), CHIPS + ('c',), 0, 0)]
    all_to_all x1 -> x0, starting transfers between devices: 10.4 us -> none  [on_device(): lax.all_to_all(packed.reshape(32, 4, 128), CHIPS + ('c',), 0, 0)]
    ppermute x1 -> x0, starting transfers between devices: 9.32 us -> none  [on_device(): entries = entries + lax.ppermute(entries, 'col', [(0, last)])]
    pallas_call x2, Pallas kernels: 2.47 us -> 10.9 us  [the longest x1 9.73 us: on_device(): pl.pallas_call(start_kernel, in_specs=[hbm] * 5, out_specs=(vmem, hbm), o...]
    unnamed x10 -> x2, local copies, waits for them, and re-layouts: 3.12 us -> 0.01 us
    all_to_all x1, blocking collectives: 27.4 us -> 24.6 us  [on_device(): own = lax.all_to_all(right, CHIPS, 0, 0)]
    all_gather x1, blocking collectives: 42.1 us -> 44.8 us  [on_device(): packed = lax.all_gather(packed, 'col', axis=0)]
  transfers between devices with their start and end apart: 4 -> 2, of which waited for: 1 -> 0; matrix products, arithmetic and copies ran while one was open for 0% -> 0% of each run, Pallas kernels for 5% -> 4%
where the time goes in v5:
time: 132 us
  blocking collectives  87.2 us (66%)
  Pallas kernels  21.1 us (16%)
  between operations  14.1 us (11%)
  starting transfers between devices  9.51 us (7%)
    all_gather x1, blocking collectives, on_device(): packed = lax.all_gather(packed, 'col', axis=0)  44.8 us
    all_to_all x1, blocking collectives, on_device(): own = lax.all_to_all(right, CHIPS, 0, 0)  24.6 us
    all_to_all x1, blocking collectives, on_device(): lax.all_to_all(packed.reshape(32, 4, 128), CHIPS + ('c',), 0, 0)  17.8 us
    pallas_call x1, Pallas kernels, on_device(): pl.pallas_call(start_kernel, in_specs=[hbm] * 5, out_specs=(vmem, hbm), o...  9.73 us
    ppermute x1, starting transfers between devices, on_device(): other = lax.ppermute(own, 'c', [(0, 1), (1, 0)])  9.47 us
    pallas_call x1, Pallas kernels, second_call(): pl.pallas_call(second_kernel, in_specs=[vmem, vmem, vmem, hbm], out_specs...  5.75 us
    pallas_call x1, Pallas kernels, first_call(): pl.pallas_call(first_kernel, in_specs=[pl.BlockSpec(memory_space=pltpu.HB...  4.46 us
  transfers between devices with their start and end apart: 2, of which 0 were waited for; matrix products, arithmetic and copies ran while one was open for 0% of the time, Pallas kernels for 4%

profile of v5, /device:TPU:1, one launch (start us, length us, event | category | flops | bytes accessed | tf_op | source)
XLA Modules:
  0.0 132.0 jit_solution(9661282414195108647)
XLA Ops:
  7.2 0.0 copy-start
  7.2 0.0 all-gather.5.cloned.1.call-start
  7.2 9.7 %shard_map.77 = (f32[16,8,128]{2,1,0:T(8,128)}, f32[520,128]{1,0:T(8,128)}) custom-call(f32[2,64,128]{2,1,0:T(8,128)} %bitcast.17, f32[512,128]{1,0:T(8,128)} %bitcast.13, f32[2,2,128,128]{3,2,1,0:T(8,128)} %cols_hbm.1, s32[2,128]{1,0:T(2,128)} %pivots_hbm.1, s32[2]{0:T(128)} %ranks_hbm.1), custom_call_target="tpu_custom_call" | custom-call | flops 131072 | bytes 262144 | tf_op jit(solution)/shard_map/pallas_call | solution.py:260
  17.0 0.0 all-gather.5.cloned.1.call-update
  17.0 17.8 %all_to_all.10 = f32[32,4,128]{2,1,0:T(4,128)S(1)} all-to-all(f32[32,4,128]{2,1,0:T(4,128)} %bitcast.16), channel_id=1, replica_groups=mesh['y'=4,'x'=4,'c'=2,'col'=16] {'y','x','c'}, dimensions={0} | all-to-all | bytes 131072 | tf_op jit(solution)/shard_map/all_to_all | solution.py:277
  34.8 44.8 %all-gather.2.rows_ref = f32[16,126,128]{2,1,0:T(8,128)S(1)} all-gather(f32[1,126,128]{2,1,0:T(8,128)S(1)} %maximum_bitcast_fusion), channel_id=3, replica_groups=mesh['y'=4,'x'=4,'c'=2,'col'=16] {'col'}, dimensions={0}, use_global_device_ids=true | all-gather | bytes 1096704 | tf_op jit(solution)/shard_map/all_gather | solution.py:279
  79.6 0.0 copy-done
  79.6 1.2 shard_map.78
  80.8 24.6 %all_to_all.11.right_ref = f32[16,8,4,8,128]{4,3,2,1,0:T(8,128)S(1)} all-to-all(f32[16,8,4,8,128]{4,3,2,1,0:T(8,128)S(1)} %shard_map.78), channel_id=1, replica_groups=mesh['y'=4,'x'=4,'c'=2,'col'=16] {'y','x'}, dimensions={0} | all-to-all | bytes 4194304 | tf_op jit(solution)/shard_map/all_to_all | solution.py:288
  105.4 9.5 %collective-permute-start = (f32[16,8,4,8,128]{4,3,2,1,0:T(8,128)S(1)}, f32[16,8,4,8,128]{4,3,2,1,0:T(8,128)}, u32[]{:S(2)}, u32[]{:S(2)}) collective-permute-start(f32[16,8,4,8,128]{4,3,2,1,0:T(8,128)S(1)} %all_to_all.11.right_ref), channel_id=1, source_target_pairs={{0,16},{16,0},{1,17},{17,1},{2,18},{18,2},{3,19},{19,3},{4,20},{20... | collective-permute-start | bytes 6291464 | tf_op jit(solution)/shard_map/ppermute | solution.py:289
  114.9 0.0 all-gather.5.cloned.1.call-done
  114.9 4.5 %shard_map.79 = (f32[512,512]{1,0:T(8,128)S(1)}, bf16[2,512,1024]{2,1,0:T(8,128)(2,1)S(1)}, f32[8,128]{1,0:T(8,128)S(1)}) custom-call(f32[16,520,128]{2,1,0:T(8,128)} %bitcast.12, f32[16,8,4,8,128]{4,3,2,1,0:T(8,128)S(1)} %all_to_all.11.right_ref), custom_call_target="tpu_custom_call" | custom-call | flops 1610612736 | bytes 7340032 | tf_op jit(solution)/shard_map/pallas_call | solution.py:220
  119.4 0.0 collective-permute-done.right_ref
  119.4 5.7 %shard_map.80 = (f32[2,2,128,128]{3,2,1,0:T(8,128)}, f32[2,1,2,128,128]{4,3,2,1,0:T(8,128)}) custom-call(f32[8,128]{1,0:T(8,128)S(1)} %get-tuple-element.9.factor_ref, f32[512,512]{1,0:T(8,128)S(1)} %get-tuple-element.10.start_ref, bf16[2,512,1024]{2,1,0:T(8,128)(2,1)S(1)} %get-tuple-element.11.left_ref, f32[16,8,4,8,128]{4,3,2,1,0:T(8,128)} %collective-permute-done.right_ref), custom_call_target="tpu_custom_call" | custom-call | flops 1610612736 | bytes 8388608 | tf_op jit(solution)/shard_map/pallas_call | solution.py:239
  (4 shorter events, 0.0 us)
Async XLA Ops:
  7.2 72.4 %copy-start = (f32[1,2,2048,128]{3,2,1,0:T(8,128)S(1)}, f32[1,2,2048,128]{3,2,1,0:T(8,128)}, u32[]{:S(2)}) copy-start(f32[1,2,2048,128]{3,2,1,0:T(8,128)} %param.11) | copy-start | bytes 6291460
  7.2 107.7 %all-gather.5.cloned.1.call-start = ((), (), s32[]{:S(2)}) async-start(), calls=%async_computation.2 | async-start | bytes 4526080 | tf_op jit(solution)/shard_map/all_gather | solution.py:276
  105.4 14.0 %collective-permute-start = (f32[16,8,4,8,128]{4,3,2,1,0:T(8,128)S(1)}, f32[16,8,4,8,128]{4,3,2,1,0:T(8,128)}, u32[]{:S(2)}, u32[]{:S(2)}) collective-permute-start(f32[16,8,4,8,128]{4,3,2,1,0:T(8,128)S(1)} %all_to_all.11.right_ref), channel_id=1, source_target_pairs={{0,16},{16,0},{1,17},{17,1},{2,18},{18,2},{3,19},{19,3},{4,20},{20... | collective-permute-start | bytes 6291464 | tf_op jit(solution)/shard_map/ppermute | solution.py:289
Sparse Core Ops, SparseCore 0:
  17.1 84.4 all-gather.4

commit v6 on v5

--- a/solution.py
+++ b/solution.py
@@ -50,9 +50,8 @@
 
 
 def start_kernel(
-    block_hbm, rows_hbm, cols_hbm, pivots_hbm, ranks_hbm, out_ref, sent_ref, block_ref, cols_ref, pivots_ref, ranks_ref, entries_ref, sems
+    block_hbm, rows_hbm, cols_hbm, pivots_hbm, ranks_hbm, out_ref, sent_ref, block_ref, cols_ref, pivots_ref, ranks_ref, sems
 ):
-    entries_to = sent_ref.at[ROWS : ROWS + 8]
     pairs = (
         (block_hbm, block_ref),
         (cols_hbm, cols_ref),
@@ -76,14 +75,10 @@
     for i in range(2):
         hit = jnp.logical_and(pivots_ref[i : i + 1, :] == rows, levels < RANK_STEP * ranks_ref[i])
         for p in range(2):
-            entries_ref[2 * i + p : 2 * i + p + 1, :] = jnp.sum(
-                jnp.where(hit, cols_ref[i, p], 0.0), axis=0, keepdims=True
-            )
-    entries_ref[4:8, :] = jnp.zeros((4, 128), jnp.float32)
-    last = pltpu.make_async_copy(entries_ref, entries_to, sems.at[5])
-    last.start()
+            at = ROWS + 2 * i + p
+            sent_ref[at : at + 1, :] = jnp.sum(jnp.where(hit, cols_ref[i, p], 0.0), axis=0, keepdims=True)
+    sent_ref[ROWS + 4 : ROWS + 8, :] = jnp.zeros((4, 128), jnp.float32)
     copies[4].wait()
-    last.wait()
 
 
 def straight(x):
@@ -260,15 +255,14 @@
     packed, sent = pl.pallas_call(
         start_kernel,
         in_specs=[hbm] * 5,
-        out_specs=(vmem, hbm),
+        out_specs=(vmem, vmem),
         out_shape=(jax.ShapeDtypeStruct((16, 8, 128), f32), jax.ShapeDtypeStruct((ROWS + 8, 128), f32)),
         scratch_shapes=[
             pltpu.VMEM((2, 64, 128), f32),
             pltpu.VMEM(col_samples.shape, f32),
             pltpu.VMEM(pivot_rows.shape, jnp.int32),
             pltpu.SMEM(rank_blocks.shape, jnp.int32),
-            pltpu.VMEM((8, 128), f32),
-            pltpu.SemaphoreType.DMA((6,)),
+            pltpu.SemaphoreType.DMA((5,)),
         ],
         compiler_params=params(61.75),
         cost_estimate=cost(2**17, 2**18),

time: 132 us -> 126 us (0.955)
  Pallas kernels: 21.1 us -> 13.4 us
  blocking collectives: 87.2 us -> 90.3 us
  starting transfers between devices: 9.51 us -> 7.94 us
    pallas_call x1, Pallas kernels: 9.73 us -> 1.99 us  [on_device(): pl.pallas_call(start_kernel, in_specs=[hbm] * 5, out_specs=(vmem, vmem),...]
    all_to_all x1, blocking collectives: 24.6 us -> 26.9 us  [on_device(): own = lax.all_to_all(right, CHIPS, 0, 0)]
    ppermute x1, starting transfers between devices: 9.47 us -> 7.9 us  [on_device(): other = lax.ppermute(own, 'c', [(0, 1), (1, 0)])]
where the time goes in v6:
time: 126 us
  blocking collectives  90.3 us (72%)
  between operations  14.1 us (11%)
  Pallas kernels  13.4 us (11%)
  starting transfers between devices  7.94 us (6%)
    all_gather x1, blocking collectives, on_device(): packed = lax.all_gather(packed, 'col', axis=0)  45.6 us
    all_to_all x1, blocking collectives, on_device(): own = lax.all_to_all(right, CHIPS, 0, 0)  26.9 us
    all_to_all x1, blocking collectives, on_device(): lax.all_to_all(packed.reshape(32, 4, 128), CHIPS + ('c',), 0, 0)  17.8 us
    ppermute x1, starting transfers between devices, on_device(): other = lax.ppermute(own, 'c', [(0, 1), (1, 0)])  7.9 us
    pallas_call x1, Pallas kernels, second_call(): pl.pallas_call(second_kernel, in_specs=[vmem, vmem, vmem, hbm], out_specs...  5.75 us
    pallas_call x1, Pallas kernels, first_call(): pl.pallas_call(first_kernel, in_specs=[pl.BlockSpec(memory_space=pltpu.HB...  4.46 us
  transfers between devices with their start and end apart: 2, of which 0 were waited for; matrix products, arithmetic and copies ran while one was open for 0% of the time, Pallas kernels for 4%

profile of v6, /device:TPU:1, one launch (start us, length us, event | category | flops | bytes accessed | tf_op | source)
XLA Modules:
  0.0 125.8 jit_solution(17318921654825525648)
XLA Ops:
  7.2 0.0 copy-start
  7.2 0.0 all-gather.5.cloned.1.call-start
  7.2 2.0 %shard_map.77 = (f32[16,8,128]{2,1,0:T(8,128)}, f32[520,128]{1,0:T(8,128)}) custom-call(f32[2,64,128]{2,1,0:T(8,128)} %bitcast.17, f32[512,128]{1,0:T(8,128)} %bitcast.13, f32[2,2,128,128]{3,2,1,0:T(8,128)} %cols_hbm.1, s32[2,128]{1,0:T(2,128)} %pivots_hbm.1, s32[2]{0:T(128)} %ranks_hbm.1), custom_call_target="tpu_custom_call" | custom-call | flops 131072 | bytes 262144 | tf_op jit(solution)/shard_map/pallas_call | solution.py:255
  9.2 0.0 all-gather.5.cloned.1.call-update
  9.2 17.8 %all_to_all.10 = f32[32,4,128]{2,1,0:T(4,128)S(1)} all-to-all(f32[32,4,128]{2,1,0:T(4,128)} %bitcast.16), channel_id=1, replica_groups=mesh['y'=4,'x'=4,'c'=2,'col'=16] {'y','x','c'}, dimensions={0} | all-to-all | bytes 131072 | tf_op jit(solution)/shard_map/all_to_all | solution.py:271
  27.1 45.6 %all-gather.2.rows_ref = f32[16,126,128]{2,1,0:T(8,128)S(1)} all-gather(f32[1,126,128]{2,1,0:T(8,128)S(1)} %maximum_bitcast_fusion), channel_id=3, replica_groups=mesh['y'=4,'x'=4,'c'=2,'col'=16] {'col'}, dimensions={0}, use_global_device_ids=true | all-gather | bytes 1096704 | tf_op jit(solution)/shard_map/all_gather | solution.py:273
  72.7 0.0 copy-done
  72.7 1.2 shard_map.78
  73.9 26.9 %all_to_all.11.right_ref = f32[16,8,4,8,128]{4,3,2,1,0:T(8,128)S(1)} all-to-all(f32[16,8,4,8,128]{4,3,2,1,0:T(8,128)S(1)} %shard_map.78), channel_id=1, replica_groups=mesh['y'=4,'x'=4,'c'=2,'col'=16] {'y','x'}, dimensions={0} | all-to-all | bytes 4194304 | tf_op jit(solution)/shard_map/all_to_all | solution.py:282
  100.8 7.9 %collective-permute-start = (f32[16,8,4,8,128]{4,3,2,1,0:T(8,128)S(1)}, f32[16,8,4,8,128]{4,3,2,1,0:T(8,128)}, u32[]{:S(2)}, u32[]{:S(2)}) collective-permute-start(f32[16,8,4,8,128]{4,3,2,1,0:T(8,128)S(1)} %all_to_all.11.right_ref), channel_id=1, source_target_pairs={{0,16},{16,0},{1,17},{17,1},{2,18},{18,2},{3,19},{19,3},{4,20},{20... | collective-permute-start | bytes 6291464 | tf_op jit(solution)/shard_map/ppermute | solution.py:283
  108.7 0.0 all-gather.5.cloned.1.call-done
  108.7 4.5 %shard_map.79 = (f32[512,512]{1,0:T(8,128)S(1)}, bf16[2,512,1024]{2,1,0:T(8,128)(2,1)S(1)}, f32[8,128]{1,0:T(8,128)S(1)}) custom-call(f32[16,520,128]{2,1,0:T(8,128)} %bitcast.12, f32[16,8,4,8,128]{4,3,2,1,0:T(8,128)S(1)} %all_to_all.11.right_ref), custom_call_target="tpu_custom_call" | custom-call | flops 1610612736 | bytes 7340032 | tf_op jit(solution)/shard_map/pallas_call | solution.py:215
  113.2 0.0 collective-permute-done.right_ref
  113.2 5.7 %shard_map.80 = (f32[2,2,128,128]{3,2,1,0:T(8,128)}, f32[2,1,2,128,128]{4,3,2,1,0:T(8,128)}) custom-call(f32[8,128]{1,0:T(8,128)S(1)} %get-tuple-element.9.factor_ref, f32[512,512]{1,0:T(8,128)S(1)} %get-tuple-element.10.start_ref, bf16[2,512,1024]{2,1,0:T(8,128)(2,1)S(1)} %get-tuple-element.11.left_ref, f32[16,8,4,8,128]{4,3,2,1,0:T(8,128)} %collective-permute-done.right_ref), custom_call_target="tpu_custom_call" | custom-call | flops 1610612736 | bytes 8388608 | tf_op jit(solution)/shard_map/pallas_call | solution.py:234
  (4 shorter events, 0.0 us)
Async XLA Ops:
  7.2 65.5 %copy-start = (f32[1,2,2048,128]{3,2,1,0:T(8,128)S(1)}, f32[1,2,2048,128]{3,2,1,0:T(8,128)}, u32[]{:S(2)}) copy-start(f32[1,2,2048,128]{3,2,1,0:T(8,128)} %param.11) | copy-start | bytes 6291460
  7.2 101.5 %all-gather.5.cloned.1.call-start = ((), (), s32[]{:S(2)}) async-start(), calls=%async_computation.2 | async-start | bytes 4526080 | tf_op jit(solution)/shard_map/all_gather | solution.py:270
  100.8 12.4 %collective-permute-start = (f32[16,8,4,8,128]{4,3,2,1,0:T(8,128)S(1)}, f32[16,8,4,8,128]{4,3,2,1,0:T(8,128)}, u32[]{:S(2)}, u32[]{:S(2)}) collective-permute-start(f32[16,8,4,8,128]{4,3,2,1,0:T(8,128)S(1)} %all_to_all.11.right_ref), channel_id=1, source_target_pairs={{0,16},{16,0},{1,17},{17,1},{2,18},{18,2},{3,19},{19,3},{4,20},{20... | collective-permute-start | bytes 6291464 | tf_op jit(solution)/shard_map/ppermute | solution.py:283
Sparse Core Ops, SparseCore 0:
  10.1 83.8 all-gather.4

commit v7 on v6

--- a/solution.py
+++ b/solution.py
@@ -11,7 +11,7 @@
 DOWN_INVERSE, UP_INVERSE = 2.0 ** -16, 2.0 ** 16
 DOWN_PRODUCT, UP_PRODUCT = 2.0 ** -24, 2.0 ** 24
 PAIRS = 8
-DEPTH = 4
+DEPTH = 2
 ROWS = 512
 
 
@@ -126,21 +126,23 @@
     return jnp.concatenate(pair, axis=0).reshape(128, 128)
 
 
-def dot3(left_high, left_low, right):
-    high, low = split(right)
-    return dot(left_high, high) + (dot(left_high, low) + dot(left_low, high))
-
-
-def first_kernel(rows_ref, right_ref, out_ref, later_ref, factor_ref, held_ref, sems):
+def dot3(left, right):
+    return dot(left[0], right[0]) + (dot(left[0], right[1]) + dot(left[1], right[0]))
+
+
+def first_kernel(rows_ref, right_ref, out_ref, later_ref, factor_ref, held_ref, high_ref, low_ref, sems):
     copies = [pltpu.make_async_copy(rows_ref.at[z], held_ref.at[z], sems.at[z]) for z in range(16)]
     for copy in copies:
         copy.start()
     core = lax.axis_index("c")
     shift = jnp.where(core == 0, 2, 126)
     keep = ((lax.broadcasted_iota(jnp.int32, (128, 128), 1) & 3) < 2) == (core == 0)
+    for n in range(PAIRS):
+        right = jnp.concatenate([tiles(right_ref[:, n, m]) for m in range(4)], axis=1)
+        high_ref[128 * n : 128 * n + 128, :], low_ref[128 * n : 128 * n + 128, :] = split(right)
     total = None
     for step in range(PAIRS // DEPTH):
-        lefts, rights = [], []
+        lefts = []
         for n in range(step * DEPTH, step * DEPTH + DEPTH):
             copies[2 * n].wait()
             copies[2 * n + 1].wait()
@@ -155,9 +157,8 @@
                     later_ref[0, span, 128 * n : 128 * n + 128] = high
                     later_ref[1, span, 128 * n : 128 * n + 128] = low
             lefts.append(jnp.concatenate(blocks, axis=0))
-            rights.append(jnp.concatenate([tiles(right_ref[:, n, m]) for m in range(4)], axis=1))
-        high, low = split(jnp.concatenate(lefts, axis=1))
-        term = dot3(high, low, jnp.concatenate(rights, axis=0))
+        at = slice(128 * DEPTH * step, 128 * DEPTH * step + 128 * DEPTH)
+        term = dot3(split(jnp.concatenate(lefts, axis=1)), (high_ref[at, :], low_ref[at, :]))
         total = term if total is None else total + term
     out_ref[...] = total
     entries = jnp.sum(held_ref[:, ROWS : ROWS + 8], axis=0)
@@ -170,7 +171,19 @@
 
 
 def second_kernel(
-    factor_ref, start_ref, left_ref, right_ref, panel_ref, cores_ref, near_ref, panel_vmem, cores_vmem, sems, out_sems
+    factor_ref,
+    start_ref,
+    left_ref,
+    right_ref,
+    panel_ref,
+    cores_ref,
+    near_ref,
+    high_ref,
+    low_ref,
+    panel_vmem,
+    cores_vmem,
+    sems,
+    out_sems,
 ):
     copies = [
         [
@@ -186,17 +199,16 @@
         (pltpu.make_async_copy(panel_vmem, panel_ref, out_sems.at[0]), panel_vmem, UP_INVERSE),
         (pltpu.make_async_copy(cores_vmem, cores_ref, out_sems.at[1]), cores_vmem, UP_PRODUCT),
     )
+    def ready(n):
+        for z in range(PAIRS):
+            copies[n][z].wait()
+            right = jnp.concatenate([tiles(near_ref[n, z, :, p]) for p in range(2)], axis=1)
+            high_ref[n, 128 * z : 128 * z + 128, :], low_ref[n, 128 * z : 128 * z + 128, :] = split(right)
+
+    ready(0)
+    ready(1)
     for n, (result, out, up) in enumerate(results):
-        for copy in copies[n]:
-            copy.wait()
-        right = jnp.concatenate(
-            [
-                jnp.concatenate([tiles(near_ref[n, z, :, p]) for p in range(2)], axis=1)
-                for z in range(PAIRS)
-            ],
-            axis=0,
-        )
-        total = start_ref[:, 256 * n : 256 * n + 256] + dot3(left_ref[0], left_ref[1], right)
+        total = start_ref[:, 256 * n : 256 * n + 256] + dot3(left_ref, (high_ref[n], low_ref[n]))
         for i in range(2):
             fr, fi = columns[:, 2 * i : 2 * i + 1], columns[:, 2 * i + 1 : 2 * i + 2]
             by_real, by_imag = total[128 * i : 128 * i + 128], total[256 + 128 * i : 384 + 128 * i]
@@ -221,7 +233,12 @@
             jax.ShapeDtypeStruct((2, 512, 1024), jnp.bfloat16),
             jax.ShapeDtypeStruct((8, 128), jnp.float32),
         ),
-        scratch_shapes=[pltpu.VMEM((16, ROWS + 8, 128), jnp.float32), pltpu.SemaphoreType.DMA((16,))],
+        scratch_shapes=[
+            pltpu.VMEM((16, ROWS + 8, 128), jnp.float32),
+            pltpu.VMEM((1024, 512), jnp.bfloat16),
+            pltpu.VMEM((1024, 512), jnp.bfloat16),
+            pltpu.SemaphoreType.DMA((16,)),
+        ],
         compiler_params=params(48),
         cost_estimate=cost(2 * 3 * 512 * 1024 * 512, 7 * 2**20),
     )(rows, right)
@@ -238,6 +255,8 @@
         out_shape=tuple(jax.ShapeDtypeStruct(shape, jnp.float32) for shape in shapes),
         scratch_shapes=[
             pltpu.VMEM((2, PAIRS, 16, 2, 8, 128), jnp.float32),
+            pltpu.VMEM((2, 1024, 256), jnp.bfloat16),
+            pltpu.VMEM((2, 1024, 256), jnp.bfloat16),
             pltpu.VMEM(shapes[0], jnp.float32),
             pltpu.VMEM(shapes[1], jnp.float32),
             pltpu.SemaphoreType.DMA((2, PAIRS)),

time: 126 us -> 125 us (level)
  Pallas kernels: 13.4 us -> 11.9 us
    pallas_call x1, Pallas kernels: 5.75 us -> 4.44 us  [second_call(): pl.pallas_call(second_kernel, in_specs=[vmem, vmem, vmem, hbm], out_specs...]
where the time goes in v7:
time: 125 us; the launch traced here: 124 us
  blocking collectives  90.3 us (72%)
  between operations  14.1 us (11%)
  Pallas kernels  11.9 us (10%)
  starting transfers between devices  7.94 us (6%)
    all_gather x1, blocking collectives, on_device(): packed = lax.all_gather(packed, 'col', axis=0)  45.6 us
    all_to_all x1, blocking collectives, on_device(): own = lax.all_to_all(right, CHIPS, 0, 0)  26.9 us
    all_to_all x1, blocking collectives, on_device(): lax.all_to_all(packed.reshape(32, 4, 128), CHIPS + ('c',), 0, 0)  17.8 us
    ppermute x1, starting transfers between devices, on_device(): other = lax.ppermute(own, 'c', [(0, 1), (1, 0)])  7.9 us
    pallas_call x1, Pallas kernels, second_call(): pl.pallas_call(second_kernel, in_specs=[vmem, vmem, vmem, hbm], out_specs...  4.44 us
    pallas_call x1, Pallas kernels, first_call(): pl.pallas_call(first_kernel, in_specs=[pl.BlockSpec(memory_space=pltpu.HB...  4.25 us
  transfers between devices with their start and end apart: 2, of which 0 were waited for; matrix products, arithmetic and copies ran while one was open for 0% of the time, Pallas kernels for 4%

profile of v7, /device:TPU:1, one launch (start us, length us, event | category | flops | bytes accessed | tf_op | source)
XLA Modules:
  0.0 124.3 jit_solution(17297524773068474815)
XLA Ops:
  7.2 0.0 copy-start
  7.2 0.0 all-gather.5.cloned.1.call-start
  7.2 2.0 %shard_map.77 = (f32[16,8,128]{2,1,0:T(8,128)}, f32[520,128]{1,0:T(8,128)}) custom-call(f32[2,64,128]{2,1,0:T(8,128)} %bitcast.17, f32[512,128]{1,0:T(8,128)} %bitcast.13, f32[2,2,128,128]{3,2,1,0:T(8,128)} %cols_hbm.1, s32[2,128]{1,0:T(2,128)} %pivots_hbm.1, s32[2]{0:T(128)} %ranks_hbm.1), custom_call_target="tpu_custom_call" | custom-call | flops 131072 | bytes 262144 | tf_op jit(solution)/shard_map/pallas_call | solution.py:274
  9.2 0.0 all-gather.5.cloned.1.call-update
  9.2 17.8 %all_to_all.10 = f32[32,4,128]{2,1,0:T(4,128)S(1)} all-to-all(f32[32,4,128]{2,1,0:T(4,128)} %bitcast.16), channel_id=1, replica_groups=mesh['y'=4,'x'=4,'c'=2,'col'=16] {'y','x','c'}, dimensions={0} | all-to-all | bytes 131072 | tf_op jit(solution)/shard_map/all_to_all | solution.py:290
  27.1 45.6 %all-gather.2.rows_ref = f32[16,126,128]{2,1,0:T(8,128)S(1)} all-gather(f32[1,126,128]{2,1,0:T(8,128)S(1)} %maximum_bitcast_fusion), channel_id=3, replica_groups=mesh['y'=4,'x'=4,'c'=2,'col'=16] {'col'}, dimensions={0}, use_global_device_ids=true | all-gather | bytes 1096704 | tf_op jit(solution)/shard_map/all_gather | solution.py:292
  72.7 0.0 copy-done
  72.7 1.2 shard_map.78
  73.9 26.9 %all_to_all.11.right_ref = f32[16,8,4,8,128]{4,3,2,1,0:T(8,128)S(1)} all-to-all(f32[16,8,4,8,128]{4,3,2,1,0:T(8,128)S(1)} %shard_map.78), channel_id=1, replica_groups=mesh['y'=4,'x'=4,'c'=2,'col'=16] {'y','x'}, dimensions={0} | all-to-all | bytes 4194304 | tf_op jit(solution)/shard_map/all_to_all | solution.py:301
  100.8 7.9 %collective-permute-start = (f32[16,8,4,8,128]{4,3,2,1,0:T(8,128)S(1)}, f32[16,8,4,8,128]{4,3,2,1,0:T(8,128)}, u32[]{:S(2)}, u32[]{:S(2)}) collective-permute-start(f32[16,8,4,8,128]{4,3,2,1,0:T(8,128)S(1)} %all_to_all.11.right_ref), channel_id=1, source_target_pairs={{0,16},{16,0},{1,17},{17,1},{2,18},{18,2},{3,19},{19,3},{4,20},{20... | collective-permute-start | bytes 6291464 | tf_op jit(solution)/shard_map/ppermute | solution.py:302
  108.7 0.0 all-gather.5.cloned.1.call-done
  108.7 4.3 %shard_map.79 = (f32[512,512]{1,0:T(8,128)S(1)}, bf16[2,512,1024]{2,1,0:T(8,128)(2,1)S(1)}, f32[8,128]{1,0:T(8,128)S(1)}) custom-call(f32[16,520,128]{2,1,0:T(8,128)} %bitcast.12, f32[16,8,4,8,128]{4,3,2,1,0:T(8,128)S(1)} %all_to_all.11.right_ref), custom_call_target="tpu_custom_call" | custom-call | flops 1610612736 | bytes 7340032 | tf_op jit(solution)/shard_map/pallas_call | solution.py:227
  113.0 0.0 collective-permute-done.right_ref
  113.0 4.4 %shard_map.80 = (f32[2,2,128,128]{3,2,1,0:T(8,128)}, f32[2,1,2,128,128]{4,3,2,1,0:T(8,128)}) custom-call(f32[8,128]{1,0:T(8,128)S(1)} %get-tuple-element.9.factor_ref, f32[512,512]{1,0:T(8,128)S(1)} %get-tuple-element.10.start_ref, bf16[2,512,1024]{2,1,0:T(8,128)(2,1)S(1)} %get-tuple-element.11.left_ref, f32[16,8,4,8,128]{4,3,2,1,0:T(8,128)} %collective-permute-done.right_ref), custom_call_target="tpu_custom_call" | custom-call | flops 1610612736 | bytes 8388608 | tf_op jit(solution)/shard_map/pallas_call | solution.py:251
  (4 shorter events, 0.0 us)
Async XLA Ops:
  7.2 65.5 %copy-start = (f32[1,2,2048,128]{3,2,1,0:T(8,128)S(1)}, f32[1,2,2048,128]{3,2,1,0:T(8,128)}, u32[]{:S(2)}) copy-start(f32[1,2,2048,128]{3,2,1,0:T(8,128)} %param.11) | copy-start | bytes 6291460
  7.2 101.5 %all-gather.5.cloned.1.call-start = ((), (), s32[]{:S(2)}) async-start(), calls=%async_computation.2 | async-start | bytes 4526080 | tf_op jit(solution)/shard_map/all_gather | solution.py:289
  100.8 12.2 %collective-permute-start = (f32[16,8,4,8,128]{4,3,2,1,0:T(8,128)S(1)}, f32[16,8,4,8,128]{4,3,2,1,0:T(8,128)}, u32[]{:S(2)}, u32[]{:S(2)}) collective-permute-start(f32[16,8,4,8,128]{4,3,2,1,0:T(8,128)S(1)} %all_to_all.11.right_ref), channel_id=1, source_target_pairs={{0,16},{16,0},{1,17},{17,1},{2,18},{18,2},{3,19},{19,3},{4,20},{20... | collective-permute-start | bytes 6291464 | tf_op jit(solution)/shard_map/ppermute | solution.py:302
Sparse Core Ops, SparseCore 0:
  10.1 83.8 all-gather.4

commit v8 on v7

--- a/solution.py
+++ b/solution.py
@@ -50,7 +50,7 @@
 
 
 def start_kernel(
-    block_hbm, rows_hbm, cols_hbm, pivots_hbm, ranks_hbm, out_ref, sent_ref, block_ref, cols_ref, pivots_ref, ranks_ref, sems
+    block_hbm, rows_hbm, cols_hbm, pivots_hbm, ranks_hbm, out_hbm, sent_hbm, block_ref, cols_ref, pivots_ref, ranks_ref, out_ref, sent_ref, sems
 ):
     pairs = (
         (block_hbm, block_ref),
@@ -67,6 +67,14 @@
     low, high = interleave(rows[:8], rows[8:])
     out_ref[0:8] = low
     out_ref[8:16] = high
+    results = [
+        pltpu.make_async_copy(out_ref, out_hbm, sems.at[5]),
+        pltpu.make_async_copy(sent_ref.at[0:ROWS], sent_hbm.at[0:ROWS], sems.at[6]),
+        pltpu.make_async_copy(sent_ref.at[ROWS : ROWS + 8], sent_hbm.at[ROWS : ROWS + 8], sems.at[7]),
+    ]
+    results[0].start()
+    copies[4].wait()
+    results[1].start()
     for copy in copies[1:4]:
         copy.wait()
     width = cols_ref.shape[2]
@@ -78,7 +86,9 @@
             at = ROWS + 2 * i + p
             sent_ref[at : at + 1, :] = jnp.sum(jnp.where(hit, cols_ref[i, p], 0.0), axis=0, keepdims=True)
     sent_ref[ROWS + 4 : ROWS + 8, :] = jnp.zeros((4, 128), jnp.float32)
-    copies[4].wait()
+    results[2].start()
+    for result in results:
+        result.wait()
 
 
 def straight(x):
@@ -274,14 +284,16 @@
     packed, sent = pl.pallas_call(
         start_kernel,
         in_specs=[hbm] * 5,
-        out_specs=(vmem, vmem),
+        out_specs=(hbm, hbm),
         out_shape=(jax.ShapeDtypeStruct((16, 8, 128), f32), jax.ShapeDtypeStruct((ROWS + 8, 128), f32)),
         scratch_shapes=[
             pltpu.VMEM((2, 64, 128), f32),
             pltpu.VMEM(col_samples.shape, f32),
             pltpu.VMEM(pivot_rows.shape, jnp.int32),
             pltpu.SMEM(rank_blocks.shape, jnp.int32),
-            pltpu.SemaphoreType.DMA((5,)),
+            pltpu.VMEM((16, 8, 128), f32),
+            pltpu.VMEM((ROWS + 8, 128), f32),
+            pltpu.SemaphoreType.DMA((8,)),
         ],
         compiler_params=params(61.75),
         cost_estimate=cost(2**17, 2**18),

time: 125 us -> 123 us (0.984)
  blocking collectives: 90.3 us -> 87.6 us
    all_to_all x1, blocking collectives: 26.9 us -> 24.9 us  [on_device(): own = lax.all_to_all(right, CHIPS, 0, 0)]
where the time goes in v8:
time: 123 us
  blocking collectives  87.6 us (71%)
  between operations  14.1 us (11%)
  Pallas kernels  11.9 us (10%)
  starting transfers between devices  9.19 us (7%)
    all_gather x1, blocking collectives, on_device(): packed = lax.all_gather(packed, 'col', axis=0)  45 us
    all_to_all x1, blocking collectives, on_device(): own = lax.all_to_all(right, CHIPS, 0, 0)  24.9 us
    all_to_all x1, blocking collectives, on_device(): lax.all_to_all(packed.reshape(32, 4, 128), CHIPS + ('c',), 0, 0)  17.8 us
    ppermute x1, starting transfers between devices, on_device(): other = lax.ppermute(own, 'c', [(0, 1), (1, 0)])  9.15 us
    pallas_call x1, Pallas kernels, second_call(): pl.pallas_call(second_kernel, in_specs=[vmem, vmem, vmem, hbm], out_specs...  4.44 us
    pallas_call x1, Pallas kernels, first_call(): pl.pallas_call(first_kernel, in_specs=[pl.BlockSpec(memory_space=pltpu.HB...  4.26 us
  transfers between devices with their start and end apart: 2, of which 0 were waited for; matrix products, arithmetic and copies ran while one was open for 0% of the time, Pallas kernels for 4%

profile of v8, /device:TPU:1, one launch (start us, length us, event | category | flops | bytes accessed | tf_op | source)
XLA Modules:
  0.0 122.9 jit_solution(11852903065122550099)
XLA Ops:
  7.2 0.0 copy-start
  7.2 0.0 all-gather.5.cloned.1.call-start
  7.2 2.0 %shard_map.77 = (f32[16,8,128]{2,1,0:T(8,128)}, f32[520,128]{1,0:T(8,128)}) custom-call(f32[2,64,128]{2,1,0:T(8,128)} %bitcast.17, f32[512,128]{1,0:T(8,128)} %bitcast.13, f32[2,2,128,128]{3,2,1,0:T(8,128)} %cols_hbm.1, s32[2,128]{1,0:T(2,128)} %pivots_hbm.1, s32[2]{0:T(128)} %ranks_hbm.1), custom_call_target="tpu_custom_call" | custom-call | flops 131072 | bytes 262144 | tf_op jit(solution)/shard_map/pallas_call | solution.py:284
  9.2 0.0 all-gather.5.cloned.1.call-update
  9.2 17.8 %all_to_all.10 = f32[32,4,128]{2,1,0:T(4,128)S(1)} all-to-all(f32[32,4,128]{2,1,0:T(4,128)} %bitcast.16), channel_id=1, replica_groups=mesh['y'=4,'x'=4,'c'=2,'col'=16] {'y','x','c'}, dimensions={0} | all-to-all | bytes 131072 | tf_op jit(solution)/shard_map/all_to_all | solution.py:302
  27.1 45.0 %all-gather.2.rows_ref = f32[16,126,128]{2,1,0:T(8,128)S(1)} all-gather(f32[1,126,128]{2,1,0:T(8,128)S(1)} %maximum_bitcast_fusion), channel_id=3, replica_groups=mesh['y'=4,'x'=4,'c'=2,'col'=16] {'col'}, dimensions={0}, use_global_device_ids=true | all-gather | bytes 1096704 | tf_op jit(solution)/shard_map/all_gather | solution.py:304
  72.1 0.0 copy-done
  72.1 1.2 shard_map.78
  73.3 24.9 %all_to_all.11.right_ref = f32[16,8,4,8,128]{4,3,2,1,0:T(8,128)S(1)} all-to-all(f32[16,8,4,8,128]{4,3,2,1,0:T(8,128)S(1)} %shard_map.78), channel_id=1, replica_groups=mesh['y'=4,'x'=4,'c'=2,'col'=16] {'y','x'}, dimensions={0} | all-to-all | bytes 4194304 | tf_op jit(solution)/shard_map/all_to_all | solution.py:313
  98.1 9.1 %collective-permute-start = (f32[16,8,4,8,128]{4,3,2,1,0:T(8,128)S(1)}, f32[16,8,4,8,128]{4,3,2,1,0:T(8,128)}, u32[]{:S(2)}, u32[]{:S(2)}) collective-permute-start(f32[16,8,4,8,128]{4,3,2,1,0:T(8,128)S(1)} %all_to_all.11.right_ref), channel_id=1, source_target_pairs={{0,16},{16,0},{1,17},{17,1},{2,18},{18,2},{3,19},{19,3},{4,20},{20... | collective-permute-start | bytes 6291464 | tf_op jit(solution)/shard_map/ppermute | solution.py:314
  107.3 0.0 all-gather.5.cloned.1.call-done
  107.3 4.3 %shard_map.79 = (f32[512,512]{1,0:T(8,128)S(1)}, bf16[2,512,1024]{2,1,0:T(8,128)(2,1)S(1)}, f32[8,128]{1,0:T(8,128)S(1)}) custom-call(f32[16,520,128]{2,1,0:T(8,128)} %bitcast.12, f32[16,8,4,8,128]{4,3,2,1,0:T(8,128)S(1)} %all_to_all.11.right_ref), custom_call_target="tpu_custom_call" | custom-call | flops 1610612736 | bytes 7340032 | tf_op jit(solution)/shard_map/pallas_call | solution.py:237
  111.6 0.0 collective-permute-done.right_ref
  111.6 4.4 %shard_map.80 = (f32[2,2,128,128]{3,2,1,0:T(8,128)}, f32[2,1,2,128,128]{4,3,2,1,0:T(8,128)}) custom-call(f32[8,128]{1,0:T(8,128)S(1)} %get-tuple-element.9.factor_ref, f32[512,512]{1,0:T(8,128)S(1)} %get-tuple-element.10.start_ref, bf16[2,512,1024]{2,1,0:T(8,128)(2,1)S(1)} %get-tuple-element.11.left_ref, f32[16,8,4,8,128]{4,3,2,1,0:T(8,128)} %collective-permute-done.right_ref), custom_call_target="tpu_custom_call" | custom-call | flops 1610612736 | bytes 8388608 | tf_op jit(solution)/shard_map/pallas_call | solution.py:261
  (4 shorter events, 0.0 us)
Async XLA Ops:
  7.2 64.9 %copy-start = (f32[1,2,2048,128]{3,2,1,0:T(8,128)S(1)}, f32[1,2,2048,128]{3,2,1,0:T(8,128)}, u32[]{:S(2)}) copy-start(f32[1,2,2048,128]{3,2,1,0:T(8,128)} %param.11) | copy-start | bytes 6291460
  7.2 100.1 %all-gather.5.cloned.1.call-start = ((), (), s32[]{:S(2)}) async-start(), calls=%async_computation.2 | async-start | bytes 4526080 | tf_op jit(solution)/shard_map/all_gather | solution.py:301
  98.1 13.5 %collective-permute-start = (f32[16,8,4,8,128]{4,3,2,1,0:T(8,128)S(1)}, f32[16,8,4,8,128]{4,3,2,1,0:T(8,128)}, u32[]{:S(2)}, u32[]{:S(2)}) collective-permute-start(f32[16,8,4,8,128]{4,3,2,1,0:T(8,128)S(1)} %all_to_all.11.right_ref), channel_id=1, source_target_pairs={{0,16},{16,0},{1,17},{17,1},{2,18},{18,2},{3,19},{19,3},{4,20},{20... | collective-permute-start | bytes 6291464 | tf_op jit(solution)/shard_map/ppermute | solution.py:314
Sparse Core Ops, SparseCore 0:
  10.1 83.8 all-gather.4

commit v9 on v8

--- a/solution.py
+++ b/solution.py
@@ -1,3 +1,5 @@
+import functools
+
 import jax
 import jax.numpy as jnp
 from jax import lax
@@ -13,6 +15,7 @@
 PAIRS = 8
 DEPTH = 2
 ROWS = 512
+BASE = 2 * PAIRS, 0
 
 
 def params(mebibytes=24):
@@ -124,9 +127,9 @@
     for n, x in enumerate((block * DOWN_INVERSE, product)):
         x = x.reshape(PAIRS, 2, 8, 128)
         real, imag = interleave(x[:, 0], x[:, 1])
+        pair = jnp.stack([real, imag], axis=1).reshape(2 * PAIRS, 8, 128)
         for d in range(16):
-            out_ref[d, :, 2 * n] = real
-            out_ref[d, :, 2 * n + 1] = imag
+            out_ref[d, BASE[n] : BASE[n] + 2 * PAIRS] = pair
 
 
 def tiles(block):
@@ -148,7 +151,7 @@
     shift = jnp.where(core == 0, 2, 126)
     keep = ((lax.broadcasted_iota(jnp.int32, (128, 128), 1) & 3) < 2) == (core == 0)
     for n in range(PAIRS):
-        right = jnp.concatenate([tiles(right_ref[:, n, m]) for m in range(4)], axis=1)
+        right = jnp.concatenate([tiles(right_ref[:, BASE[m // 2] + 2 * n + m % 2]) for m in range(4)], axis=1)
         high_ref[128 * n : 128 * n + 128, :], low_ref[128 * n : 128 * n + 128, :] = split(right)
     total = None
     for step in range(PAIRS // DEPTH):
@@ -197,7 +200,9 @@
 ):
     copies = [
         [
-            pltpu.make_async_copy(right_ref.at[:, z, 2 * n : 2 * n + 2], near_ref.at[n, z], sems.at[n, z])
+            pltpu.make_async_copy(
+                right_ref.at[:, BASE[n] + 2 * z : BASE[n] + 2 * z + 2], near_ref.at[n, z], sems.at[n, z]
+            )
             for z in range(PAIRS)
         ]
         for n in range(2)
@@ -275,6 +280,12 @@
         compiler_params=params(48),
         cost_estimate=cost(2 * 3 * 512 * 1024 * 512, 8 * 2**20),
     )(factor, start, left, right)
+
+
+def spread(pairs, right):
+    count = 2 * PAIRS + 2 * pairs
+    got = lax.all_to_all(right[:, :count], CHIPS, 0, 0)
+    return jnp.pad(got, ((0, 0), (0, right.shape[1] - count), (0, 0), (0, 0)))
 
 
 def on_device(col_samples, row_samples, pivot_rows, rank_blocks, upper_inverse, upanel_left):
@@ -306,11 +317,13 @@
         right_kernel,
         in_specs=[vmem, vmem],
         out_specs=vmem,
-        out_shape=jax.ShapeDtypeStruct((16, PAIRS, 4, 8, 128), f32),
+        out_shape=jax.ShapeDtypeStruct((16, 4 * PAIRS, 8, 128), f32),
         compiler_params=params(),
         cost_estimate=cost(2 * 3 * 128 * 2048 * 256, 5 * 2**20),
     )(packed, upanel_left[0])
-    own = lax.all_to_all(right, CHIPS, 0, 0)
+    place = lax.axis_index("col")
+    kind = (place >= 4).astype(jnp.int32) + (place >= 8).astype(jnp.int32)
+    own = lax.switch(kind, [functools.partial(spread, pairs) for pairs in (2, 4, 8)], right)
     other = lax.ppermute(own, "c", [(0, 1), (1, 0)])
     start, left, factor = first_call(rows, own)
     return second_call(factor, start, left, other)

time: 123 us -> 118 us (0.959)
  blocking collectives: 87.6 us -> 61.3 us
  starting transfers between devices: 9.19 us -> 19.5 us
  waiting for transfers between devices: 0.04 us -> 7.46 us
  local copies, waits for them, and re-layouts: 0.01 us -> 1.65 us
    all_to_all x2 -> x1, blocking collectives: 42.7 us -> 16.6 us  [spread(): got = lax.all_to_all(right[:, :count], CHIPS, 0, 0)]
    all_to_all x0 -> x1, starting transfers between devices: none -> 10.4 us  [on_device(): lax.all_to_all(packed.reshape(32, 4, 128), CHIPS + ('c',), 0, 0)]
    all_to_all x0 -> x1, waiting for transfers between devices: none -> 7.42 us  [on_device(): lax.all_to_all(packed.reshape(32, 4, 128), CHIPS + ('c',), 0, 0)]
    pallas_call x1, Pallas kernels: 4.26 us -> 5.86 us  [first_call(): pl.pallas_call(first_kernel, in_specs=[pl.BlockSpec(memory_space=pltpu.HB...]
    unnamed x2 -> x4, local copies, waits for them, and re-layouts: 0.01 us -> 1.33 us
  transfers between devices with their start and end apart: 2 -> 3, of which waited for: 0 -> 1; matrix products, arithmetic and copies ran while one was open for 0% -> 0% of each run, Pallas kernels for 4% -> 6%
where the time goes in v9:
time: 118 us; the launch traced here: 117 us
  blocking collectives  61.3 us (52%)
  starting transfers between devices  19.5 us (17%)
  between operations  14.2 us (12%)
  Pallas kernels  12.6 us (11%)
  waiting for transfers between devices  7.46 us (6%)
  local copies, waits for them, and re-layouts  1.65 us (1%)
    all_gather x1, blocking collectives, on_device(): packed = lax.all_gather(packed, 'col', axis=0)  44.7 us
    all_to_all x1, blocking collectives, spread(): got = lax.all_to_all(right[:, :count], CHIPS, 0, 0)  16.6 us
    all_to_all x1, starting transfers between devices, on_device(): lax.all_to_all(packed.reshape(32, 4, 128), CHIPS + ('c',), 0, 0)  10.4 us
    ppermute x1, starting transfers between devices, on_device(): other = lax.ppermute(own, 'c', [(0, 1), (1, 0)])  9.1 us
    all_to_all x1, waiting for transfers between devices, on_device(): lax.all_to_all(packed.reshape(32, 4, 128), CHIPS + ('c',), 0, 0)  7.42 us
    pallas_call x1, Pallas kernels, first_call(): pl.pallas_call(first_kernel, in_specs=[pl.BlockSpec(memory_space=pltpu.HB...  5.86 us
    pallas_call x1, Pallas kernels, second_call(): pl.pallas_call(second_kernel, in_specs=[vmem, vmem, vmem, hbm], out_specs...  3.6 us
  transfers between devices with their start and end apart: 3, of which 1 were waited for; matrix products, arithmetic and copies ran while one was open for 0% of the time, Pallas kernels for 6%

profile of v9, /device:TPU:1, one launch (start us, length us, event | category | flops | bytes accessed | tf_op | source)
XLA Modules:
  0.0 116.8 jit_solution(14189320011572858318)
XLA Ops:
  7.2 0.0 copy-start
  7.2 0.0 all-gather.5.cloned.1.call-start
  7.2 2.0 %shard_map.77 = (f32[16,8,128]{2,1,0:T(8,128)}, f32[520,128]{1,0:T(8,128)}) custom-call(f32[2,64,128]{2,1,0:T(8,128)} %bitcast.17, f32[512,128]{1,0:T(8,128)} %bitcast.13, f32[2,2,128,128]{3,2,1,0:T(8,128)} %cols_hbm.1, s32[2,128]{1,0:T(2,128)} %pivots_hbm.1, s32[2]{0:T(128)} %ranks_hbm.1), custom_call_target="tpu_custom_call" | custom-call | flops 131072 | bytes 262144 | tf_op jit(solution)/shard_map/pallas_call | solution.py:295
  9.2 0.0 all-gather.5.cloned.1.call-update
  9.2 10.4 %all-to-all-start.3 = ((f32[32,4,128]{2,1,0:T(4,128)}), f32[32,4,128]{2,1,0:T(4,128)S(1)}, u32[]{:S(2)}, u32[]{:S(2)}) async-start(f32[32,4,128]{2,1,0:T(4,128)} %bitcast.16), calls=%async_computation.3 | async-start | bytes 131072 | tf_op jit(solution)/shard_map/all_to_all | solution.py:313
  19.7 7.4 %all-to-all-done.3 = f32[32,4,128]{2,1,0:T(4,128)S(1)} async-done(((f32[32,4,128]{2,1,0:T(4,128)}), f32[32,4,128]{2,1,0:T(4,128)S(1)}, u32[]{:S(2)}, u32[]{:S(2)}) %all-to-all-start.3) | async-done | bytes 65568 | tf_op jit(solution)/shard_map/all_to_all | solution.py:313
  27.1 44.7 %all-gather.2.rows_ref = f32[16,126,128]{2,1,0:T(8,128)S(1)} all-gather(f32[1,126,128]{2,1,0:T(8,128)S(1)} %maximum_bitcast_fusion), channel_id=3, replica_groups=mesh['y'=4,'x'=4,'c'=2,'col'=16] {'col'}, dimensions={0}, use_global_device_ids=true | all-gather | bytes 1096704 | tf_op jit(solution)/shard_map/all_gather | solution.py:315
  71.8 0.0 copy-done
  71.8 1.2 %shard_map.78 = f32[16,32,8,128]{3,2,1,0:T(8,128)S(1)} custom-call(f32[16,126,128]{2,1,0:T(8,128)S(1)} %all-gather.2.rows_ref, f32[2,2048,128]{2,1,0:T(8,128)S(1)} %bitcast.11), custom_call_target="tpu_custom_call" | custom-call | flops 402653184 | bytes 5242880 | tf_op jit(solution)/shard_map/pallas_call | solution.py:316
  73.0 16.9 %conditional.1 = (f32[16,32,8,128]{3,2,1,0:T(8,128)S(1)}) conditional(s32[]{:T(128)} %clamp.3, f32[16,32,8,128]{3,2,1,0:T(8,128)S(1)} %shard_map.78, f32[16,32,8,128]{3,2,1,0:T(8,128)S(1)} %shard_map.78, f32[16,32,8,128]{3,2,1,0:T(8,128)S(1)} %shard_map.78), branch_computations={%region_0.1_spmd, %region_1.2_spmd, %region_2.3_spmd} | conditional | bytes 9961484 | solution.py:326
  73.0 0.1 slice.14
  73.1 16.6 %all_to_all.17 = f32[16,20,8,128]{3,2,1,0:T(8,128)S(1)} all-to-all(f32[16,20,8,128]{3,2,1,0:T(8,128)S(1)} %slice.14), channel_id=1, replica_groups=mesh['y'=4,'x'=4,'c'=2,'col'=16] {'y','x'}, dimensions={0} | all-to-all | bytes 2621440 | tf_op jit(solution)/shard_map/cond/branch_0_fun/all_to_all | solution.py:287
  89.7 0.2 pad.6
  90.0 0.0 copy-start.1
  90.0 1.3 %copy-done.1 = f32[16,32,8,128]{3,2,1,0:T(8,128)} copy-done((f32[16,32,8,128]{3,2,1,0:T(8,128)}, f32[16,32,8,128]{3,2,1,0:T(8,128)S(1)}, u32[]{:S(2)}) %copy-start.1) | copy-done | bytes 2097176
  91.3 9.1 %collective-permute-start = (f32[16,32,8,128]{3,2,1,0:T(8,128)}, f32[16,32,8,128]{3,2,1,0:T(8,128)S(1)}, u32[]{:S(2)}, u32[]{:S(2)}) collective-permute-start(f32[16,32,8,128]{3,2,1,0:T(8,128)} %copy-done.1), channel_id=1, source_target_pairs={{0,16},{16,0},{1,17},{17,1},{2,18},{18,2},{3,19},{19,3},{4,20},{20... | collective-permute-start | bytes 6291464 | tf_op jit(solution)/shard_map/ppermute | solution.py:327
  100.4 0.0 all-gather.5.cloned.1.call-done
  100.4 5.9 %shard_map.79 = (f32[512,512]{1,0:T(8,128)S(1)}, bf16[2,512,1024]{2,1,0:T(8,128)(2,1)S(1)}, f32[8,128]{1,0:T(8,128)S(1)}) custom-call(f32[16,520,128]{2,1,0:T(8,128)} %bitcast.12, f32[16,32,8,128]{3,2,1,0:T(8,128)} %copy-done.1), custom_call_target="tpu_custom_call" | custom-call | flops 1610612736 | bytes 7340032 | tf_op jit(solution)/shard_map/pallas_call | solution.py:242
  106.3 0.0 collective-permute-done.right_ref
  106.3 3.6 %shard_map.80 = (f32[2,2,128,128]{3,2,1,0:T(8,128)}, f32[2,1,2,128,128]{4,3,2,1,0:T(8,128)}) custom-call(f32[8,128]{1,0:T(8,128)S(1)} %get-tuple-element.16.factor_ref, f32[512,512]{1,0:T(8,128)S(1)} %get-tuple-element.17.start_ref, bf16[2,512,1024]{2,1,0:T(8,128)(2,1)S(1)} %get-tuple-element.18.left_ref, f32[16,32,8,128]{3,2,1,0:T(8,128)S(1)} %collective-permute-done.right_ref), custom_call_target="tpu_custom_call" | custom-call | flops 1610612736 | bytes 8388608 | tf_op jit(solution)/shard_map/pallas_call | solution.py:266
  (4 shorter events, 0.0 us)
Async XLA Ops:
  7.2 64.7 %copy-start = (f32[1,2,2048,128]{3,2,1,0:T(8,128)S(1)}, f32[1,2,2048,128]{3,2,1,0:T(8,128)}, u32[]{:S(2)}) copy-start(f32[1,2,2048,128]{3,2,1,0:T(8,128)} %param.14) | copy-start | bytes 6291460
  7.2 93.2 %all-gather.5.cloned.1.call-start = ((), (), s32[]{:S(2)}) async-start(), calls=%async_computation.4 | async-start | bytes 4526080 | tf_op jit(solution)/shard_map/all_gather | solution.py:312
  9.2 17.8 %all-to-all-start.3 = ((f32[32,4,128]{2,1,0:T(4,128)}), f32[32,4,128]{2,1,0:T(4,128)S(1)}, u32[]{:S(2)}, u32[]{:S(2)}) async-start(f32[32,4,128]{2,1,0:T(4,128)} %bitcast.16), calls=%async_computation.3 | async-start | bytes 131072 | tf_op jit(solution)/shard_map/all_to_all | solution.py:313
  90.0 1.3 %copy-start.1 = (f32[16,32,8,128]{3,2,1,0:T(8,128)}, f32[16,32,8,128]{3,2,1,0:T(8,128)S(1)}, u32[]{:S(2)}) copy-start(f32[16,32,8,128]{3,2,1,0:T(8,128)S(1)} %get-tuple-element.19.right_ref) | copy-start | bytes 6291460
  91.3 15.0 %collective-permute-start = (f32[16,32,8,128]{3,2,1,0:T(8,128)}, f32[16,32,8,128]{3,2,1,0:T(8,128)S(1)}, u32[]{:S(2)}, u32[]{:S(2)}) collective-permute-start(f32[16,32,8,128]{3,2,1,0:T(8,128)} %copy-done.1), channel_id=1, source_target_pairs={{0,16},{16,0},{1,17},{17,1},{2,18},{18,2},{3,19},{19,3},{4,20},{20... | collective-permute-start | bytes 6291464 | tf_op jit(solution)/shard_map/ppermute | solution.py:327
Sparse Core Ops, SparseCore 0:
  10.1 83.7 all-gather.4

commit v10 on v9

--- a/solution.py
+++ b/solution.py
@@ -143,7 +143,19 @@
     return dot(left[0], right[0]) + (dot(left[0], right[1]) + dot(left[1], right[0]))
 
 
-def first_kernel(rows_ref, right_ref, out_ref, later_ref, factor_ref, held_ref, high_ref, low_ref, sems):
+def first_kernel(rows_ref, right_ref, out_ref, later_ref, factor_ref, held_ref, near_ref, high_ref, low_ref, sems, near_sems):
+    nears = [
+        [
+            pltpu.make_async_copy(
+                right_ref.at[:, BASE[m] + 2 * n : BASE[m] + 2 * n + 2], near_ref.at[m, n], near_sems.at[m, n]
+            )
+            for m in range(2)
+        ]
+        for n in range(PAIRS)
+    ]
+    for pair in nears:
+        for copy in pair:
+            copy.start()
     copies = [pltpu.make_async_copy(rows_ref.at[z], held_ref.at[z], sems.at[z]) for z in range(16)]
     for copy in copies:
         copy.start()
@@ -151,7 +163,9 @@
     shift = jnp.where(core == 0, 2, 126)
     keep = ((lax.broadcasted_iota(jnp.int32, (128, 128), 1) & 3) < 2) == (core == 0)
     for n in range(PAIRS):
-        right = jnp.concatenate([tiles(right_ref[:, BASE[m // 2] + 2 * n + m % 2]) for m in range(4)], axis=1)
+        for copy in nears[n]:
+            copy.wait()
+        right = jnp.concatenate([tiles(near_ref[m // 2, n, :, m % 2]) for m in range(4)], axis=1)
         high_ref[128 * n : 128 * n + 128, :], low_ref[128 * n : 128 * n + 128, :] = split(right)
     total = None
     for step in range(PAIRS // DEPTH):
@@ -241,7 +255,7 @@
     vmem = pl.BlockSpec(memory_space=pltpu.VMEM)
     return pl.pallas_call(
         first_kernel,
-        in_specs=[pl.BlockSpec(memory_space=pltpu.HBM), vmem],
+        in_specs=[pl.BlockSpec(memory_space=pltpu.HBM)] * 2,
         out_specs=(vmem, vmem, vmem),
         out_shape=(
             jax.ShapeDtypeStruct((512, 512), jnp.float32),
@@ -250,9 +264,11 @@
         ),
         scratch_shapes=[
             pltpu.VMEM((16, ROWS + 8, 128), jnp.float32),
+            pltpu.VMEM((2, PAIRS, 16, 2, 8, 128), jnp.float32),
             pltpu.VMEM((1024, 512), jnp.bfloat16),
             pltpu.VMEM((1024, 512), jnp.bfloat16),
             pltpu.SemaphoreType.DMA((16,)),
+            pltpu.SemaphoreType.DMA((2, PAIRS)),
         ],
         compiler_params=params(48),
         cost_estimate=cost(2 * 3 * 512 * 1024 * 512, 7 * 2**20),
@@ -322,8 +338,9 @@
         cost_estimate=cost(2 * 3 * 128 * 2048 * 256, 5 * 2**20),
     )(packed, upanel_left[0])
     place = lax.axis_index("col")
-    kind = (place >= 4).astype(jnp.int32) + (place >= 8).astype(jnp.int32)
-    own = lax.switch(kind, [functools.partial(spread, pairs) for pairs in (2, 4, 8)], right)
+    sizes = 1, 2, 4, 6, PAIRS
+    kind = sum((place >= 2 * pairs).astype(jnp.int32) for pairs in sizes[:-1])
+    own = lax.switch(kind, [functools.partial(spread, pairs) for pairs in sizes], right)
     other = lax.ppermute(own, "c", [(0, 1), (1, 0)])
     start, left, factor = first_call(rows, own)
     return second_call(factor, start, left, other)

time: 118 us -> 118 us (level)
  blocking collectives: 61.3 us -> 60.1 us
where the time goes in v10:
time: 118 us; the launch traced here: 116 us
  blocking collectives  60.1 us (51%)
  starting transfers between devices  19.7 us (17%)
  between operations  14.2 us (12%)
  Pallas kernels  13 us (11%)
  waiting for transfers between devices  7.46 us (6%)
  local copies, waits for them, and re-layouts  1.63 us (1%)
    all_gather x1, blocking collectives, on_device(): packed = lax.all_gather(packed, 'col', axis=0)  44.7 us
    all_to_all x1, blocking collectives, spread(): got = lax.all_to_all(right[:, :count], CHIPS, 0, 0)  15.4 us
    all_to_all x1, starting transfers between devices, on_device(): lax.all_to_all(packed.reshape(32, 4, 128), CHIPS + ('c',), 0, 0)  10.4 us
    ppermute x1, starting transfers between devices, on_device(): other = lax.ppermute(own, 'c', [(0, 1), (1, 0)])  9.28 us
    all_to_all x1, waiting for transfers between devices, on_device(): lax.all_to_all(packed.reshape(32, 4, 128), CHIPS + ('c',), 0, 0)  7.42 us
    pallas_call x1, Pallas kernels, first_call(): pl.pallas_call(first_kernel, in_specs=[pl.BlockSpec(memory_space=pltpu.HB...  6.19 us
    pallas_call x1, Pallas kernels, second_call(): pl.pallas_call(second_kernel, in_specs=[vmem, vmem, vmem, hbm], out_specs...  3.6 us
  transfers between devices with their start and end apart: 3, of which 1 were waited for; matrix products, arithmetic and copies ran while one was open for 0% of the time, Pallas kernels for 6%

profile of v10, /device:TPU:1, one launch (start us, length us, event | category | flops | bytes accessed | tf_op | source)
XLA Modules:
  0.0 116.1 jit_solution(6290111871036355768)
XLA Ops:
  7.2 0.0 copy-start
  7.2 0.0 all-gather.5.cloned.1.call-start
  7.2 2.0 %shard_map.77 = (f32[16,8,128]{2,1,0:T(8,128)}, f32[520,128]{1,0:T(8,128)}) custom-call(f32[2,64,128]{2,1,0:T(8,128)} %bitcast.17, f32[512,128]{1,0:T(8,128)} %bitcast.13, f32[2,2,128,128]{3,2,1,0:T(8,128)} %cols_hbm.1, s32[2,128]{1,0:T(2,128)} %pivots_hbm.1, s32[2]{0:T(128)} %ranks_hbm.1), custom_call_target="tpu_custom_call" | custom-call | flops 131072 | bytes 262144 | tf_op jit(solution)/shard_map/pallas_call | solution.py:311
  9.2 0.0 all-gather.5.cloned.1.call-update
  9.2 10.4 %all-to-all-start.5 = ((f32[32,4,128]{2,1,0:T(4,128)}), f32[32,4,128]{2,1,0:T(4,128)S(1)}, u32[]{:S(2)}, u32[]{:S(2)}) async-start(f32[32,4,128]{2,1,0:T(4,128)} %bitcast.16), calls=%async_computation.5 | async-start | bytes 131072 | tf_op jit(solution)/shard_map/all_to_all | solution.py:329
  19.7 7.4 %all-to-all-done.5 = f32[32,4,128]{2,1,0:T(4,128)S(1)} async-done(((f32[32,4,128]{2,1,0:T(4,128)}), f32[32,4,128]{2,1,0:T(4,128)S(1)}, u32[]{:S(2)}, u32[]{:S(2)}) %all-to-all-start.5) | async-done | bytes 65568 | tf_op jit(solution)/shard_map/all_to_all | solution.py:329
  27.1 44.7 %all-gather.2.rows_ref = f32[16,126,128]{2,1,0:T(8,128)S(1)} all-gather(f32[1,126,128]{2,1,0:T(8,128)S(1)} %maximum_bitcast_fusion), channel_id=3, replica_groups=mesh['y'=4,'x'=4,'c'=2,'col'=16] {'col'}, dimensions={0}, use_global_device_ids=true | all-gather | bytes 1096704 | tf_op jit(solution)/shard_map/all_gather | solution.py:331
  71.8 0.0 copy-done
  71.8 1.2 %shard_map.78 = f32[16,32,8,128]{3,2,1,0:T(8,128)S(1)} custom-call(f32[16,126,128]{2,1,0:T(8,128)S(1)} %all-gather.2.rows_ref, f32[2,2048,128]{2,1,0:T(8,128)S(1)} %bitcast.11), custom_call_target="tpu_custom_call" | custom-call | flops 402653184 | bytes 5242880 | tf_op jit(solution)/shard_map/pallas_call | solution.py:332
  73.0 15.7 %conditional.1 = (f32[16,32,8,128]{3,2,1,0:T(8,128)S(1)}) conditional(s32[]{:T(128)} %clamp.3, f32[16,32,8,128]{3,2,1,0:T(8,128)S(1)} %shard_map.78, f32[16,32,8,128]{3,2,1,0:T(8,128)S(1)} %shard_map.78, f32[16,32,8,128]{3,2,1,0:T(8,128)S(1)} %shard_map.78, f32[16,32,8,128]{3,2,1,0:T(8,128)S(1)} %shard_map.78, ...), branch_computations={%region_0.1_spmd, %region_1.2_spmd, %region_2.3_spmd, %region_3.4_... | conditional | bytes 11272204 | solution.py:343
  73.0 0.1 slice.18
  73.1 15.4 %all_to_all.25 = f32[16,18,8,128]{3,2,1,0:T(8,128)S(1)} all-to-all(f32[16,18,8,128]{3,2,1,0:T(8,128)S(1)} %slice.18), channel_id=1, replica_groups=mesh['y'=4,'x'=4,'c'=2,'col'=16] {'y','x'}, dimensions={0} | all-to-all | bytes 2359296 | tf_op jit(solution)/shard_map/cond/branch_0_fun/all_to_all | solution.py:303
  88.5 0.2 pad.12
  88.8 0.0 copy-start.1
  88.8 1.3 %copy-done.1 = f32[16,32,8,128]{3,2,1,0:T(8,128)} copy-done((f32[16,32,8,128]{3,2,1,0:T(8,128)}, f32[16,32,8,128]{3,2,1,0:T(8,128)S(1)}, u32[]{:S(2)}) %copy-start.1) | copy-done | bytes 2097176
  90.1 9.3 %collective-permute-start = (f32[16,32,8,128]{3,2,1,0:T(8,128)}, f32[16,32,8,128]{3,2,1,0:T(8,128)S(1)}, u32[]{:S(2)}, u32[]{:S(2)}) collective-permute-start(f32[16,32,8,128]{3,2,1,0:T(8,128)} %copy-done.1), channel_id=1, source_target_pairs={{0,16},{16,0},{1,17},{17,1},{2,18},{18,2},{3,19},{19,3},{4,20},{20... | collective-permute-start | bytes 6291464 | tf_op jit(solution)/shard_map/ppermute | solution.py:344
  99.4 0.0 all-gather.5.cloned.1.call-done
  99.4 6.2 %shard_map.79 = (f32[512,512]{1,0:T(8,128)S(1)}, bf16[2,512,1024]{2,1,0:T(8,128)(2,1)S(1)}, f32[8,128]{1,0:T(8,128)S(1)}) custom-call(f32[16,520,128]{2,1,0:T(8,128)} %bitcast.12, f32[16,32,8,128]{3,2,1,0:T(8,128)} %copy-done.1), custom_call_target="tpu_custom_call" | custom-call | flops 1610612736 | bytes 7340032 | tf_op jit(solution)/shard_map/pallas_call | solution.py:256
  105.6 0.0 collective-permute-done.right_ref
  105.6 3.6 %shard_map.80 = (f32[2,2,128,128]{3,2,1,0:T(8,128)}, f32[2,1,2,128,128]{4,3,2,1,0:T(8,128)}) custom-call(f32[8,128]{1,0:T(8,128)S(1)} %get-tuple-element.20.factor_ref, f32[512,512]{1,0:T(8,128)S(1)} %get-tuple-element.21.start_ref, bf16[2,512,1024]{2,1,0:T(8,128)(2,1)S(1)} %get-tuple-element.22.left_ref, f32[16,32,8,128]{3,2,1,0:T(8,128)S(1)} %collective-permute-done.right_ref), custom_call_target="tpu_custom_call" | custom-call | flops 1610612736 | bytes 8388608 | tf_op jit(solution)/shard_map/pallas_call | solution.py:282
  (4 shorter events, 0.0 us)
Async XLA Ops:
  7.2 64.7 %copy-start = (f32[1,2,2048,128]{3,2,1,0:T(8,128)S(1)}, f32[1,2,2048,128]{3,2,1,0:T(8,128)}, u32[]{:S(2)}) copy-start(f32[1,2,2048,128]{3,2,1,0:T(8,128)} %param.16) | copy-start | bytes 6291460
  7.2 92.2 %all-gather.5.cloned.1.call-start = ((), (), s32[]{:S(2)}) async-start(), calls=%async_computation.6 | async-start | bytes 4526080 | tf_op jit(solution)/shard_map/all_gather | solution.py:328
  9.2 17.8 %all-to-all-start.5 = ((f32[32,4,128]{2,1,0:T(4,128)}), f32[32,4,128]{2,1,0:T(4,128)S(1)}, u32[]{:S(2)}, u32[]{:S(2)}) async-start(f32[32,4,128]{2,1,0:T(4,128)} %bitcast.16), calls=%async_computation.5 | async-start | bytes 131072 | tf_op jit(solution)/shard_map/all_to_all | solution.py:329
  88.8 1.3 %copy-start.1 = (f32[16,32,8,128]{3,2,1,0:T(8,128)}, f32[16,32,8,128]{3,2,1,0:T(8,128)S(1)}, u32[]{:S(2)}) copy-start(f32[16,32,8,128]{3,2,1,0:T(8,128)S(1)} %get-tuple-element.23.right_ref) | copy-start | bytes 6291460
  90.1 15.5 %collective-permute-start = (f32[16,32,8,128]{3,2,1,0:T(8,128)}, f32[16,32,8,128]{3,2,1,0:T(8,128)S(1)}, u32[]{:S(2)}, u32[]{:S(2)}) collective-permute-start(f32[16,32,8,128]{3,2,1,0:T(8,128)} %copy-done.1), channel_id=1, source_target_pairs={{0,16},{16,0},{1,17},{17,1},{2,18},{18,2},{3,19},{19,3},{4,20},{20... | collective-permute-start | bytes 6291464 | tf_op jit(solution)/shard_map/ppermute | solution.py:344
Sparse Core Ops, SparseCore 0:
  10.1 83.7 all-gather.4

commit v11 on v9

--- a/solution.py
+++ b/solution.py
@@ -190,25 +190,12 @@
     right_ref,
     panel_ref,
     cores_ref,
-    near_ref,
     high_ref,
     low_ref,
     panel_vmem,
     cores_vmem,
-    sems,
     out_sems,
 ):
-    copies = [
-        [
-            pltpu.make_async_copy(
-                right_ref.at[:, BASE[n] + 2 * z : BASE[n] + 2 * z + 2], near_ref.at[n, z], sems.at[n, z]
-            )
-            for z in range(PAIRS)
-        ]
-        for n in range(2)
-    ]
-    for copy in copies[0] + copies[1]:
-        copy.start()
     columns = factor_ref[...].T
     results = (
         (pltpu.make_async_copy(panel_vmem, panel_ref, out_sems.at[0]), panel_vmem, UP_INVERSE),
@@ -216,8 +203,7 @@
     )
     def ready(n):
         for z in range(PAIRS):
-            copies[n][z].wait()
-            right = jnp.concatenate([tiles(near_ref[n, z, :, p]) for p in range(2)], axis=1)
+            right = jnp.concatenate([tiles(right_ref[:, BASE[n] + 2 * z + p]) for p in range(2)], axis=1)
             high_ref[n, 128 * z : 128 * z + 128, :], low_ref[n, 128 * z : 128 * z + 128, :] = split(right)
 
     ready(0)
@@ -265,16 +251,14 @@
     shapes = (2, 2, 128, 128), (2, 1, 2, 128, 128)
     return pl.pallas_call(
         second_kernel,
-        in_specs=[vmem, vmem, vmem, hbm],
+        in_specs=[vmem, vmem, vmem, vmem],
         out_specs=(hbm, hbm),
         out_shape=tuple(jax.ShapeDtypeStruct(shape, jnp.float32) for shape in shapes),
         scratch_shapes=[
-            pltpu.VMEM((2, PAIRS, 16, 2, 8, 128), jnp.float32),
             pltpu.VMEM((2, 1024, 256), jnp.bfloat16),
             pltpu.VMEM((2, 1024, 256), jnp.bfloat16),
             pltpu.VMEM(shapes[0], jnp.float32),
             pltpu.VMEM(shapes[1], jnp.float32),
-            pltpu.SemaphoreType.DMA((2, PAIRS)),
             pltpu.SemaphoreType.DMA((2,)),
         ],
         compiler_params=params(48),

time: 118 us -> 117 us (level)
  no operation moved by 1% of the time
where the time goes in v11:
time: 117 us; the launch traced here: 116 us
  blocking collectives  61.3 us (52%)
  starting transfers between devices  19.5 us (17%)
  between operations  14.2 us (12%)
  Pallas kernels  11.8 us (10%)
  waiting for transfers between devices  7.46 us (6%)
  local copies, waits for them, and re-layouts  1.65 us (1%)
    all_gather x1, blocking collectives, on_device(): packed = lax.all_gather(packed, 'col', axis=0)  44.7 us
    all_to_all x1, blocking collectives, spread(): got = lax.all_to_all(right[:, :count], CHIPS, 0, 0)  16.6 us
    all_to_all x1, starting transfers between devices, on_device(): lax.all_to_all(packed.reshape(32, 4, 128), CHIPS + ('c',), 0, 0)  10.4 us
    ppermute x1, starting transfers between devices, on_device(): other = lax.ppermute(own, 'c', [(0, 1), (1, 0)])  9.1 us
    all_to_all x1, waiting for transfers between devices, on_device(): lax.all_to_all(packed.reshape(32, 4, 128), CHIPS + ('c',), 0, 0)  7.42 us
    pallas_call x1, Pallas kernels, first_call(): pl.pallas_call(first_kernel, in_specs=[pl.BlockSpec(memory_space=pltpu.HB...  5.86 us
    pallas_call x1, Pallas kernels, second_call(): pl.pallas_call(second_kernel, in_specs=[vmem, vmem, vmem, vmem], out_spec...  2.71 us
  transfers between devices with their start and end apart: 3, of which 1 were waited for; matrix products, arithmetic and copies ran while one was open for 0% of the time, Pallas kernels for 6%

profile of v11, /device:TPU:1, one launch (start us, length us, event | category | flops | bytes accessed | tf_op | source)
XLA Modules:
  0.0 115.9 jit_solution(7772987557249993347)
XLA Ops:
  7.2 0.0 copy-start
  7.2 0.0 all-gather.5.cloned.1.call-start
  7.2 2.0 %shard_map.77 = (f32[16,8,128]{2,1,0:T(8,128)}, f32[520,128]{1,0:T(8,128)}) custom-call(f32[2,64,128]{2,1,0:T(8,128)} %bitcast.17, f32[512,128]{1,0:T(8,128)} %bitcast.13, f32[2,2,128,128]{3,2,1,0:T(8,128)} %cols_hbm.1, s32[2,128]{1,0:T(2,128)} %pivots_hbm.1, s32[2]{0:T(128)} %ranks_hbm.1), custom_call_target="tpu_custom_call" | custom-call | flops 131072 | bytes 262144 | tf_op jit(solution)/shard_map/pallas_call | solution.py:279
  9.2 0.0 all-gather.5.cloned.1.call-update
  9.2 10.4 %all-to-all-start.3 = ((f32[32,4,128]{2,1,0:T(4,128)}), f32[32,4,128]{2,1,0:T(4,128)S(1)}, u32[]{:S(2)}, u32[]{:S(2)}) async-start(f32[32,4,128]{2,1,0:T(4,128)} %bitcast.16), calls=%async_computation.3 | async-start | bytes 131072 | tf_op jit(solution)/shard_map/all_to_all | solution.py:297
  19.7 7.4 %all-to-all-done.3 = f32[32,4,128]{2,1,0:T(4,128)S(1)} async-done(((f32[32,4,128]{2,1,0:T(4,128)}), f32[32,4,128]{2,1,0:T(4,128)S(1)}, u32[]{:S(2)}, u32[]{:S(2)}) %all-to-all-start.3) | async-done | bytes 65568 | tf_op jit(solution)/shard_map/all_to_all | solution.py:297
  27.1 44.7 %all-gather.2.rows_ref = f32[16,126,128]{2,1,0:T(8,128)S(1)} all-gather(f32[1,126,128]{2,1,0:T(8,128)S(1)} %maximum_bitcast_fusion), channel_id=3, replica_groups=mesh['y'=4,'x'=4,'c'=2,'col'=16] {'col'}, dimensions={0}, use_global_device_ids=true | all-gather | bytes 1096704 | tf_op jit(solution)/shard_map/all_gather | solution.py:299
  71.8 0.0 copy-done
  71.8 1.2 %shard_map.78 = f32[16,32,8,128]{3,2,1,0:T(8,128)S(1)} custom-call(f32[16,126,128]{2,1,0:T(8,128)S(1)} %all-gather.2.rows_ref, f32[2,2048,128]{2,1,0:T(8,128)S(1)} %bitcast.11), custom_call_target="tpu_custom_call" | custom-call | flops 402653184 | bytes 5242880 | tf_op jit(solution)/shard_map/pallas_call | solution.py:300
  73.0 16.9 %conditional.1 = (f32[16,32,8,128]{3,2,1,0:T(8,128)S(1)}) conditional(s32[]{:T(128)} %clamp.3, f32[16,32,8,128]{3,2,1,0:T(8,128)S(1)} %shard_map.78, f32[16,32,8,128]{3,2,1,0:T(8,128)S(1)} %shard_map.78, f32[16,32,8,128]{3,2,1,0:T(8,128)S(1)} %shard_map.78), branch_computations={%region_0.1_spmd, %region_1.2_spmd, %region_2.3_spmd} | conditional | bytes 9961484 | solution.py:310
  73.0 0.1 slice.14
  73.1 16.6 %all_to_all.17 = f32[16,20,8,128]{3,2,1,0:T(8,128)S(1)} all-to-all(f32[16,20,8,128]{3,2,1,0:T(8,128)S(1)} %slice.14), channel_id=1, replica_groups=mesh['y'=4,'x'=4,'c'=2,'col'=16] {'y','x'}, dimensions={0} | all-to-all | bytes 2621440 | tf_op jit(solution)/shard_map/cond/branch_0_fun/all_to_all | solution.py:271
  89.7 0.2 pad.6
  90.0 0.0 copy-start.1
  90.0 1.3 %copy-done.1 = f32[16,32,8,128]{3,2,1,0:T(8,128)} copy-done((f32[16,32,8,128]{3,2,1,0:T(8,128)}, f32[16,32,8,128]{3,2,1,0:T(8,128)S(1)}, u32[]{:S(2)}) %copy-start.1) | copy-done | bytes 2097176
  91.3 9.1 %collective-permute-start = (f32[16,32,8,128]{3,2,1,0:T(8,128)}, f32[16,32,8,128]{3,2,1,0:T(8,128)S(1)}, u32[]{:S(2)}, u32[]{:S(2)}) collective-permute-start(f32[16,32,8,128]{3,2,1,0:T(8,128)} %copy-done.1), channel_id=1, source_target_pairs={{0,16},{16,0},{1,17},{17,1},{2,18},{18,2},{3,19},{19,3},{4,20},{20... | collective-permute-start | bytes 6291464 | tf_op jit(solution)/shard_map/ppermute | solution.py:311
  100.4 0.0 all-gather.5.cloned.1.call-done
  100.4 5.9 %shard_map.79 = (f32[512,512]{1,0:T(8,128)S(1)}, bf16[2,512,1024]{2,1,0:T(8,128)(2,1)S(1)}, f32[8,128]{1,0:T(8,128)S(1)}) custom-call(f32[16,520,128]{2,1,0:T(8,128)} %bitcast.12, f32[16,32,8,128]{3,2,1,0:T(8,128)} %copy-done.1), custom_call_target="tpu_custom_call" | custom-call | flops 1610612736 | bytes 7340032 | tf_op jit(solution)/shard_map/pallas_call | solution.py:228
  106.3 0.0 collective-permute-done.right_ref
  106.3 2.7 %shard_map.80 = (f32[2,2,128,128]{3,2,1,0:T(8,128)}, f32[2,1,2,128,128]{4,3,2,1,0:T(8,128)}) custom-call(f32[8,128]{1,0:T(8,128)S(1)} %get-tuple-element.16.factor_ref, f32[512,512]{1,0:T(8,128)S(1)} %get-tuple-element.17.start_ref, bf16[2,512,1024]{2,1,0:T(8,128)(2,1)S(1)} %get-tuple-element.18.left_ref, f32[16,32,8,128]{3,2,1,0:T(8,128)S(1)} %collective-permute-done.right_ref), custom_call_target="tpu_custom_call" | custom-call | flops 1610612736 | bytes 8388608 | tf_op jit(solution)/shard_map/pallas_call | solution.py:252
  (4 shorter events, 0.0 us)
Async XLA Ops:
  7.2 64.7 %copy-start = (f32[1,2,2048,128]{3,2,1,0:T(8,128)S(1)}, f32[1,2,2048,128]{3,2,1,0:T(8,128)}, u32[]{:S(2)}) copy-start(f32[1,2,2048,128]{3,2,1,0:T(8,128)} %param.14) | copy-start | bytes 6291460
  7.2 93.2 %all-gather.5.cloned.1.call-start = ((), (), s32[]{:S(2)}) async-start(), calls=%async_computation.4 | async-start | bytes 4526080 | tf_op jit(solution)/shard_map/all_gather | solution.py:296
  9.2 17.8 %all-to-all-start.3 = ((f32[32,4,128]{2,1,0:T(4,128)}), f32[32,4,128]{2,1,0:T(4,128)S(1)}, u32[]{:S(2)}, u32[]{:S(2)}) async-start(f32[32,4,128]{2,1,0:T(4,128)} %bitcast.16), calls=%async_computation.3 | async-start | bytes 131072 | tf_op jit(solution)/shard_map/all_to_all | solution.py:297
  90.0 1.3 %copy-start.1 = (f32[16,32,8,128]{3,2,1,0:T(8,128)}, f32[16,32,8,128]{3,2,1,0:T(8,128)S(1)}, u32[]{:S(2)}) copy-start(f32[16,32,8,128]{3,2,1,0:T(8,128)S(1)} %get-tuple-element.19.right_ref) | copy-start | bytes 6291460
  91.3 15.0 %collective-permute-start = (f32[16,32,8,128]{3,2,1,0:T(8,128)}, f32[16,32,8,128]{3,2,1,0:T(8,128)S(1)}, u32[]{:S(2)}, u32[]{:S(2)}) collective-permute-start(f32[16,32,8,128]{3,2,1,0:T(8,128)} %copy-done.1), channel_id=1, source_target_pairs={{0,16},{16,0},{1,17},{17,1},{2,18},{18,2},{3,19},{19,3},{4,20},{20... | collective-permute-start | bytes 6291464 | tf_op jit(solution)/shard_map/ppermute | solution.py:311
Sparse Core Ops, SparseCore 0:
  10.1 83.7 all-gather.4
